TPU v7x, 256 devices: a whole 4x4x8 slice. The times are simulated.
256 devices in a mesh: ctx: 32 (over x_hi, z, core), dp: 8 (over x_lo, y).
Axes of the slice: x: 4 (x_hi: 2, x_lo: 2; x = x_hi * 2 + x_lo), y: 4, z: 8, core: 2. Of those that a mesh axis runs over, the one named last changes fastest.
Arguments:
- q_raw: bfloat16 [8, 8192, 2048], P('dp', 'ctx')
- raw_keys_input: bfloat16 [8, 8192, 1024], P('dp', 'ctx')
- values: bfloat16 [8, 8192, 1024], P('dp', 'ctx'), may hold values from -6 to 6
- grad_out: bfloat16 [8, 8192, 2048], P('dp', 'ctx')
- q_gain: float32 [128], replicated
- k_gain: float32 [128], replicated, may hold values from 0.5 to 1.5
- doc_starts: int32 [8, 4], P('dp'), may hold values from 1 to 8191, as said below
- flags: int32 [8, 32], P('dp'), may hold values 0 or 1
Outputs:
- dq_raw: bfloat16 [8, 8192, 2048], P('dp', 'ctx')
- raw_key_gradient: bfloat16 [8, 8192, 1024], P('dp', 'ctx')
- dvalues: bfloat16 [8, 8192, 1024], P('dp', 'ctx')
- dq_gain: float32 [128], replicated
- dk_gain: float32 [128], replicated
Inputs may be any that keep to these rules, and one draw needn't show every extreme that they name: `doc_starts`: each row lists 4 distinct offsets in increasing order.
All inputs are finite; a program needn't handle non-finite values. No bound on the sum of `flags` on one device may be relied on, other than what follows from the above.
Results may differ from a plain program's by a relative error of at most 0.004.
The roundings to bfloat16 on the way count: a program that leaves them out, or rounds other values in their place, can miss the bound.
Values may be sent and summed in bfloat16 or wider, within the bound.
No kernel may reach another device: no remote copies, remote signals or barrier semaphores. Data moves between devices by JAX's collectives and lax.ppermute only.
A program may use at most 128 MiB of HBM per device.

v0:
```python
import jax
import jax.numpy as jnp
from jax import lax
from jax.sharding import PartitionSpec as P

QUERY_HEADS = 16
KEY_VALUE_HEADS = 8
HEAD_SIZE = 128
WINDOW = 1024


query_scale = 168.0 ** (-0.5)
eps = 1e-06


def passed_along(block, axis, distance):
    devices = range(lax.axis_size(axis))
    route = [(i - distance, i) for i in devices if i - distance in devices]
    return lax.ppermute(block, axis, route)


def normalize(x, gain):
    ratio = lax.rsqrt(jnp.mean(x * x, axis=-1, keepdims=True) + eps)
    unit = x * ratio
    return (unit * gain, unit, ratio)


def norm_back(grad, unit, ratio, gain):
    scaled = grad * gain
    dx = ratio * (scaled - unit * jnp.mean(scaled * unit, axis=-1, keepdims=True))
    dgain = jnp.sum((grad * unit).reshape(-1, grad.shape[-1]), axis=0)
    return (dx, dgain)


def segment_of(pos, starts, flag_row, shard_length):
    listed = jnp.sum((starts[None, :] <= pos[:, None]).astype(jnp.int32), axis=1)
    heads = jnp.arange(flag_row.shape[0], dtype=jnp.int32) * shard_length
    flagged = jnp.sum(jnp.where(heads[None, :] <= pos[:, None], flag_row[None, :], 0), axis=1)
    return listed + flagged


def head_block(query_block, output_gradient, key_rows, value_rows, allowed):
    score = (
        jnp.einsum("qgd,kd->gqk", query_block, key_rows, preferred_element_type=jnp.float32)
        * query_scale
    )
    score = jnp.where(allowed[None], score, -1e30)
    top = jnp.max(score, axis=-1, keepdims=True)
    expo = jnp.exp(score - top)
    prob = expo / jnp.sum(expo, axis=-1, keepdims=True)
    prob_b = prob.astype(jnp.bfloat16)
    outv = jnp.einsum("gqk,kd->qgd", prob_b, value_rows, preferred_element_type=jnp.float32)
    delta = jnp.sum(output_gradient.astype(jnp.float32) * outv, axis=-1)
    dprob = jnp.einsum(
        "qgd,kd->gqk", output_gradient, value_rows, preferred_element_type=jnp.float32
    )
    dscore = (prob * (dprob - jnp.transpose(delta)[:, :, None]) * query_scale).astype(jnp.bfloat16)
    dvals = jnp.einsum("gqk,qgd->kd", prob_b, output_gradient, preferred_element_type=jnp.float32)
    dquery = jnp.einsum("gqk,kd->qgd", dscore, key_rows, preferred_element_type=jnp.float32)
    dkeys = jnp.einsum("gqk,qgd->kd", dscore, query_block, preferred_element_type=jnp.float32)
    return (dquery, dkeys, dvals)


def on_device(q_raw, raw_keys_input, values, grad_out, q_gain, k_gain, doc_starts, flags):
    shard_length = q_raw.shape[1]
    hops = WINDOW // shard_length
    query_group = QUERY_HEADS // KEY_VALUE_HEADS
    window_span = (hops + 1) * shard_length
    ctx_index = lax.axis_index("ctx")
    qx = q_raw[0].astype(jnp.float32).reshape(shard_length, QUERY_HEADS, HEAD_SIZE)
    key_extra = (
        raw_keys_input[0].astype(jnp.float32).reshape(shard_length, KEY_VALUE_HEADS, HEAD_SIZE)
    )
    qn_f, q_unit, q_ratio = normalize(qx, q_gain)
    kn_f, k_unit, k_ratio = normalize(key_extra, k_gain)
    normed_query = qn_f.astype(jnp.bfloat16)
    kn = kn_f.astype(jnp.bfloat16)
    value_rows = values[0].reshape(shard_length, KEY_VALUE_HEADS, HEAD_SIZE)
    output_gradient = grad_out[0].reshape(shard_length, QUERY_HEADS, HEAD_SIZE)
    received = [passed_along((kn, value_rows), "ctx", hop) for hop in range(1, hops + 1)]
    key_rows = jnp.concatenate([received[hop - 1][0] for hop in range(hops, 0, -1)] + [kn], axis=0)
    value_block = jnp.concatenate(
        [received[hop - 1][1] for hop in range(hops, 0, -1)] + [value_rows], axis=0
    )
    row_number = ctx_index * shard_length
    qpos = row_number + jnp.arange(shard_length, dtype=jnp.int32)
    kpos = row_number - hops * shard_length + jnp.arange(window_span, dtype=jnp.int32)
    dist = qpos[:, None] - kpos[None, :]
    allowed = (dist >= 0) & (dist < WINDOW) & (kpos[None, :] >= 0)
    starts = doc_starts[0]
    flag_row = flags[0]
    allowed = allowed & (
        segment_of(qpos, starts, flag_row, shard_length)[:, None]
        == segment_of(kpos, starts, flag_row, shard_length)[None, :]
    )
    query_head = jnp.transpose(
        normed_query.reshape(shard_length, KEY_VALUE_HEADS, query_group, HEAD_SIZE), (1, 0, 2, 3)
    )
    head_gradient = jnp.transpose(
        output_gradient.reshape(shard_length, KEY_VALUE_HEADS, query_group, HEAD_SIZE), (1, 0, 2, 3)
    )
    kh = jnp.transpose(key_rows, (1, 0, 2))
    vh = jnp.transpose(value_block, (1, 0, 2))
    dquery, dkeys, dvals = lax.map(
        lambda xs: head_block(xs[0], xs[1], xs[2], xs[3], allowed),
        (query_head, head_gradient, kh, vh),
    )
    dquery = jnp.transpose(dquery, (1, 0, 2, 3)).reshape(shard_length, QUERY_HEADS, HEAD_SIZE)
    dkeys = jnp.transpose(dkeys, (1, 0, 2))
    dvals = jnp.transpose(dvals, (1, 0, 2))

    def block_of(hop):
        first = (hops - hop) * shard_length
        return (dkeys[first : first + shard_length], dvals[first : first + shard_length])

    own_k, own_v = block_of(0)
    total_k, value_total = (own_k, own_v)
    for hop in range(1, hops + 1):
        part_k, part_v = block_of(hop)
        back = passed_along((part_k.astype(jnp.bfloat16), part_v.astype(jnp.bfloat16)), "ctx", -hop)
        total_k = total_k + back[0].astype(jnp.float32)
        value_total = value_total + back[1].astype(jnp.float32)
    dq_x, dq_part = norm_back(dquery, q_unit, q_ratio, q_gain)
    key_gradient_extra, dk_part = norm_back(total_k, k_unit, k_ratio, k_gain)
    dq_gain, dk_gain = lax.psum((dq_part, dk_part), ("ctx", "dp"))
    dq_raw = dq_x.reshape(1, shard_length, QUERY_HEADS * HEAD_SIZE).astype(jnp.bfloat16)
    raw_key_gradient = key_gradient_extra.reshape(
        1, shard_length, KEY_VALUE_HEADS * HEAD_SIZE
    ).astype(jnp.bfloat16)
    dvalues = value_total.reshape(1, shard_length, KEY_VALUE_HEADS * HEAD_SIZE).astype(jnp.bfloat16)
    return (dq_raw, raw_key_gradient, dvalues, dq_gain, dk_gain)


def solution(mesh):
    in_specs = (
        P("dp", "ctx", None),
        P("dp", "ctx", None),
        P("dp", "ctx", None),
        P("dp", "ctx", None),
        P(),
        P(),
        P("dp", None),
        P("dp", None),
    )
    out_specs = (P("dp", "ctx", None), P("dp", "ctx", None), P("dp", "ctx", None), P(), P())
    return jax.shard_map(
        on_device, mesh=mesh, in_specs=in_specs, out_specs=out_specs, check_vma=False
    )
```

profile of v0, /device:TPU:6, one launch (start us, length us, event | category | flops | bytes accessed | tf_op | source)
XLA Modules:
  0.0 483.5 jit_solution(16544763722100399045)
XLA Ops:
  3.8 5.2 %collective-permute-start = (bf16[256,8,128]{0,2,1:T(8,128)(2,1)}, bf16[256,8,128]{0,2,1:T(8,128)(2,1)}, u32[]{:S(2)}, u32[]{:S(2)}) collective-permute-start(bf16[256,8,128]{0,2,1:T(8,128)(2,1)} %fusion.79), channel_id=1, source_target_pairs={{0,32},{8,40},{16,48},{24,56},{32,64},{40,72},{48,80},{56,88},{64,... | collective-permute-start | bytes 1572872 | tf_op jit(solution)/shard_map/ppermute | solution.py:19
  12.0 5.0 %collective-permute-start.2 = (bf16[256,8,128]{0,2,1:T(8,128)(2,1)}, bf16[256,8,128]{0,2,1:T(8,128)(2,1)}, u32[]{:S(2)}, u32[]{:S(2)}) collective-permute-start(bf16[256,8,128]{0,2,1:T(8,128)(2,1)} %fusion.79), channel_id=1, source_target_pairs={{0,16},{8,24},{16,32},{24,40},{32,48},{40,56},{48,64},{56,72},{64,... | collective-permute-start | bytes 1572872 | tf_op jit(solution)/shard_map/ppermute | solution.py:19
  20.3 3.4 collective-permute-start.4
  44.5 37.0 %collective-permute-done.4 = bf16[256,8,128]{0,2,1:T(8,128)(2,1)} collective-permute-done((bf16[256,8,128]{0,2,1:T(8,128)(2,1)S(1)}, bf16[256,8,128]{0,2,1:T(8,128)(2,1)}, u32[]{:S(2)}, u32[]{:S(2)}) %collective-permute-start.4) | collective-permute-done | bytes 524320 | tf_op jit(solution)/shard_map/ppermute | solution.py:19
  81.5 9.8 %collective-permute-start.6 = (bf16[256,8,128]{0,2,1:T(8,128)(2,1)S(1)}, bf16[256,8,128]{0,2,1:T(8,128)(2,1)S(1)}, u32[]{:S(2)}, u32[]{:S(2)}) collective-permute-start(bf16[256,8,128]{0,2,1:T(8,128)(2,1)S(1)} %bitcast.222), channel_id=1, source_target_pairs={{0,16},{8,24},{16,32},{24,40},{32,48},{40,56},{48,64},{56,72},{64,... | collective-permute-start | bytes 1572872 | tf_op jit(solution)/shard_map/ppermute | solution.py:19
  92.4 12.8 %collective-permute-start.7 = (bf16[256,8,128]{0,2,1:T(8,128)(2,1)S(1)}, bf16[256,8,128]{0,2,1:T(8,128)(2,1)S(1)}, u32[]{:S(2)}, u32[]{:S(2)}) collective-permute-start(bf16[256,8,128]{0,2,1:T(8,128)(2,1)S(1)} %bitcast.223), channel_id=1, source_target_pairs={{0,8},{8,16},{16,24},{24,32},{32,40},{40,48},{48,56},{56,64},{64,7... | collective-permute-start | bytes 1572872 | tf_op jit(solution)/shard_map/ppermute | solution.py:19
  108.4 4.5 collective-permute-done.5
  115.2 10.5 %collective-permute-done.7 = bf16[256,8,128]{0,2,1:T(8,128)(2,1)S(1)} collective-permute-done((bf16[256,8,128]{0,2,1:T(8,128)(2,1)S(1)}, bf16[256,8,128]{0,2,1:T(8,128)(2,1)S(1)}, u32[]{:S(2)}, u32[]{:S(2)}) %collective-permute-start.7) | collective-permute-done | bytes 524320 | tf_op jit(solution)/shard_map/ppermute | solution.py:19
  127.2 152.7 %while.15 = (s32[]{:T(128)}, f32[8,256,2,128]{1,3,2,0:T(8,128)}, f32[8,1280,128]{1,2,0:T(8,128)}, f32[8,1280,128]{2,1,0:T(8,128)}, bf16[8,1280,128]{1,2,0:T(8,12...) while((s32[]{:T(128)}, f32[8,256,2,128]{1,3,2,0:T(8,128)}, ...), condition=%wide.region_10.11_spmd.clone, body=%wide.region_6.10_spmd.clone.sunk | while | flops 1357123840 | bytes 16810916 | solution.py:104
  128.2 3.6 fusion.144
  140.9 3.3 fusion.149
  147.3 3.6 fusion.144
  166.4 3.6 fusion.144
  185.6 3.6 fusion.144
  204.6 3.6 fusion.144
  217.3 3.4 fusion.149
  223.7 3.6 fusion.144
  236.4 3.4 fusion.149
  242.8 3.6 fusion.144
  255.5 3.3 fusion.149
  261.9 3.6 fusion.144
  286.2 4.7 collective-permute-start.11
  292.7 4.7 collective-permute-start.12
  308.2 29.6 %collective-permute-done.12 = bf16[256,8,128]{2,0,1:T(8,128)(2,1)} collective-permute-done((bf16[256,8,128]{2,0,1:T(8,128)(2,1)}, bf16[256,8,128]{2,0,1:T(8,128)(2,1)}, u32[]{:S(2)}, u32[]{:S(2)}) %collective-permute-start.12) | collective-permute-done | bytes 524320 | tf_op jit(solution)/shard_map/ppermute | solution.py:19
  337.8 7.4 %collective-permute-start.8 = (bf16[256,8,128]{0,2,1:T(8,128)(2,1)}, bf16[256,8,128]{0,2,1:T(8,128)(2,1)}, u32[]{:S(2)}, u32[]{:S(2)}) collective-permute-start(bf16[256,8,128]{0,2,1:T(8,128)(2,1)} %get-tuple-element.214), channel_id=1, source_target_pairs={{8,0},{16,8},{24,16},{32,24},{40,32},{48,40},{56,48},{64,56},{72,6... | collective-permute-start | bytes 1572872 | tf_op jit(solution)/shard_map/ppermute | solution.py:19
  345.2 4.6 collective-permute-done.13
  349.8 7.3 %collective-permute-start.9 = (bf16[256,8,128]{0,2,1:T(8,128)(2,1)}, bf16[256,8,128]{0,2,1:T(8,128)(2,1)}, u32[]{:S(2)}, u32[]{:S(2)}) collective-permute-start(bf16[256,8,128]{0,2,1:T(8,128)(2,1)} %get-tuple-element.217), channel_id=1, source_target_pairs={{16,0},{24,8},{32,16},{40,24},{48,32},{56,40},{64,48},{72,56},{80,... | collective-permute-start | bytes 1572872 | tf_op jit(solution)/shard_map/ppermute | solution.py:19
  357.1 8.6 %collective-permute-done.14 = bf16[256,8,128]{2,0,1:T(8,128)(2,1)} collective-permute-done((bf16[256,8,128]{2,0,1:T(8,128)(2,1)}, bf16[256,8,128]{2,0,1:T(8,128)(2,1)}, u32[]{:S(2)}, u32[]{:S(2)}) %collective-permute-start.14) | collective-permute-done | bytes 524320 | tf_op jit(solution)/shard_map/ppermute | solution.py:19
  365.7 4.7 collective-permute-start.15
  370.5 4.0 multiply_convert_fusion
  374.5 25.4 %collective-permute-done.15 = bf16[256,8,128]{2,0,1:T(8,128)(2,1)S(1)} collective-permute-done((bf16[256,8,128]{2,0,1:T(8,128)(2,1)}, bf16[256,8,128]{2,0,1:T(8,128)(2,1)S(1)}, u32[]{:S(2)}, u32[]{:S(2)}) %collective-permute-start.15) | collective-permute-done | bytes 524320 | tf_op jit(solution)/shard_map/ppermute | solution.py:19
  407.1 76.3 %all-reduce = (f32[128]{0:T(128)}, f32[128]{0:T(128)}) all-reduce(f32[128]{0:T(128)S(1)} %get-tuple-element.175, f32[128]{0:T(128)S(1)} %get-tuple-element.177), channel_id=1, replica_groups=mesh['ctx'=32,'dp'=8] {'ctx','dp'}, use_global_device_ids=true, to_apply=%region_14.15 | all-reduce | flops 256 | bytes 2048 | tf_op jit(solution)/shard_map/psum | solution.py:125
  (181 shorter events, 174.1 us)
Async XLA Ops:
  0.6 19.4 %copy-start.8 = (bf16[1,256,1024]{2,1,0:T(8,128)(2,1)S(1)}, bf16[1,256,1024]{2,1,0:T(8,128)(2,1)}, u32[]{:S(2)}) copy-start(bf16[1,256,1024]{2,1,0:T(8,128)(2,1)} %param.12) | copy-start | bytes 1572868
  0.6 23.1 %copy-start.2 = (bf16[1,256,2048]{2,1,0:T(8,128)(2,1)S(1)}, bf16[1,256,2048]{2,1,0:T(8,128)(2,1)}, u32[]{:S(2)}) copy-start(bf16[1,256,2048]{2,1,0:T(8,128)(2,1)} %param.10) | copy-start | bytes 3145732
  2.0 113.0 %copy-start = (bf16[1,256,1024]{1,2,0:T(8,128)(2,1)}, bf16[1,256,1024]{1,2,0:T(8,128)(2,1)S(1)}, u32[]{:S(2)}) copy-start(bf16[1,256,1024]{1,2,0:T(8,128)(2,1)S(1)} %copy.88) | copy-start | bytes 1572868
  3.8 37.5 %collective-permute-start = (bf16[256,8,128]{0,2,1:T(8,128)(2,1)}, bf16[256,8,128]{0,2,1:T(8,128)(2,1)}, u32[]{:S(2)}, u32[]{:S(2)}) collective-permute-start(bf16[256,8,128]{0,2,1:T(8,128)(2,1)} %fusion.79), channel_id=1, source_target_pairs={{0,32},{8,40},{16,48},{24,56},{32,64},{40,72},{48,80},{56,88},{64,... | collective-permute-start | bytes 1572872 | tf_op jit(solution)/shard_map/ppermute | solution.py:19
  9.0 83.4 %collective-permute-start.1 = (bf16[256,8,128]{0,2,1:T(8,128)(2,1)}, bf16[256,8,128]{0,2,1:T(8,128)(2,1)}, u32[]{:S(2)}, u32[]{:S(2)}) collective-permute-start(bf16[256,8,128]{0,2,1:T(8,128)(2,1)} %fusion.79), channel_id=1, source_target_pairs={{0,24},{8,32},{16,40},{24,48},{32,56},{40,64},{48,72},{56,80},{64,... | collective-permute-start | bytes 1572872 | tf_op jit(solution)/shard_map/ppermute | solution.py:19
  12.0 94.3 %collective-permute-start.2 = (bf16[256,8,128]{0,2,1:T(8,128)(2,1)}, bf16[256,8,128]{0,2,1:T(8,128)(2,1)}, u32[]{:S(2)}, u32[]{:S(2)}) collective-permute-start(bf16[256,8,128]{0,2,1:T(8,128)(2,1)} %fusion.79), channel_id=1, source_target_pairs={{0,16},{8,24},{16,32},{24,40},{32,48},{40,56},{48,64},{56,72},{64,... | collective-permute-start | bytes 1572872 | tf_op jit(solution)/shard_map/ppermute | solution.py:19
  17.0 90.3 %collective-permute-start.3 = (bf16[256,8,128]{0,2,1:T(8,128)(2,1)}, bf16[256,8,128]{0,2,1:T(8,128)(2,1)}, u32[]{:S(2)}, u32[]{:S(2)}) collective-permute-start(bf16[256,8,128]{0,2,1:T(8,128)(2,1)} %fusion.79), channel_id=1, source_target_pairs={{0,8},{8,16},{16,24},{24,32},{32,40},{40,48},{48,56},{56,64},{64,7... | collective-permute-start | bytes 1572872 | tf_op jit(solution)/shard_map/ppermute | solution.py:19
  20.3 61.2 %collective-permute-start.4 = (bf16[256,8,128]{0,2,1:T(8,128)(2,1)S(1)}, bf16[256,8,128]{0,2,1:T(8,128)(2,1)}, u32[]{:S(2)}, u32[]{:S(2)}) collective-permute-start(bf16[256,8,128]{0,2,1:T(8,128)(2,1)S(1)} %bitcast.220), channel_id=1, source_target_pairs={{0,32},{8,40},{16,48},{24,56},{32,64},{40,72},{48,80},{56,88},{64,... | collective-permute-start | bytes 1572872 | tf_op jit(solution)/shard_map/ppermute | solution.py:19
  26.8 5.6 %copy-start.11 = (f32[128]{0:T(128)S(1)}, f32[128]{0:T(128)}, u32[]{:S(2)}) copy-start(f32[128]{0:T(128)} %param.14) | copy-start | bytes 1540
  41.4 71.5 %collective-permute-start.5 = (bf16[256,8,128]{0,2,1:T(8,128)(2,1)S(1)}, bf16[256,8,128]{0,2,1:T(8,128)(2,1)S(1)}, u32[]{:S(2)}, u32[]{:S(2)}) collective-permute-start(bf16[256,8,128]{0,2,1:T(8,128)(2,1)S(1)} %bitcast.221), channel_id=1, source_target_pairs={{0,24},{8,32},{16,40},{24,48},{32,56},{40,64},{48,72},{56,80},{64,... | collective-permute-start | bytes 1572872 | tf_op jit(solution)/shard_map/ppermute | solution.py:19
  81.5 33.5 %collective-permute-start.6 = (bf16[256,8,128]{0,2,1:T(8,128)(2,1)S(1)}, bf16[256,8,128]{0,2,1:T(8,128)(2,1)S(1)}, u32[]{:S(2)}, u32[]{:S(2)}) collective-permute-start(bf16[256,8,128]{0,2,1:T(8,128)(2,1)S(1)} %bitcast.222), channel_id=1, source_target_pairs={{0,16},{8,24},{16,32},{24,40},{32,48},{40,56},{48,64},{56,72},{64,... | collective-permute-start | bytes 1572872 | tf_op jit(solution)/shard_map/ppermute | solution.py:19
  92.4 22.7 %copy-start.10 = (f32[128]{0:T(128)S(1)}, f32[128]{0:T(128)}, u32[]{:S(2)}) copy-start(f32[128]{0:T(128)} %param.15) | copy-start | bytes 1540
  92.4 33.3 %collective-permute-start.7 = (bf16[256,8,128]{0,2,1:T(8,128)(2,1)S(1)}, bf16[256,8,128]{0,2,1:T(8,128)(2,1)S(1)}, u32[]{:S(2)}, u32[]{:S(2)}) collective-permute-start(bf16[256,8,128]{0,2,1:T(8,128)(2,1)S(1)} %bitcast.223), channel_id=1, source_target_pairs={{0,8},{8,16},{16,24},{24,32},{32,40},{40,48},{48,56},{56,64},{64,7... | collective-permute-start | bytes 1572872 | tf_op jit(solution)/shard_map/ppermute | solution.py:19
  115.2 10.6 %copy-start.7 = (bf16[1280,8,128]{0,2,1:T(8,128)(2,1)}, bf16[1280,8,128]{0,2,1:T(8,128)(2,1)S(1)}, u32[]{:S(2)}) copy-start(bf16[1280,8,128]{0,2,1:T(8,128)(2,1)S(1)} %constant_dynamic-update-slice_fusion) | copy-start | bytes 7864324
  128.2 4.7 copy-start.6
  185.5 4.7 copy-start.6
  204.6 4.7 copy-start.6
  242.8 4.7 copy-start.6
  261.9 4.7 copy-start.6
  279.9 10.9 %slice-start = ((s8[5242880]{0:T(1024)(128)(4,1)}), s8[4194304]{0:T(1024)(128)(4,1)S(1)}, s32[]{:S(2)}) async-start(s8[5242880]{0:T(1024)(128)(4,1)} %bitcast.215), calls=%async_computation | async-start | bytes 8388608
  279.9 10.9 %slice-start.1 = ((s8[5242880]{0:T(1024)(128)(4,1)}), s8[1048576]{0:T(1024)(128)(4,1)S(1)}, s32[]{:S(2)}) async-start(s8[5242880]{0:T(1024)(128)(4,1)} %bitcast.215), calls=%async_computation.1 | async-start | bytes 2097152
  284.2 119.1 %collective-permute-start.10 = (bf16[256,8,128]{0,2,1:T(8,128)(2,1)}, bf16[256,8,128]{0,2,1:T(8,128)(2,1)}, u32[]{:S(2)}, u32[]{:S(2)}) collective-permute-start(bf16[256,8,128]{0,2,1:T(8,128)(2,1)} %get-tuple-element.216), channel_id=1, source_target_pairs={{24,0},{32,8},{40,16},{48,24},{56,32},{64,40},{72,48},{80,56},{88,... | collective-permute-start | bytes 1572872 | tf_op jit(solution)/shard_map/ppermute | solution.py:19
  286.2 117.2 %collective-permute-start.11 = (bf16[256,8,128]{0,2,1:T(8,128)(2,1)}, bf16[256,8,128]{0,2,1:T(8,128)(2,1)}, u32[]{:S(2)}, u32[]{:S(2)}) collective-permute-start(bf16[256,8,128]{0,2,1:T(8,128)(2,1)} %get-tuple-element.215), channel_id=1, source_target_pairs={{32,0},{40,8},{48,16},{56,24},{64,32},{72,40},{80,48},{88,56},{96,... | collective-permute-start | bytes 1572872 | tf_op jit(solution)/shard_map/ppermute | solution.py:19
  291.3 10.8 %copy-start.5 = (f32[8,256,2,128]{1,3,2,0:T(8,128)S(1)}, f32[8,256,2,128]{1,3,2,0:T(8,128)}, u32[]{:S(2)}) copy-start(f32[8,256,2,128]{1,3,2,0:T(8,128)} %get-tuple-element.54) | copy-start | bytes 6291460
  292.7 45.1 %collective-permute-start.12 = (bf16[256,8,128]{2,0,1:T(8,128)(2,1)}, bf16[256,8,128]{2,0,1:T(8,128)(2,1)}, u32[]{:S(2)}, u32[]{:S(2)}) collective-permute-start(bf16[256,8,128]{2,0,1:T(8,128)(2,1)} %get-tuple-element.210), channel_id=1, source_target_pairs={{8,0},{16,8},{24,16},{32,24},{40,32},{48,40},{56,48},{64,56},{72,6... | collective-permute-start | bytes 1572872 | tf_op jit(solution)/shard_map/ppermute | solution.py:19
  297.4 52.5 %collective-permute-start.13 = (bf16[256,8,128]{2,0,1:T(8,128)(2,1)}, bf16[256,8,128]{2,0,1:T(8,128)(2,1)}, u32[]{:S(2)}, u32[]{:S(2)}) collective-permute-start(bf16[256,8,128]{2,0,1:T(8,128)(2,1)} %get-tuple-element.213), channel_id=1, source_target_pairs={{16,0},{24,8},{32,16},{40,24},{48,32},{56,40},{64,48},{72,56},{80,... | collective-permute-start | bytes 1572872 | tf_op jit(solution)/shard_map/ppermute | solution.py:19
  300.2 65.5 %collective-permute-start.14 = (bf16[256,8,128]{2,0,1:T(8,128)(2,1)}, bf16[256,8,128]{2,0,1:T(8,128)(2,1)}, u32[]{:S(2)}, u32[]{:S(2)}) collective-permute-start(bf16[256,8,128]{2,0,1:T(8,128)(2,1)} %get-tuple-element.212), channel_id=1, source_target_pairs={{24,0},{32,8},{40,16},{48,24},{56,32},{64,40},{72,48},{80,56},{88,... | collective-permute-start | bytes 1572872 | tf_op jit(solution)/shard_map/ppermute | solution.py:19
  305.2 65.3 %copy-start.3 = (bf16[1,256,2048]{2,1,0:T(8,128)(2,1)S(1)}, bf16[1,256,2048]{2,1,0:T(8,128)(2,1)}, u32[]{:S(2)}) copy-start(bf16[1,256,2048]{2,1,0:T(8,128)(2,1)} %param.10) | copy-start | bytes 3145732
  305.2 65.3 %copy-start.4 = (f32[1,256,2048]{2,1,0:T(8,128)S(1)}, f32[1,256,2048]{2,1,0:T(8,128)}, u32[]{:S(2)}) copy-start(f32[1,256,2048]{2,1,0:T(8,128)} %mul.171) | copy-start | bytes 6291460
  337.8 65.6 %collective-permute-start.8 = (bf16[256,8,128]{0,2,1:T(8,128)(2,1)}, bf16[256,8,128]{0,2,1:T(8,128)(2,1)}, u32[]{:S(2)}, u32[]{:S(2)}) collective-permute-start(bf16[256,8,128]{0,2,1:T(8,128)(2,1)} %get-tuple-element.214), channel_id=1, source_target_pairs={{8,0},{16,8},{24,16},{32,24},{40,32},{48,40},{56,48},{64,56},{72,6... | collective-permute-start | bytes 1572872 | tf_op jit(solution)/shard_map/ppermute | solution.py:19
  349.8 53.5 %collective-permute-start.9 = (bf16[256,8,128]{0,2,1:T(8,128)(2,1)}, bf16[256,8,128]{0,2,1:T(8,128)(2,1)}, u32[]{:S(2)}, u32[]{:S(2)}) collective-permute-start(bf16[256,8,128]{0,2,1:T(8,128)(2,1)} %get-tuple-element.217), channel_id=1, source_target_pairs={{16,0},{24,8},{32,16},{40,24},{48,32},{56,40},{64,48},{72,56},{80,... | collective-permute-start | bytes 1572872 | tf_op jit(solution)/shard_map/ppermute | solution.py:19
  365.7 34.2 %collective-permute-start.15 = (bf16[256,8,128]{2,0,1:T(8,128)(2,1)}, bf16[256,8,128]{2,0,1:T(8,128)(2,1)S(1)}, u32[]{:S(2)}, u32[]{:S(2)}) collective-permute-start(bf16[256,8,128]{2,0,1:T(8,128)(2,1)} %get-tuple-element.211), channel_id=1, source_target_pairs={{32,0},{40,8},{48,16},{56,24},{64,32},{72,40},{80,48},{88,56},{96,... | collective-permute-start | bytes 1572872 | tf_op jit(solution)/shard_map/ppermute | solution.py:19
  (7 other events, 26.8 us)
where the time goes:
time: 488 us; the launch traced here: 483 us
  matrix products  136 us (28%)
  waiting for transfers between devices  122 us (25%)
  starting transfers between devices  79.7 us (16%)
  blocking collectives  76.3 us (16%)
  local copies, waits for them, and re-layouts  39 us (8%)
  other arithmetic  28.8 us (6%)
    ppermute x16, waiting for transfers between devices, passed_along(): return lax.ppermute(block, axis, route)  122 us
    ppermute x16, starting transfers between devices, passed_along(): return lax.ppermute(block, axis, route)  79.7 us
    psum x1, blocking collectives, on_device(): dq_gain, dk_gain = lax.psum((dq_part, dk_part), ('ctx', 'dp'))  76.3 us
    sub x8, matrix products, head_block(): expo = jnp.exp(score - top)  28.9 us
    dot_general x8, matrix products, head_block(): jnp.einsum('gqk,qgd->kd', prob_b, output_gradient, preferred_element_type...  26.7 us
    dot_general x8, matrix products, head_block(): jnp.einsum('gqk,kd->qgd', prob_b, value_rows, preferred_element_type=jnp....  25.7 us
    dot_general x8, matrix products, head_block(): jnp.einsum('qgd,kd->gqk', output_gradient, value_rows, preferred_element_...  19.8 us
    dot_general x8, matrix products, head_block(): jnp.einsum('gqk,qgd->kd', dscore, query_block, preferred_element_type=jnp...  18.5 us
  transfers between devices with their start and end apart: 16, of which 8 were waited for; matrix products, arithmetic and copies ran while one was open for 8% of the time, Pallas kernels for 0%

commit v1 on v0

v1 whole, which is shorter than its diff:
```python
import functools

import jax
import jax.numpy as jnp
from jax import lax
from jax.experimental import pallas as pl
from jax.experimental.pallas import tpu as pltpu
from jax.sharding import PartitionSpec as P

QUERY_HEADS = 16
KEY_VALUE_HEADS = 8
D = 128
WINDOW = 1024
T = 256
TC = 2 * T
NKV = 4
CHUNKS = (1, 1, 1, 1)
LOG2E = 1.4426950408889634
SCALE = 168.0 ** (-0.5)
EPS = 1e-06

f32 = jnp.float32
bf16 = jnp.bfloat16
VM = pl.BlockSpec(memory_space=pltpu.VMEM)
SM = pl.BlockSpec(memory_space=pltpu.SMEM)
PARAMS = pltpu.CompilerParams(vmem_limit_bytes=24 * 1024 * 1024)
SMALL = pltpu.CompilerParams(vmem_limit_bytes=12 * 1024 * 1024)
NT = (((1,), (1,)), ((), ()))
NN = (((1,), (0,)), ((), ()))
TN = (((0,), (0,)), ((), ()))


def dot(a, b, dims):
    return lax.dot_general(a, b, dims, preferred_element_type=f32)


def cost(us):
    return pl.CostEstimate(flops=int(us * 1e9), bytes_accessed=int(us * 1e6), transcendentals=0)


def al(x, n):
    return pl.multiple_of(x, n)


def split_kv_kernel(idx, k, v, send):
    other = 1 - idx[0] % 2
    for h in range(NKV):
        cols = pl.ds(al(other * (NKV * D) + h * D, D), D)
        send[:, 2 * h * D : (2 * h + 1) * D] = k[:, cols]
        send[:, (2 * h + 1) * D : (2 * h + 2) * D] = v[:, cols]


def split_kv(idx, k, v):
    return pl.pallas_call(
        split_kv_kernel,
        out_shape=jax.ShapeDtypeStruct((T, 2 * NKV * D), bf16),
        in_specs=[SM, VM, VM],
        out_specs=VM,
        compiler_params=SMALL,
        cost_estimate=cost(1),
        name="split_kv",
    )(idx, k, v)


def join_kv_kernel(idx, k, v, recv, *outs):
    a = idx[0] % 2
    mine = pl.ds(al(a * T, T), T)
    theirs = pl.ds(al((1 - a) * T, T), T)
    h = 0
    for out, n in zip(outs, CHUNKS):
        for i in range(n):
            cols = pl.ds(al(a * (NKV * D) + h * D, D), D)
            out[mine, 2 * i * D : (2 * i + 1) * D] = k[:, cols]
            out[mine, (2 * i + 1) * D : (2 * i + 2) * D] = v[:, cols]
            out[theirs, 2 * i * D : (2 * i + 2) * D] = recv[:, 2 * h * D : (2 * h + 2) * D]
            h += 1


def join_kv(idx, k, v, recv):
    return pl.pallas_call(
        join_kv_kernel,
        out_shape=[jax.ShapeDtypeStruct((TC, 2 * n * D), bf16) for n in CHUNKS],
        in_specs=[SM, VM, VM, VM],
        out_specs=[VM] * len(CHUNKS),
        compiler_params=SMALL,
        cost_estimate=cost(1),
        name="join_kv",
    )(idx, k, v, recv)


def split_q_kernel(idx, q, do, send):
    other = 1 - idx[0] % 2
    w = 2 * NKV * D
    cols = pl.ds(al(other * w, w), w)
    send[:, :w] = q[:, cols]
    send[:, w:] = do[:, cols]


def split_q(idx, q, do):
    return pl.pallas_call(
        split_q_kernel,
        out_shape=jax.ShapeDtypeStruct((T, 4 * NKV * D), bf16),
        in_specs=[SM, VM, VM],
        out_specs=VM,
        compiler_params=SMALL,
        cost_estimate=cost(1.5),
        name="split_q",
    )(idx, q, do)


def join_q_kernel(idx, q, do, recv, qa, doa):
    a = idx[0] % 2
    w = 2 * NKV * D
    mine = pl.ds(al(a * T, T), T)
    theirs = pl.ds(al((1 - a) * T, T), T)
    cols = pl.ds(al(a * w, w), w)
    qa[mine, :] = q[:, cols]
    doa[mine, :] = do[:, cols]
    qa[theirs, :] = recv[:, :w]
    doa[theirs, :] = recv[:, w:]


def join_q(idx, q, do, recv):
    w = 2 * NKV * D
    return pl.pallas_call(
        join_q_kernel,
        out_shape=[jax.ShapeDtypeStruct((TC, w), bf16)] * 2,
        in_specs=[SM, VM, VM, VM],
        out_specs=[VM, VM],
        compiler_params=SMALL,
        cost_estimate=cost(2),
        name="join_q",
    )(idx, q, do, recv)


def unit_of(x):
    r = lax.rsqrt(jnp.mean(x * x, axis=-1, keepdims=True) + EPS)
    return x * r, r


def rows8(x, op):
    return op(x.reshape(x.shape[0] // 8, 8, x.shape[1]), axis=0)


def attn_kernel(
    idx, starts, flags, qg, kg, q, do, kv0, kv1, kv2,
    dq, d2, d1, d0, gains,
    bias, s_scr, dp_scr, pb_scr, ds_scr, kn_scr, qn_scr, do_scr, dk_acc, dv_acc,
):
    step = pl.program_id(0)
    first = (idx[0] // 2) * TC

    jl = lax.broadcasted_iota(jnp.int32, (T, T), 0)
    il = lax.broadcasted_iota(jnp.int32, (T, T), 1)
    late = jl > il

    @pl.when(step == 0)
    def _():
        gains[...] = jnp.zeros_like(gains)
        for qb in range(2):
            base = first + qb * T
            qpos = base + lax.broadcasted_iota(jnp.int32, (1, T), 1)
            lo = jnp.maximum(qpos - (WINDOW - 1), 0)
            for n in range(starts.shape[1]):
                b = starts[0, n]
                lo = jnp.maximum(lo, jnp.where(b <= qpos, b, 0))
            for n in range(flags.shape[1]):
                b = flags[0, n] * (n * T)
                lo = jnp.maximum(lo, jnp.where(b <= qpos, b, 0))
            for t in range(4):
                if t == 0:
                    kpos = jnp.where(late, base - WINDOW + jl, base + jl)
                else:
                    kpos = base - WINDOW + t * T + jl
                bias[qb, t] = jnp.where(kpos >= lo, 0.0, -jnp.inf).astype(f32)

    dkg = jnp.zeros((8, D), f32)
    for b, ref in enumerate((kv2, kv1, kv0)):
        xh, _ = unit_of(ref[:, :D].astype(f32))
        kn_scr[b * TC : (b + 1) * TC, :] = (xh * kg[...]).astype(bf16)
    for qb in range(2):
        for g in range(2):
            x = q[qb * T : (qb + 1) * T, g * D : (g + 1) * D].astype(f32)
            xh, _ = unit_of(x)
            qn_scr[qb, g * T : (g + 1) * T, :] = (xh * qg[...]).astype(bf16)
            do_scr[qb, g * T : (g + 1) * T, :] = do[qb * T : (qb + 1) * T, g * D : (g + 1) * D]

    def keys(kb):
        return kn_scr[kb * T : (kb + 1) * T, :]

    def vals(kb):
        ref = (kv2, kv1, kv0)[kb // 2]
        return ref[(kb % 2) * T : (kb % 2 + 1) * T, D:]

    dqg = jnp.zeros((8, D), f32)
    for qb in range(2):
        for g in range(2):
            lanes = slice(g * T, (g + 1) * T)
            qn = qn_scr[qb, lanes, :]
            dog = do_scr[qb, lanes, :]
            m = None
            for t in range(4):
                s = dot(keys(qb + t), qn, NT)
                if t == 0:
                    s = jnp.where(late, s, dot(keys(qb + 4), qn, NT))
                s = s * (SCALE * LOG2E) + bias[qb, t]
                s_scr[t] = s
                mt = rows8(s, jnp.max)
                m = mt if m is None else jnp.maximum(m, mt)
            m = jnp.max(m, axis=0, keepdims=True)
            el = None
            for t in range(4):
                e = jnp.exp2(s_scr[t] - m)
                s_scr[t] = e
                lt = rows8(e, jnp.sum)
                el = lt if el is None else el + lt
            rl = 1.0 / jnp.sum(el, axis=0, keepdims=True)
            delta = None
            for t in range(4):
                dp = dot(vals(qb + t), dog, NT)
                if t == 0:
                    dp = jnp.where(late, dp, dot(vals(qb + 4), dog, NT))
                dp_scr[t] = dp
                p = s_scr[t] * rl
                s_scr[t] = p
                pb = p.astype(bf16)
                dt = rows8(pb.astype(f32) * dp, jnp.sum)
                delta = dt if delta is None else delta + dt
                if t == 0:
                    pb_scr[0, :, lanes] = jnp.where(late, p, 0.0).astype(bf16)
                    pb_scr[4, :, lanes] = jnp.where(late, 0.0, p).astype(bf16)
                else:
                    pb_scr[t, :, lanes] = pb
            delta = jnp.sum(delta, axis=0, keepdims=True)
            for t in range(4):
                ds = s_scr[t] * (dp_scr[t] - delta) * SCALE
                if t == 0:
                    ds_scr[0, :, lanes] = jnp.where(late, ds, 0.0).astype(bf16)
                    ds_scr[4, :, lanes] = jnp.where(late, 0.0, ds).astype(bf16)
                else:
                    ds_scr[t, :, lanes] = ds.astype(bf16)
            dqn = None
            for t in range(5):
                part = dot(ds_scr[t, :, lanes], keys(qb + t), TN)
                dqn = part if dqn is None else dqn + part
            xh, r = unit_of(q[qb * T : (qb + 1) * T, g * D : (g + 1) * D].astype(f32))
            dqg = dqg + rows8(dqn * xh, jnp.sum)
            dxh = dqn * qg[...]
            dx = r * (dxh - xh * jnp.mean(dxh * xh, axis=-1, keepdims=True))
            dq[qb * T : (qb + 1) * T, g * D : (g + 1) * D] = dx.astype(bf16)
        for t in range(5):
            kb = qb + t
            rows = slice(kb * T, (kb + 1) * T)
            dv = dot(pb_scr[t], do_scr[qb], NN)
            dk = dot(ds_scr[t], qn_scr[qb], NN)
            if qb == 0 or t == 4:
                dv_acc[rows, :] = dv
                dk_acc[rows, :] = dk
            else:
                dv_acc[rows, :] += dv
                dk_acc[rows, :] += dk

    for b, (ref, out) in enumerate(((kv2, d2), (kv1, d1), (kv0, d0))):
        xh, _ = unit_of(ref[:, :D].astype(f32))
        dk = dk_acc[b * TC : (b + 1) * TC, :]
        dkg = dkg + rows8(dk * xh, jnp.sum)
        out[:, :D] = dk.astype(out.dtype)
        out[:, D:] = dv_acc[b * TC : (b + 1) * TC, :].astype(out.dtype)
    gains[0] += dqg
    gains[1] += dkg


def attn(h0, n, idx, starts, flags, qg, kg, q, do, kv0, kv1, kv2):
    col = pl.BlockSpec((TC, 2 * D), lambda i: (0, i))
    qcol = pl.BlockSpec((TC, 2 * D), lambda i: (0, h0 + i))
    full = pl.BlockSpec((1, D), lambda i: (0, 0))
    return pl.pallas_call(
        attn_kernel,
        grid=(n,),
        out_shape=[
            jax.ShapeDtypeStruct((TC, 2 * n * D), bf16),
            jax.ShapeDtypeStruct((TC, 2 * n * D), bf16),
            jax.ShapeDtypeStruct((TC, 2 * n * D), f32),
            jax.ShapeDtypeStruct((TC, 2 * n * D), f32),
            jax.ShapeDtypeStruct((2, 8, D), f32),
        ],
        in_specs=[SM, SM, SM, full, full, qcol, qcol, col, col, col],
        out_specs=[col, col, col, col, pl.BlockSpec((2, 8, D), lambda i: (0, 0, 0))],
        scratch_shapes=[
            pltpu.VMEM((2, 4, T, T), f32),
            pltpu.VMEM((4, T, T), f32),
            pltpu.VMEM((4, T, T), f32),
            pltpu.VMEM((5, T, 2 * T), bf16),
            pltpu.VMEM((5, T, 2 * T), bf16),
            pltpu.VMEM((3 * TC, D), bf16),
            pltpu.VMEM((2, 2 * T, D), bf16),
            pltpu.VMEM((2, 2 * T, D), bf16),
            pltpu.VMEM((3 * TC, D), f32),
            pltpu.VMEM((3 * TC, D), f32),
        ],
        compiler_params=PARAMS,
        cost_estimate=cost(6 * n),
        name="attn",
    )(idx, starts, flags, qg, kg, q, do, kv0, kv1, kv2)


def add_kernel(x, y, out):
    out[...] = (x[...] + y[...].astype(f32)).astype(bf16)


def add_back(d1, r1):
    return pl.pallas_call(
        add_kernel,
        out_shape=jax.ShapeDtypeStruct(r1.shape, bf16),
        in_specs=[VM, VM],
        out_specs=VM,
        compiler_params=SMALL,
        cost_estimate=cost(1),
        name="add_back",
    )(d1, r1)


def finish_kernel(n, idx, kg, d0, r2, kv, keep, send):
    a = idx[0] % 2
    for out, rows in ((keep, pl.ds(al(a * T, T), T)), (send, pl.ds(al((1 - a) * T, T), T))):
        for i in range(n):
            kc = slice(2 * i * D, (2 * i + 1) * D)
            vc = slice((2 * i + 1) * D, (2 * i + 2) * D)
            dk = d0[rows, kc] + r2[rows, kc].astype(f32)
            xh, r = unit_of(kv[rows, kc].astype(f32))
            dxh = dk * kg[...]
            dx = r * (dxh - xh * jnp.mean(dxh * xh, axis=-1, keepdims=True))
            out[:, kc] = dx.astype(bf16)
            out[:, vc] = (d0[rows, vc] + r2[rows, vc].astype(f32)).astype(bf16)


def finish(n, idx, kg, d0, r2, kv):
    return pl.pallas_call(
        functools.partial(finish_kernel, n),
        out_shape=[jax.ShapeDtypeStruct((T, 2 * n * D), bf16)] * 2,
        in_specs=[SM, VM, VM, VM, VM],
        out_specs=[VM, VM],
        compiler_params=SMALL,
        cost_estimate=cost(1),
        name="finish",
    )(idx, kg, d0, r2, kv)


def out_kv_kernel(idx, *refs):
    a = idx[0] % 2
    g = len(CHUNKS)
    keeps, recvs, (dk, dv) = refs[:g], refs[g : 2 * g], refs[2 * g :]
    h = 0
    for keep, recv, n in zip(keeps, recvs, CHUNKS):
        for i in range(n):
            for ref, side in ((keep, a), (recv, 1 - a)):
                cols = pl.ds(al(side * (NKV * D) + h * D, D), D)
                dk[:, cols] = ref[:, 2 * i * D : (2 * i + 1) * D]
                dv[:, cols] = ref[:, (2 * i + 1) * D : (2 * i + 2) * D]
            h += 1


def out_kv(idx, keeps, recvs):
    return pl.pallas_call(
        out_kv_kernel,
        out_shape=[jax.ShapeDtypeStruct((T, KEY_VALUE_HEADS * D), bf16)] * 2,
        in_specs=[SM] + [VM] * (2 * len(CHUNKS)),
        out_specs=[VM, VM],
        compiler_params=SMALL,
        cost_estimate=cost(1),
        name="out_kv",
    )(idx, *keeps, *recvs)


def split_dq_kernel(idx, *refs):
    a = idx[0] % 2
    parts, (send,) = refs[:-1], refs[-1:]
    c = 0
    for part in parts:
        w = part.shape[1]
        send[:, c : c + w] = part[pl.ds(al((1 - a) * T, T), T), :]
        c += w


def split_dq(idx, parts):
    return pl.pallas_call(
        split_dq_kernel,
        out_shape=jax.ShapeDtypeStruct((T, 2 * NKV * D), bf16),
        in_specs=[SM] + [VM] * len(parts),
        out_specs=VM,
        compiler_params=SMALL,
        cost_estimate=cost(1),
        name="split_dq",
    )(idx, *parts)


def out_q_kernel(idx, *refs):
    a = idx[0] % 2
    parts, recv, dq = refs[:-2], refs[-2], refs[-1]
    w = 2 * NKV * D
    c = 0
    for part in parts:
        n = part.shape[1]
        dq[:, pl.ds(al(a * w + c, D), n)] = part[pl.ds(al(a * T, T), T), :]
        c += n
    dq[:, pl.ds(al((1 - a) * w, w), w)] = recv[...]


def out_q(idx, parts, recv):
    return pl.pallas_call(
        out_q_kernel,
        out_shape=jax.ShapeDtypeStruct((T, QUERY_HEADS * D), bf16),
        in_specs=[SM] + [VM] * (len(parts) + 1),
        out_specs=VM,
        compiler_params=SMALL,
        cost_estimate=cost(1),
        name="out_q",
    )(idx, *parts, recv)


def along(x, distance):
    n = lax.axis_size("ctx")
    return lax.ppermute(x, "ctx", [(i, i + distance) for i in range(n) if 0 <= i + distance < n])


def swap(x, axis, bit):
    n = lax.axis_size(axis)
    return lax.ppermute(x, axis, [(i, i ^ bit) for i in range(n)])


def total(x):
    for bit in (1, 2, 4, 8, 16):
        x = x + swap(x, "ctx", bit)
    for bit in (1, 2, 4):
        x = x + swap(x, "dp", bit)
    return x


def on_device(q_raw, raw_keys_input, values, grad_out, q_gain, k_gain, doc_starts, flags):
    idx = lax.axis_index("ctx").astype(jnp.int32).reshape(1)
    q, k, v, do = q_raw[0], raw_keys_input[0], values[0], grad_out[0]
    qg, kg = q_gain.reshape(1, D), k_gain.reshape(1, D)

    kv0 = join_kv(idx, k, v, swap(split_kv(idx, k, v), "ctx", 1))
    qa, doa = join_q(idx, q, do, swap(split_q(idx, q, do), "ctx", 1))
    kv1 = [along(x, 2) for x in kv0]
    kv2 = [along(x, 2) for x in kv1]

    dqs, d1s, d0s, r1s, gains = [], [], [], [], None
    h0 = 0
    for c, n in enumerate(CHUNKS):
        dq, d2, d1, d0, gain = attn(
            h0, n, idx, doc_starts, flags, qg, kg, qa, doa, kv0[c], kv1[c], kv2[c]
        )
        h0 += n
        dqs.append(dq)
        d1s.append(d1)
        d0s.append(d0)
        r1s.append(along(d2, -2))
        gains = gain if gains is None else gains + gain
    keeps, recvs = [], []
    for c, n in enumerate(CHUNKS):
        r2 = along(add_back(d1s[c], r1s[c]), -2)
        keep, send = finish(n, idx, kg, d0s[c], r2, kv0[c])
        keeps.append(keep)
        recvs.append(swap(send, "ctx", 1))
    dk, dv = out_kv(idx, keeps, recvs)
    dq = out_q(idx, dqs, swap(split_dq(idx, dqs), "ctx", 1))
    gain = total(jnp.sum(gains, axis=1))
    return dq[None], dk[None], dv[None], gain[0], gain[1]


def solution(mesh):
    in_specs = (
        P("dp", "ctx", None),
        P("dp", "ctx", None),
        P("dp", "ctx", None),
        P("dp", "ctx", None),
        P(),
        P(),
        P("dp", None),
        P("dp", None),
    )
    out_specs = (P("dp", "ctx", None), P("dp", "ctx", None), P("dp", "ctx", None), P(), P())
    return jax.shard_map(
        on_device, mesh=mesh, in_specs=in_specs, out_specs=out_specs, check_vma=False
    )
```

time: 488 us -> 155 us (0.32)
  matrix products: 136 us -> 0 us
  blocking collectives: 76.3 us -> 0 us
  waiting for transfers between devices: 122 us -> 60.3 us
  local copies, waits for them, and re-layouts: 39 us -> 4.69 us
  Pallas kernels: 0 us -> 29.7 us
  other arithmetic: 28.8 us -> 0.05 us
  starting transfers between devices: 79.7 us -> 57.8 us
    dot_general x40 -> x0, matrix products: 107 us -> none  [the longest x8 26.7 us: head_block(): jnp.einsum('gqk,qgd->kd', prob_b, output_gradient, preferred_element_type...]
    psum x1 -> x0, blocking collectives: 76.3 us -> none  [on_device(): dq_gain, dk_gain = lax.psum((dq_part, dk_part), ('ctx', 'dp'))]
    ppermute x16 -> x31, waiting for transfers between devices: 122 us -> 60.3 us  [the longest x16 33 us: along(): lax.ppermute(x, 'ctx', [(i, i + distance) for i in range(n) if 0 <= i + d...]
    pallas_call x0 -> x19, Pallas kernels: none -> 29.7 us  [the longest x4 25.6 us: attn(): pl.pallas_call(attn_kernel, grid=(n,), out_shape=[jax.ShapeDtypeStruct((T...]
    sub x8 -> x0, matrix products: 28.9 us -> none  [head_block(): expo = jnp.exp(score - top)]
    ppermute x16 -> x31, starting transfers between devices: 79.7 us -> 57.8 us  [the longest x16 50 us: along(): lax.ppermute(x, 'ctx', [(i, i + distance) for i in range(n) if 0 <= i + d...]
    unnamed x43 -> x20, local copies, waits for them, and re-layouts: 15.1 us -> 4.17 us
    and x8 -> x0, other arithmetic: 8.29 us -> none  [on_device(): allowed & (segment_of(qpos, starts, flag_row, shard_length)[:, None] == s...]
  transfers between devices with their start and end apart: 16 -> 31, of which waited for: 8 -> 16; matrix products, arithmetic and copies ran while one was open for 8% -> 0% of each run, Pallas kernels for 0% -> 19%
where the time goes in v1:
time: 155 us; the launch traced here: 154 us
  waiting for transfers between devices  60.3 us (39%)
  starting transfers between devices  57.8 us (37%)
  Pallas kernels  29.7 us (19%)
  local copies, waits for them, and re-layouts  4.69 us (3%)
    ppermute x16, starting transfers between devices, along(): lax.ppermute(x, 'ctx', [(i, i + distance) for i in range(n) if 0 <= i + d...  50 us
    ppermute x16, waiting for transfers between devices, along(): lax.ppermute(x, 'ctx', [(i, i + distance) for i in range(n) if 0 <= i + d...  33 us
    ppermute x15, waiting for transfers between devices, swap(): return lax.ppermute(x, axis, [(i, i ^ bit) for i in range(n)])  27.3 us
    pallas_call x4, Pallas kernels, attn(): pl.pallas_call(attn_kernel, grid=(n,), out_shape=[jax.ShapeDtypeStruct((T...  25.6 us
    ppermute x15, starting transfers between devices, swap(): return lax.ppermute(x, axis, [(i, i ^ bit) for i in range(n)])  7.78 us
    unnamed x20, local copies, waits for them, and re-layouts  4.17 us
  transfers between devices with their start and end apart: 31, of which 16 were waited for; matrix products, arithmetic and copies ran while one was open for 0% of the time, Pallas kernels for 19%

profile of v1, /device:TPU:6, one launch (start us, length us, event | category | flops | bytes accessed | tf_op | source)
XLA Modules:
  0.0 153.6 jit_solution(2667393377336193138)
XLA Ops:
  4.6 2.1 %collective-permute-done.1.recv = bf16[256,1024]{1,0:T(8,128)(2,1)S(1)} collective-permute-done((bf16[256,1024]{1,0:T(8,128)(2,1)S(1)}, bf16[256,1024]{1,0:T(8,128)(2,1)S(1)}, u32[]{:S(2)}, u32[]{:S(2)}) %collective-permute-start.1) | collective-permute-done | bytes 524320 | tf_op jit(solution)/shard_map/ppermute | solution.py:428
  6.9 3.8 %collective-permute-start.8 = (bf16[512,256]{1,0:T(8,128)(2,1)S(1)}, bf16[512,256]{1,0:T(8,128)(2,1)S(1)}, u32[]{:S(2)}, u32[]{:S(2)}) collective-permute-start(bf16[512,256]{1,0:T(8,128)(2,1)S(1)} %get-tuple-element.49.kv0.kv), channel_id=1, source_target_pairs={{0,16},{8,24},{16,32},{24,40},{32,48},{40,56},{48,64},{56,72},{64,... | collective-permute-start | bytes 786440 | tf_op jit(solution)/shard_map/ppermute | solution.py:423
  10.7 3.8 %collective-permute-start.2 = (bf16[512,256]{1,0:T(8,128)(2,1)S(1)}, bf16[512,256]{1,0:T(8,128)(2,1)S(1)}, u32[]{:S(2)}, u32[]{:S(2)}) collective-permute-start(bf16[512,256]{1,0:T(8,128)(2,1)S(1)} %get-tuple-element.43.kv0.kv), channel_id=1, source_target_pairs={{0,16},{8,24},{16,32},{24,40},{32,48},{40,56},{48,64},{56,72},{64,... | collective-permute-start | bytes 786440 | tf_op jit(solution)/shard_map/ppermute | solution.py:423
  14.5 3.8 %collective-permute-start.4 = (bf16[512,256]{1,0:T(8,128)(2,1)S(1)}, bf16[512,256]{1,0:T(8,128)(2,1)S(1)}, u32[]{:S(2)}, u32[]{:S(2)}) collective-permute-start(bf16[512,256]{1,0:T(8,128)(2,1)S(1)} %get-tuple-element.45.kv0.kv), channel_id=1, source_target_pairs={{0,16},{8,24},{16,32},{24,40},{32,48},{40,56},{48,64},{56,72},{64,... | collective-permute-start | bytes 786440 | tf_op jit(solution)/shard_map/ppermute | solution.py:423
  18.4 5.0 %collective-permute-start.6 = (bf16[512,256]{1,0:T(8,128)(2,1)S(1)}, bf16[512,256]{1,0:T(8,128)(2,1)S(1)}, u32[]{:S(2)}, u32[]{:S(2)}) collective-permute-start(bf16[512,256]{1,0:T(8,128)(2,1)S(1)} %get-tuple-element.47.kv0.kv), channel_id=1, source_target_pairs={{0,16},{8,24},{16,32},{24,40},{32,48},{40,56},{48,64},{56,72},{64,... | collective-permute-start | bytes 786440 | tf_op jit(solution)/shard_map/ppermute | solution.py:423
  23.4 2.9 %collective-permute-start.9 = (bf16[512,256]{1,0:T(8,128)(2,1)S(1)}, bf16[512,256]{1,0:T(8,128)(2,1)S(1)}, u32[]{:S(2)}, u32[]{:S(2)}) collective-permute-start(bf16[512,256]{1,0:T(8,128)(2,1)S(1)} %collective-permute-done.8.kv1), channel_id=1, source_target_pairs={{0,16},{8,24},{16,32},{24,40},{32,48},{40,56},{48,64},{56,72},{64,... | collective-permute-start | bytes 786440 | tf_op jit(solution)/shard_map/ppermute | solution.py:423
  30.1 3.7 %collective-permute-done.4.kv1 = bf16[512,256]{1,0:T(8,128)(2,1)S(1)} collective-permute-done((bf16[512,256]{1,0:T(8,128)(2,1)S(1)}, bf16[512,256]{1,0:T(8,128)(2,1)S(1)}, u32[]{:S(2)}, u32[]{:S(2)}) %collective-permute-start.4) | collective-permute-done | bytes 262176 | tf_op jit(solution)/shard_map/ppermute | solution.py:423
  35.7 3.7 %collective-permute-done.6.kv1 = bf16[512,256]{1,0:T(8,128)(2,1)S(1)} collective-permute-done((bf16[512,256]{1,0:T(8,128)(2,1)S(1)}, bf16[512,256]{1,0:T(8,128)(2,1)S(1)}, u32[]{:S(2)}, u32[]{:S(2)}) %collective-permute-start.6) | collective-permute-done | bytes 262176 | tf_op jit(solution)/shard_map/ppermute | solution.py:423
  41.5 3.5 %collective-permute-done.9.kv2 = bf16[512,256]{1,0:T(8,128)(2,1)S(1)} collective-permute-done((bf16[512,256]{1,0:T(8,128)(2,1)S(1)}, bf16[512,256]{1,0:T(8,128)(2,1)S(1)}, u32[]{:S(2)}, u32[]{:S(2)}) %collective-permute-start.9) | collective-permute-done | bytes 262176 | tf_op jit(solution)/shard_map/ppermute | solution.py:423
  45.7 6.4 %attn.7 = (bf16[512,256]{1,0:T(8,128)(2,1)S(1)}, bf16[512,256]{1,0:T(8,128)(2,1)S(1)}, f32[512,256]{1,0:T(8,128)S(1)}, f32[512,256]{1,0:T(8,128)S(1)}, f32[2,8,128]{2,1,0:T(8,128)S(1)}) custom-call(s32[1]{0:T(128)} %bitcast.idx, s32[1,4]{1,0:T(1,128)S(1)} %copy-done.6, s32[1,32]{1,0:T(1,128)S(1)} %copy-done.7, f32[1,128]{1,0:T(1,128)S(1)} %bitcast.22, ...), custom_call_target="tpu_custom_call" | custom-call | flops 6000000000 | bytes 6000000 | tf_op jit(solution)/shard_map/attn/pallas_call | solution.py:277
  52.1 4.2 %collective-permute-start.17 = (bf16[512,256]{1,0:T(8,128)(2,1)S(1)}, bf16[512,256]{1,0:T(8,128)(2,1)S(1)}, u32[]{:S(2)}, u32[]{:S(2)}) collective-permute-start(bf16[512,256]{1,0:T(8,128)(2,1)S(1)} %get-tuple-element.65), channel_id=1, source_target_pairs={{16,0},{24,8},{32,16},{40,24},{48,32},{56,40},{64,48},{72,56},{80,... | collective-permute-start | bytes 786440 | tf_op jit(solution)/shard_map/ppermute | solution.py:423
  56.4 5.0 %collective-permute-done.7.kv2 = bf16[512,256]{1,0:T(8,128)(2,1)S(1)} collective-permute-done((bf16[512,256]{1,0:T(8,128)(2,1)S(1)}, bf16[512,256]{1,0:T(8,128)(2,1)S(1)}, u32[]{:S(2)}, u32[]{:S(2)}) %collective-permute-start.7) | collective-permute-done | bytes 262176 | tf_op jit(solution)/shard_map/ppermute | solution.py:423
  61.4 6.4 %attn.6 = (bf16[512,256]{1,0:T(8,128)(2,1)S(1)}, bf16[512,256]{1,0:T(8,128)(2,1)S(1)}, f32[512,256]{1,0:T(8,128)S(1)}, f32[512,256]{1,0:T(8,128)S(1)}, f32[2,8,128]{2,1,0:T(8,128)S(1)}) custom-call(s32[1]{0:T(128)} %bitcast.idx, s32[1,4]{1,0:T(1,128)S(1)} %copy-done.6, s32[1,32]{1,0:T(1,128)S(1)} %copy-done.7, f32[1,128]{1,0:T(1,128)S(1)} %bitcast.23, ...), custom_call_target="tpu_custom_call" | custom-call | flops 6000000000 | bytes 6000000 | tf_op jit(solution)/shard_map/attn/pallas_call | solution.py:277
  67.8 3.9 %collective-permute-start.15 = (bf16[512,256]{1,0:T(8,128)(2,1)S(1)}, bf16[512,256]{1,0:T(8,128)(2,1)S(1)}, u32[]{:S(2)}, u32[]{:S(2)}) collective-permute-start(bf16[512,256]{1,0:T(8,128)(2,1)S(1)} %get-tuple-element.61), channel_id=1, source_target_pairs={{16,0},{24,8},{32,16},{40,24},{48,32},{56,40},{64,48},{72,56},{80,... | collective-permute-start | bytes 786440 | tf_op jit(solution)/shard_map/ppermute | solution.py:423
  71.7 6.4 %attn.5 = (bf16[512,256]{1,0:T(8,128)(2,1)S(1)}, bf16[512,256]{1,0:T(8,128)(2,1)S(1)}, f32[512,256]{1,0:T(8,128)S(1)}, f32[512,256]{1,0:T(8,128)S(1)}, f32[2,8,128]{2,1,0:T(8,128)S(1)}) custom-call(s32[1]{0:T(128)} %bitcast.idx, s32[1,4]{1,0:T(1,128)S(1)} %copy-done.6, s32[1,32]{1,0:T(1,128)S(1)} %copy-done.7, f32[1,128]{1,0:T(1,128)S(1)} %bitcast.24, ...), custom_call_target="tpu_custom_call" | custom-call | flops 6000000000 | bytes 6000000 | tf_op jit(solution)/shard_map/attn/pallas_call | solution.py:277
  78.1 6.4 %attn.4 = (bf16[512,256]{1,0:T(8,128)(2,1)S(1)}, bf16[512,256]{1,0:T(8,128)(2,1)S(1)}, f32[512,256]{1,0:T(8,128)S(1)}, f32[512,256]{1,0:T(8,128)S(1)}, f32[2,8,128]{2,1,0:T(8,128)S(1)}) custom-call(s32[1]{0:T(128)} %bitcast.idx, s32[1,4]{1,0:T(1,128)S(1)} %copy-done.6, s32[1,32]{1,0:T(1,128)S(1)} %copy-done.7, f32[1,128]{1,0:T(1,128)S(1)} %bitcast.25, ...), custom_call_target="tpu_custom_call" | custom-call | flops 6000000000 | bytes 6000000 | tf_op jit(solution)/shard_map/attn/pallas_call | solution.py:277
  86.3 3.3 %collective-permute-done.24 = f32[2,128]{1,0:T(2,128)S(1)} collective-permute-done((f32[2,128]{1,0:T(2,128)S(1)}, f32[2,128]{1,0:T(2,128)S(1)}, u32[]{:S(2)}, u32[]{:S(2)}) %collective-permute-start.24) | collective-permute-done | bytes 1056 | tf_op jit(solution)/shard_map/ppermute | solution.py:428
  89.6 4.5 %collective-permute-done.25 = f32[2,128]{1,0:T(2,128)S(1)} collective-permute-done((f32[2,128]{1,0:T(2,128)S(1)}, f32[2,128]{1,0:T(2,128)S(1)}, u32[]{:S(2)}, u32[]{:S(2)}) %collective-permute-start.25) | collective-permute-done | bytes 1056 | tf_op jit(solution)/shard_map/ppermute | solution.py:428
  95.8 5.8 %collective-permute-done.26 = f32[2,128]{1,0:T(2,128)S(1)} collective-permute-done((f32[2,128]{1,0:T(2,128)S(1)}, f32[2,128]{1,0:T(2,128)S(1)}, u32[]{:S(2)}, u32[]{:S(2)}) %collective-permute-start.26) | collective-permute-done | bytes 1056 | tf_op jit(solution)/shard_map/ppermute | solution.py:428
  101.5 5.1 %collective-permute-done.27 = f32[2,128]{1,0:T(2,128)S(1)} collective-permute-done((f32[2,128]{1,0:T(2,128)S(1)}, f32[2,128]{1,0:T(2,128)S(1)}, u32[]{:S(2)}, u32[]{:S(2)}) %collective-permute-start.27) | collective-permute-done | bytes 1056 | tf_op jit(solution)/shard_map/ppermute | solution.py:428
  108.2 2.0 %collective-permute-done.28 = f32[2,128]{1,0:T(2,128)S(1)} collective-permute-done((f32[2,128]{1,0:T(2,128)S(1)}, f32[2,128]{1,0:T(2,128)S(1)}, u32[]{:S(2)}, u32[]{:S(2)}) %collective-permute-start.28) | collective-permute-done | bytes 1056 | tf_op jit(solution)/shard_map/ppermute | solution.py:428
  110.2 3.2 %collective-permute-start.29 = (f32[2,128]{1,0:T(2,128)S(1)}, f32[2,128]{1,0:T(2,128)S(1)}, u32[]{:S(2)}, u32[]{:S(2)}) collective-permute-start(f32[2,128]{1,0:T(2,128)S(1)} %add.41), channel_id=1, source_target_pairs={{0,2},{1,3},{2,0},{3,1},{4,6},{5,7},{6,4},{7,5},{8,10},{9,11},{10,... | collective-permute-start | bytes 3080 | tf_op jit(solution)/shard_map/ppermute | solution.py:428
  113.4 2.9 %collective-permute-start.13 = (bf16[512,256]{1,0:T(8,128)(2,1)S(1)}, bf16[512,256]{1,0:T(8,128)(2,1)S(1)}, u32[]{:S(2)}, u32[]{:S(2)}) collective-permute-start(bf16[512,256]{1,0:T(8,128)(2,1)S(1)} %get-tuple-element.57), channel_id=1, source_target_pairs={{16,0},{24,8},{32,16},{40,24},{48,32},{56,40},{64,48},{72,56},{80,... | collective-permute-start | bytes 786440 | tf_op jit(solution)/shard_map/ppermute | solution.py:423
  116.3 2.9 %collective-permute-start.11 = (bf16[512,256]{1,0:T(8,128)(2,1)S(1)}, bf16[512,256]{1,0:T(8,128)(2,1)S(1)}, u32[]{:S(2)}, u32[]{:S(2)}) collective-permute-start(bf16[512,256]{1,0:T(8,128)(2,1)S(1)} %get-tuple-element.53), channel_id=1, source_target_pairs={{16,0},{24,8},{32,16},{40,24},{48,32},{56,40},{64,48},{72,56},{80,... | collective-permute-start | bytes 786440 | tf_op jit(solution)/shard_map/ppermute | solution.py:423
  119.4 3.5 %collective-permute-done.30 = f32[2,128]{1,0:T(2,128)S(1)} collective-permute-done((f32[2,128]{1,0:T(2,128)S(1)}, f32[2,128]{1,0:T(2,128)S(1)}, u32[]{:S(2)}, u32[]{:S(2)}) %collective-permute-start.30) | collective-permute-done | bytes 1056 | tf_op jit(solution)/shard_map/ppermute | solution.py:428
  123.0 4.1 %collective-permute-start.18 = (bf16[512,256]{1,0:T(8,128)(2,1)S(1)}, bf16[512,256]{1,0:T(8,128)(2,1)S(1)}, u32[]{:S(2)}, u32[]{:S(2)}) collective-permute-start(bf16[512,256]{1,0:T(8,128)(2,1)S(1)} %add_back.7), channel_id=1, source_target_pairs={{16,0},{24,8},{32,16},{40,24},{48,32},{56,40},{64,48},{72,56},{80,... | collective-permute-start | bytes 786440 | tf_op jit(solution)/shard_map/ppermute | solution.py:423
  127.2 1.9 %collective-permute-start.16 = (bf16[512,256]{1,0:T(8,128)(2,1)S(1)}, bf16[512,256]{1,0:T(8,128)(2,1)S(1)}, u32[]{:S(2)}, u32[]{:S(2)}) collective-permute-start(bf16[512,256]{1,0:T(8,128)(2,1)S(1)} %add_back.6), channel_id=1, source_target_pairs={{16,0},{24,8},{32,16},{40,24},{48,32},{56,40},{64,48},{72,56},{80,... | collective-permute-start | bytes 786440 | tf_op jit(solution)/shard_map/ppermute | solution.py:423
  129.2 1.9 %collective-permute-start.14 = (bf16[512,256]{1,0:T(8,128)(2,1)S(1)}, bf16[512,256]{1,0:T(8,128)(2,1)S(1)}, u32[]{:S(2)}, u32[]{:S(2)}) collective-permute-start(bf16[512,256]{1,0:T(8,128)(2,1)S(1)} %add_back.5), channel_id=1, source_target_pairs={{16,0},{24,8},{32,16},{40,24},{48,32},{56,40},{64,48},{72,56},{80,... | collective-permute-start | bytes 786440 | tf_op jit(solution)/shard_map/ppermute | solution.py:423
  131.2 2.9 %collective-permute-start.12 = (bf16[512,256]{1,0:T(8,128)(2,1)S(1)}, bf16[512,256]{1,0:T(8,128)(2,1)S(1)}, u32[]{:S(2)}, u32[]{:S(2)}) collective-permute-start(bf16[512,256]{1,0:T(8,128)(2,1)S(1)} %add_back.4), channel_id=1, source_target_pairs={{16,0},{24,8},{32,16},{40,24},{48,32},{56,40},{64,48},{72,56},{80,... | collective-permute-start | bytes 786440 | tf_op jit(solution)/shard_map/ppermute | solution.py:423
  134.5 5.1 %collective-permute-done.16.r2 = bf16[512,256]{1,0:T(8,128)(2,1)S(1)} collective-permute-done((bf16[512,256]{1,0:T(8,128)(2,1)S(1)}, bf16[512,256]{1,0:T(8,128)(2,1)S(1)}, u32[]{:S(2)}, u32[]{:S(2)}) %collective-permute-start.16) | collective-permute-done | bytes 262176 | tf_op jit(solution)/shard_map/ppermute | solution.py:423
  139.9 5.3 %collective-permute-done.14.r2 = bf16[512,256]{1,0:T(8,128)(2,1)S(1)} collective-permute-done((bf16[512,256]{1,0:T(8,128)(2,1)S(1)}, bf16[512,256]{1,0:T(8,128)(2,1)S(1)}, u32[]{:S(2)}, u32[]{:S(2)}) %collective-permute-start.14) | collective-permute-done | bytes 262176 | tf_op jit(solution)/shard_map/ppermute | solution.py:423
  145.6 4.9 %collective-permute-done.12.r2 = bf16[512,256]{1,0:T(8,128)(2,1)S(1)} collective-permute-done((bf16[512,256]{1,0:T(8,128)(2,1)S(1)}, bf16[512,256]{1,0:T(8,128)(2,1)S(1)}, u32[]{:S(2)}, u32[]{:S(2)}) %collective-permute-start.12) | collective-permute-done | bytes 262176 | tf_op jit(solution)/shard_map/ppermute | solution.py:423
  (79 shorter events, 22.1 us)
Async XLA Ops:
  3.2 38.2 %collective-permute-start = (bf16[256,2048]{1,0:T(8,128)(2,1)S(1)}, bf16[256,2048]{1,0:T(8,128)(2,1)S(1)}, u32[]{:S(2)}, u32[]{:S(2)}) collective-permute-start(bf16[256,2048]{1,0:T(8,128)(2,1)S(1)} %split_q.1), channel_id=1, source_target_pairs={{0,8},{8,0},{16,24},{24,16},{32,40},{40,32},{48,56},{56,48},{64,72... | collective-permute-start | bytes 3145736 | tf_op jit(solution)/shard_map/ppermute | solution.py:428
  4.4 36.9 %copy-start.1 = (bf16[1,256,2048]{2,1,0:T(8,128)(2,1)S(1)}, bf16[1,256,2048]{2,1,0:T(8,128)(2,1)}, u32[]{:S(2)}) copy-start(bf16[1,256,2048]{2,1,0:T(8,128)(2,1)} %param.8) | copy-start | bytes 3145732
  4.5 2.2 %collective-permute-start.1 = (bf16[256,1024]{1,0:T(8,128)(2,1)S(1)}, bf16[256,1024]{1,0:T(8,128)(2,1)S(1)}, u32[]{:S(2)}, u32[]{:S(2)}) collective-permute-start(bf16[256,1024]{1,0:T(8,128)(2,1)S(1)} %split_kv.1), channel_id=1, source_target_pairs={{0,8},{8,0},{16,24},{24,16},{32,40},{40,32},{48,56},{56,48},{64,72... | collective-permute-start | bytes 1572872 | tf_op jit(solution)/shard_map/ppermute | solution.py:428
  6.9 16.5 %collective-permute-start.8 = (bf16[512,256]{1,0:T(8,128)(2,1)S(1)}, bf16[512,256]{1,0:T(8,128)(2,1)S(1)}, u32[]{:S(2)}, u32[]{:S(2)}) collective-permute-start(bf16[512,256]{1,0:T(8,128)(2,1)S(1)} %get-tuple-element.49.kv0.kv), channel_id=1, source_target_pairs={{0,16},{8,24},{16,32},{24,40},{32,48},{40,56},{48,64},{56,72},{64,... | collective-permute-start | bytes 786440 | tf_op jit(solution)/shard_map/ppermute | solution.py:423
  10.7 17.5 %collective-permute-start.2 = (bf16[512,256]{1,0:T(8,128)(2,1)S(1)}, bf16[512,256]{1,0:T(8,128)(2,1)S(1)}, u32[]{:S(2)}, u32[]{:S(2)}) collective-permute-start(bf16[512,256]{1,0:T(8,128)(2,1)S(1)} %get-tuple-element.43.kv0.kv), channel_id=1, source_target_pairs={{0,16},{8,24},{16,32},{24,40},{32,48},{40,56},{48,64},{56,72},{64,... | collective-permute-start | bytes 786440 | tf_op jit(solution)/shard_map/ppermute | solution.py:423
  14.5 19.3 %collective-permute-start.4 = (bf16[512,256]{1,0:T(8,128)(2,1)S(1)}, bf16[512,256]{1,0:T(8,128)(2,1)S(1)}, u32[]{:S(2)}, u32[]{:S(2)}) collective-permute-start(bf16[512,256]{1,0:T(8,128)(2,1)S(1)} %get-tuple-element.45.kv0.kv), channel_id=1, source_target_pairs={{0,16},{8,24},{16,32},{24,40},{32,48},{40,56},{48,64},{56,72},{64,... | collective-permute-start | bytes 786440 | tf_op jit(solution)/shard_map/ppermute | solution.py:423
  18.4 21.0 %collective-permute-start.6 = (bf16[512,256]{1,0:T(8,128)(2,1)S(1)}, bf16[512,256]{1,0:T(8,128)(2,1)S(1)}, u32[]{:S(2)}, u32[]{:S(2)}) collective-permute-start(bf16[512,256]{1,0:T(8,128)(2,1)S(1)} %get-tuple-element.47.kv0.kv), channel_id=1, source_target_pairs={{0,16},{8,24},{16,32},{24,40},{32,48},{40,56},{48,64},{56,72},{64,... | collective-permute-start | bytes 786440 | tf_op jit(solution)/shard_map/ppermute | solution.py:423
  23.4 21.6 %collective-permute-start.9 = (bf16[512,256]{1,0:T(8,128)(2,1)S(1)}, bf16[512,256]{1,0:T(8,128)(2,1)S(1)}, u32[]{:S(2)}, u32[]{:S(2)}) collective-permute-start(bf16[512,256]{1,0:T(8,128)(2,1)S(1)} %collective-permute-done.8.kv1), channel_id=1, source_target_pairs={{0,16},{8,24},{16,32},{24,40},{32,48},{40,56},{48,64},{56,72},{64,... | collective-permute-start | bytes 786440 | tf_op jit(solution)/shard_map/ppermute | solution.py:423
  28.2 49.9 %collective-permute-start.3 = (bf16[512,256]{1,0:T(8,128)(2,1)S(1)}, bf16[512,256]{1,0:T(8,128)(2,1)S(1)}, u32[]{:S(2)}, u32[]{:S(2)}) collective-permute-start(bf16[512,256]{1,0:T(8,128)(2,1)S(1)} %collective-permute-done.2.kv1), channel_id=1, source_target_pairs={{0,16},{8,24},{16,32},{24,40},{32,48},{40,56},{48,64},{56,72},{64,... | collective-permute-start | bytes 786440 | tf_op jit(solution)/shard_map/ppermute | solution.py:423
  33.8 37.9 %collective-permute-start.5 = (bf16[512,256]{1,0:T(8,128)(2,1)S(1)}, bf16[512,256]{1,0:T(8,128)(2,1)S(1)}, u32[]{:S(2)}, u32[]{:S(2)}) collective-permute-start(bf16[512,256]{1,0:T(8,128)(2,1)S(1)} %collective-permute-done.4.kv1), channel_id=1, source_target_pairs={{0,16},{8,24},{16,32},{24,40},{32,48},{40,56},{48,64},{56,72},{64,... | collective-permute-start | bytes 786440 | tf_op jit(solution)/shard_map/ppermute | solution.py:423
  39.4 22.0 %collective-permute-start.7 = (bf16[512,256]{1,0:T(8,128)(2,1)S(1)}, bf16[512,256]{1,0:T(8,128)(2,1)S(1)}, u32[]{:S(2)}, u32[]{:S(2)}) collective-permute-start(bf16[512,256]{1,0:T(8,128)(2,1)S(1)} %collective-permute-done.6.kv1), channel_id=1, source_target_pairs={{0,16},{8,24},{16,32},{24,40},{32,48},{40,56},{48,64},{56,72},{64,... | collective-permute-start | bytes 786440 | tf_op jit(solution)/shard_map/ppermute | solution.py:423
  52.1 70.8 %collective-permute-start.17 = (bf16[512,256]{1,0:T(8,128)(2,1)S(1)}, bf16[512,256]{1,0:T(8,128)(2,1)S(1)}, u32[]{:S(2)}, u32[]{:S(2)}) collective-permute-start(bf16[512,256]{1,0:T(8,128)(2,1)S(1)} %get-tuple-element.65), channel_id=1, source_target_pairs={{16,0},{24,8},{32,16},{40,24},{48,32},{56,40},{64,48},{72,56},{80,... | collective-permute-start | bytes 786440 | tf_op jit(solution)/shard_map/ppermute | solution.py:423
  67.8 59.3 %collective-permute-start.15 = (bf16[512,256]{1,0:T(8,128)(2,1)S(1)}, bf16[512,256]{1,0:T(8,128)(2,1)S(1)}, u32[]{:S(2)}, u32[]{:S(2)}) collective-permute-start(bf16[512,256]{1,0:T(8,128)(2,1)S(1)} %get-tuple-element.61), channel_id=1, source_target_pairs={{16,0},{24,8},{32,16},{40,24},{48,32},{56,40},{64,48},{72,56},{80,... | collective-permute-start | bytes 786440 | tf_op jit(solution)/shard_map/ppermute | solution.py:423
  84.5 1.5 collective-permute-start.23
  86.0 3.6 %collective-permute-start.24 = (f32[2,128]{1,0:T(2,128)S(1)}, f32[2,128]{1,0:T(2,128)S(1)}, u32[]{:S(2)}, u32[]{:S(2)}) collective-permute-start(f32[2,128]{1,0:T(2,128)S(1)} %add.36), channel_id=1, source_target_pairs={{0,16},{8,24},{16,0},{24,8},{32,48},{40,56},{48,32},{56,40},{64,80... | collective-permute-start | bytes 3080 | tf_op jit(solution)/shard_map/ppermute | solution.py:428
  89.6 4.5 %collective-permute-start.25 = (f32[2,128]{1,0:T(2,128)S(1)}, f32[2,128]{1,0:T(2,128)S(1)}, u32[]{:S(2)}, u32[]{:S(2)}) collective-permute-start(f32[2,128]{1,0:T(2,128)S(1)} %add.37), channel_id=1, source_target_pairs={{0,32},{8,40},{16,48},{24,56},{32,0},{40,8},{48,16},{56,24},{64,96... | collective-permute-start | bytes 3080 | tf_op jit(solution)/shard_map/ppermute | solution.py:428
  94.1 7.5 %collective-permute-start.26 = (f32[2,128]{1,0:T(2,128)S(1)}, f32[2,128]{1,0:T(2,128)S(1)}, u32[]{:S(2)}, u32[]{:S(2)}) collective-permute-start(f32[2,128]{1,0:T(2,128)S(1)} %add.38), channel_id=1, source_target_pairs={{0,64},{8,72},{16,80},{24,88},{32,96},{40,104},{48,112},{56,120},{... | collective-permute-start | bytes 3080 | tf_op jit(solution)/shard_map/ppermute | solution.py:428
  101.5 5.1 %collective-permute-start.27 = (f32[2,128]{1,0:T(2,128)S(1)}, f32[2,128]{1,0:T(2,128)S(1)}, u32[]{:S(2)}, u32[]{:S(2)}) collective-permute-start(f32[2,128]{1,0:T(2,128)S(1)} %add.39), channel_id=1, source_target_pairs={{0,128},{8,136},{16,144},{24,152},{32,160},{40,168},{48,176},{56,1... | collective-permute-start | bytes 3080 | tf_op jit(solution)/shard_map/ppermute | solution.py:428
  106.6 3.6 %collective-permute-start.28 = (f32[2,128]{1,0:T(2,128)S(1)}, f32[2,128]{1,0:T(2,128)S(1)}, u32[]{:S(2)}, u32[]{:S(2)}) collective-permute-start(f32[2,128]{1,0:T(2,128)S(1)} %add.40), channel_id=1, source_target_pairs={{0,1},{1,0},{2,3},{3,2},{4,5},{5,4},{6,7},{7,6},{8,9},{9,8},{10,11... | collective-permute-start | bytes 3080 | tf_op jit(solution)/shard_map/ppermute | solution.py:428
  110.2 9.0 %collective-permute-start.29 = (f32[2,128]{1,0:T(2,128)S(1)}, f32[2,128]{1,0:T(2,128)S(1)}, u32[]{:S(2)}, u32[]{:S(2)}) collective-permute-start(f32[2,128]{1,0:T(2,128)S(1)} %add.41), channel_id=1, source_target_pairs={{0,2},{1,3},{2,0},{3,1},{4,6},{5,7},{6,4},{7,5},{8,10},{9,11},{10,... | collective-permute-start | bytes 3080 | tf_op jit(solution)/shard_map/ppermute | solution.py:428
  113.4 15.7 %collective-permute-start.13 = (bf16[512,256]{1,0:T(8,128)(2,1)S(1)}, bf16[512,256]{1,0:T(8,128)(2,1)S(1)}, u32[]{:S(2)}, u32[]{:S(2)}) collective-permute-start(bf16[512,256]{1,0:T(8,128)(2,1)S(1)} %get-tuple-element.57), channel_id=1, source_target_pairs={{16,0},{24,8},{32,16},{40,24},{48,32},{56,40},{64,48},{72,56},{80,... | collective-permute-start | bytes 786440 | tf_op jit(solution)/shard_map/ppermute | solution.py:423
  116.3 14.8 %collective-permute-start.11 = (bf16[512,256]{1,0:T(8,128)(2,1)S(1)}, bf16[512,256]{1,0:T(8,128)(2,1)S(1)}, u32[]{:S(2)}, u32[]{:S(2)}) collective-permute-start(bf16[512,256]{1,0:T(8,128)(2,1)S(1)} %get-tuple-element.53), channel_id=1, source_target_pairs={{16,0},{24,8},{32,16},{40,24},{48,32},{56,40},{64,48},{72,56},{80,... | collective-permute-start | bytes 786440 | tf_op jit(solution)/shard_map/ppermute | solution.py:423
  119.2 3.7 %collective-permute-start.30 = (f32[2,128]{1,0:T(2,128)S(1)}, f32[2,128]{1,0:T(2,128)S(1)}, u32[]{:S(2)}, u32[]{:S(2)}) collective-permute-start(f32[2,128]{1,0:T(2,128)S(1)} %add.42), channel_id=1, source_target_pairs={{0,4},{1,5},{2,6},{3,7},{4,0},{5,1},{6,2},{7,3},{8,12},{9,13},{10,... | collective-permute-start | bytes 3080 | tf_op jit(solution)/shard_map/ppermute | solution.py:428
  122.9 28.4 %collective-permute-start.10 = (bf16[256,1024]{1,0:T(8,128)(2,1)S(1)}, bf16[256,1024]{1,0:T(8,128)(2,1)S(1)}, u32[]{:S(2)}, u32[]{:S(2)}) collective-permute-start(bf16[256,1024]{1,0:T(8,128)(2,1)S(1)} %split_dq.1), channel_id=1, source_target_pairs={{0,8},{8,0},{16,24},{24,16},{32,40},{40,32},{48,56},{56,48},{64,72... | collective-permute-start | bytes 1572872 | tf_op jit(solution)/shard_map/ppermute | solution.py:428
  123.0 11.1 %collective-permute-start.18 = (bf16[512,256]{1,0:T(8,128)(2,1)S(1)}, bf16[512,256]{1,0:T(8,128)(2,1)S(1)}, u32[]{:S(2)}, u32[]{:S(2)}) collective-permute-start(bf16[512,256]{1,0:T(8,128)(2,1)S(1)} %add_back.7), channel_id=1, source_target_pairs={{16,0},{24,8},{32,16},{40,24},{48,32},{56,40},{64,48},{72,56},{80,... | collective-permute-start | bytes 786440 | tf_op jit(solution)/shard_map/ppermute | solution.py:423
  127.2 12.4 %collective-permute-start.16 = (bf16[512,256]{1,0:T(8,128)(2,1)S(1)}, bf16[512,256]{1,0:T(8,128)(2,1)S(1)}, u32[]{:S(2)}, u32[]{:S(2)}) collective-permute-start(bf16[512,256]{1,0:T(8,128)(2,1)S(1)} %add_back.6), channel_id=1, source_target_pairs={{16,0},{24,8},{32,16},{40,24},{48,32},{56,40},{64,48},{72,56},{80,... | collective-permute-start | bytes 786440 | tf_op jit(solution)/shard_map/ppermute | solution.py:423
  129.2 16.0 %collective-permute-start.14 = (bf16[512,256]{1,0:T(8,128)(2,1)S(1)}, bf16[512,256]{1,0:T(8,128)(2,1)S(1)}, u32[]{:S(2)}, u32[]{:S(2)}) collective-permute-start(bf16[512,256]{1,0:T(8,128)(2,1)S(1)} %add_back.5), channel_id=1, source_target_pairs={{16,0},{24,8},{32,16},{40,24},{48,32},{56,40},{64,48},{72,56},{80,... | collective-permute-start | bytes 786440 | tf_op jit(solution)/shard_map/ppermute | solution.py:423
  131.2 19.3 %collective-permute-start.12 = (bf16[512,256]{1,0:T(8,128)(2,1)S(1)}, bf16[512,256]{1,0:T(8,128)(2,1)S(1)}, u32[]{:S(2)}, u32[]{:S(2)}) collective-permute-start(bf16[512,256]{1,0:T(8,128)(2,1)S(1)} %add_back.4), channel_id=1, source_target_pairs={{16,0},{24,8},{32,16},{40,24},{48,32},{56,40},{64,48},{72,56},{80,... | collective-permute-start | bytes 786440 | tf_op jit(solution)/shard_map/ppermute | solution.py:423
  134.4 18.0 %collective-permute-start.22 = (bf16[256,256]{1,0:T(8,128)(2,1)S(1)}, bf16[256,256]{1,0:T(8,128)(2,1)S(1)}, u32[]{:S(2)}, u32[]{:S(2)}) collective-permute-start(bf16[256,256]{1,0:T(8,128)(2,1)S(1)} %get-tuple-element.70), channel_id=1, source_target_pairs={{0,8},{8,0},{16,24},{24,16},{32,40},{40,32},{48,56},{56,48},{64,72... | collective-permute-start | bytes 393224 | tf_op jit(solution)/shard_map/ppermute | solution.py:428
  139.8 12.6 %collective-permute-start.21 = (bf16[256,256]{1,0:T(8,128)(2,1)S(1)}, bf16[256,256]{1,0:T(8,128)(2,1)S(1)}, u32[]{:S(2)}, u32[]{:S(2)}) collective-permute-start(bf16[256,256]{1,0:T(8,128)(2,1)S(1)} %get-tuple-element.69), channel_id=1, source_target_pairs={{0,8},{8,0},{16,24},{24,16},{32,40},{40,32},{48,56},{56,48},{64,72... | collective-permute-start | bytes 393224 | tf_op jit(solution)/shard_map/ppermute | solution.py:428
  145.5 7.0 %collective-permute-start.20 = (bf16[256,256]{1,0:T(8,128)(2,1)S(1)}, bf16[256,256]{1,0:T(8,128)(2,1)S(1)}, u32[]{:S(2)}, u32[]{:S(2)}) collective-permute-start(bf16[256,256]{1,0:T(8,128)(2,1)S(1)} %get-tuple-element.68), channel_id=1, source_target_pairs={{0,8},{8,0},{16,24},{24,16},{32,40},{40,32},{48,56},{56,48},{64,72... | collective-permute-start | bytes 393224 | tf_op jit(solution)/shard_map/ppermute | solution.py:428
  150.7 1.7 %collective-permute-start.19 = (bf16[256,256]{1,0:T(8,128)(2,1)S(1)}, bf16[256,256]{1,0:T(8,128)(2,1)S(1)}, u32[]{:S(2)}, u32[]{:S(2)}) collective-permute-start(bf16[256,256]{1,0:T(8,128)(2,1)S(1)} %get-tuple-element.67), channel_id=1, source_target_pairs={{0,8},{8,0},{16,24},{24,16},{32,40},{40,32},{48,56},{56,48},{64,72... | collective-permute-start | bytes 393224 | tf_op jit(solution)/shard_map/ppermute | solution.py:428
  (9 other events, 47.3 us)

commit v2 on v1

--- a/solution.py
+++ b/solution.py
@@ -22,6 +22,7 @@
 f32 = jnp.float32
 bf16 = jnp.bfloat16
 VM = pl.BlockSpec(memory_space=pltpu.VMEM)
+ANY = pl.BlockSpec(memory_space=pl.ANY)
 SM = pl.BlockSpec(memory_space=pltpu.SMEM)
 PARAMS = pltpu.CompilerParams(vmem_limit_bytes=24 * 1024 * 1024)
 SMALL = pltpu.CompilerParams(vmem_limit_bytes=12 * 1024 * 1024)
@@ -62,33 +63,31 @@
     )(idx, k, v)
 
 
-def join_kv_kernel(idx, k, v, recv, *outs):
+def join_kv_kernel(h0, n, idx, k, v, recv, *rest):
+    out = rest[-1]
     a = idx[0] % 2
     mine = pl.ds(al(a * T, T), T)
     theirs = pl.ds(al((1 - a) * T, T), T)
-    h = 0
-    for out, n in zip(outs, CHUNKS):
-        for i in range(n):
-            cols = pl.ds(al(a * (NKV * D) + h * D, D), D)
-            out[mine, 2 * i * D : (2 * i + 1) * D] = k[:, cols]
-            out[mine, (2 * i + 1) * D : (2 * i + 2) * D] = v[:, cols]
-            out[theirs, 2 * i * D : (2 * i + 2) * D] = recv[:, 2 * h * D : (2 * h + 2) * D]
-            h += 1
-
-
-def join_kv(idx, k, v, recv):
-    return pl.pallas_call(
-        join_kv_kernel,
-        out_shape=[jax.ShapeDtypeStruct((TC, 2 * n * D), bf16) for n in CHUNKS],
-        in_specs=[SM, VM, VM, VM],
-        out_specs=[VM] * len(CHUNKS),
-        compiler_params=SMALL,
-        cost_estimate=cost(1),
+    for i in range(n):
+        cols = pl.ds(al(a * (NKV * D) + (h0 + i) * D, D), D)
+        out[mine, 2 * i * D : (2 * i + 1) * D] = k[:, cols]
+        out[mine, (2 * i + 1) * D : (2 * i + 2) * D] = v[:, cols]
+    out[theirs, :] = recv[:, 2 * h0 * D : 2 * (h0 + n) * D]
+
+
+def join_kv(h0, n, idx, k, v, recv, after):
+    return pl.pallas_call(
+        functools.partial(join_kv_kernel, h0, n),
+        out_shape=jax.ShapeDtypeStruct((TC, 2 * n * D), bf16),
+        in_specs=[SM, VM, VM, VM] + [ANY] * len(after),
+        out_specs=VM,
+        compiler_params=SMALL,
+        cost_estimate=cost(0.2),
         name="join_kv",
-    )(idx, k, v, recv)
-
-
-def split_q_kernel(idx, q, do, send):
+    )(idx, k, v, recv, *after)
+
+
+def split_q_kernel(idx, q, do, after, send):
     other = 1 - idx[0] % 2
     w = 2 * NKV * D
     cols = pl.ds(al(other * w, w), w)
@@ -96,16 +95,16 @@
     send[:, w:] = do[:, cols]
 
 
-def split_q(idx, q, do):
+def split_q(idx, q, do, after):
     return pl.pallas_call(
         split_q_kernel,
         out_shape=jax.ShapeDtypeStruct((T, 4 * NKV * D), bf16),
-        in_specs=[SM, VM, VM],
-        out_specs=VM,
-        compiler_params=SMALL,
-        cost_estimate=cost(1.5),
+        in_specs=[SM, VM, VM, ANY],
+        out_specs=VM,
+        compiler_params=SMALL,
+        cost_estimate=cost(0.2),
         name="split_q",
-    )(idx, q, do)
+    )(idx, q, do, after)
 
 
 def join_q_kernel(idx, q, do, recv, qa, doa):
@@ -143,10 +142,12 @@
 
 
 def attn_kernel(
-    idx, starts, flags, qg, kg, q, do, kv0, kv1, kv2,
+    n_after, idx, starts, flags, qg, kg, gains_in, q, do, kv0, kv1, kv2, *rest
+):
+    (
     dq, d2, d1, d0, gains,
     bias, s_scr, dp_scr, pb_scr, ds_scr, kn_scr, qn_scr, do_scr, dk_acc, dv_acc,
-):
+    ) = rest[n_after:]
     step = pl.program_id(0)
     first = (idx[0] // 2) * TC
 
@@ -156,7 +157,7 @@
 
     @pl.when(step == 0)
     def _():
-        gains[...] = jnp.zeros_like(gains)
+        gains[...] = gains_in[...]
         for qb in range(2):
             base = first + qb * T
             qpos = base + lax.broadcasted_iota(jnp.int32, (1, T), 1)
@@ -270,12 +271,13 @@
     gains[1] += dkg
 
 
-def attn(h0, n, idx, starts, flags, qg, kg, q, do, kv0, kv1, kv2):
+def attn(h0, n, idx, starts, flags, qg, kg, gains, q, do, kv0, kv1, kv2, after):
     col = pl.BlockSpec((TC, 2 * D), lambda i: (0, i))
     qcol = pl.BlockSpec((TC, 2 * D), lambda i: (0, h0 + i))
     full = pl.BlockSpec((1, D), lambda i: (0, 0))
-    return pl.pallas_call(
-        attn_kernel,
+    gain = pl.BlockSpec((2, 8, D), lambda i: (0, 0, 0))
+    return pl.pallas_call(
+        functools.partial(attn_kernel, len(after)),
         grid=(n,),
         out_shape=[
             jax.ShapeDtypeStruct((TC, 2 * n * D), bf16),
@@ -284,8 +286,8 @@
             jax.ShapeDtypeStruct((TC, 2 * n * D), f32),
             jax.ShapeDtypeStruct((2, 8, D), f32),
         ],
-        in_specs=[SM, SM, SM, full, full, qcol, qcol, col, col, col],
-        out_specs=[col, col, col, col, pl.BlockSpec((2, 8, D), lambda i: (0, 0, 0))],
+        in_specs=[SM, SM, SM, full, full, gain, qcol, qcol, col, col, col] + [ANY] * len(after),
+        out_specs=[col, col, col, col, gain],
         scratch_shapes=[
             pltpu.VMEM((2, 4, T, T), f32),
             pltpu.VMEM((4, T, T), f32),
@@ -301,23 +303,23 @@
         compiler_params=PARAMS,
         cost_estimate=cost(6 * n),
         name="attn",
-    )(idx, starts, flags, qg, kg, q, do, kv0, kv1, kv2)
-
-
-def add_kernel(x, y, out):
-    out[...] = (x[...] + y[...].astype(f32)).astype(bf16)
-
-
-def add_back(d1, r1):
+    )(idx, starts, flags, qg, kg, gains, q, do, kv0, kv1, kv2, *after)
+
+
+def add_kernel(x, y, *rest):
+    rest[-1][...] = (x[...] + y[...].astype(f32)).astype(bf16)
+
+
+def add_back(d1, r1, *after):
     return pl.pallas_call(
         add_kernel,
         out_shape=jax.ShapeDtypeStruct(r1.shape, bf16),
-        in_specs=[VM, VM],
-        out_specs=VM,
-        compiler_params=SMALL,
-        cost_estimate=cost(1),
+        in_specs=[VM, VM] + [ANY] * len(after),
+        out_specs=VM,
+        compiler_params=SMALL,
+        cost_estimate=cost(0.2),
         name="add_back",
-    )(d1, r1)
+    )(d1, r1, *after)
 
 
 def finish_kernel(n, idx, kg, d0, r2, kv, keep, send):
@@ -428,45 +430,89 @@
     return lax.ppermute(x, axis, [(i, i ^ bit) for i in range(n)])
 
 
-def total(x):
-    for bit in (1, 2, 4, 8, 16):
-        x = x + swap(x, "ctx", bit)
-    for bit in (1, 2, 4):
-        x = x + swap(x, "dp", bit)
-    return x
+def fold_kernel(gains, *rest):
+    rest[-1][...] = jnp.sum(gains[...], axis=1)
+
+
+def fold(gains, *after):
+    return pl.pallas_call(
+        fold_kernel,
+        out_shape=jax.ShapeDtypeStruct((2, D), f32),
+        in_specs=[VM] + [ANY] * len(after),
+        out_specs=VM,
+        compiler_params=SMALL,
+        cost_estimate=cost(0.1),
+        name="fold",
+    )(gains, *after)
+
+
+def plus_kernel(x, y, *rest):
+    rest[-1][...] = x[...] + y[...]
+
+
+def plus(x, y, *after):
+    return pl.pallas_call(
+        plus_kernel,
+        out_shape=jax.ShapeDtypeStruct(x.shape, f32),
+        in_specs=[VM, VM] + [ANY] * len(after),
+        out_specs=VM,
+        compiler_params=SMALL,
+        cost_estimate=cost(0.1),
+        name="plus",
+    )(x, y, *after)
 
 
 def on_device(q_raw, raw_keys_input, values, grad_out, q_gain, k_gain, doc_starts, flags):
     idx = lax.axis_index("ctx").astype(jnp.int32).reshape(1)
     q, k, v, do = q_raw[0], raw_keys_input[0], values[0], grad_out[0]
     qg, kg = q_gain.reshape(1, D), k_gain.reshape(1, D)
-
-    kv0 = join_kv(idx, k, v, swap(split_kv(idx, k, v), "ctx", 1))
-    qa, doa = join_q(idx, q, do, swap(split_q(idx, q, do), "ctx", 1))
-    kv1 = [along(x, 2) for x in kv0]
+    count = len(CHUNKS)
+    first = [sum(CHUNKS[:c]) for c in range(count)]
+
+    send = split_kv(idx, k, v)
+    recv = swap(send, "ctx", 1)
+    kv0, kv1, kv2 = [], [], []
+    for c, n in enumerate(CHUNKS):
+        kv0.append(join_kv(first[c], n, idx, k, v, recv, kv1[c - 2 : c - 1] if c >= 2 else []))
+        kv1.append(along(kv0[c], 2))
     kv2 = [along(x, 2) for x in kv1]
-
-    dqs, d1s, d0s, r1s, gains = [], [], [], [], None
-    h0 = 0
+    qa, doa = join_q(idx, q, do, swap(split_q(idx, q, do, send), "ctx", 1))
+
+    last = count - 1
+    dqs, d0s, sums, r2s, gains = [], [], [], [], jnp.zeros((2, 8, D), f32)
     for c, n in enumerate(CHUNKS):
-        dq, d2, d1, d0, gain = attn(
-            h0, n, idx, doc_starts, flags, qg, kg, qa, doa, kv0[c], kv1[c], kv2[c]
+        after = kv1[c + 1 : c + 2]
+        if c >= 2:
+            after = after + [sums[c - 2]]
+        if c >= 3:
+            after = after + [r2s[c - 3]]
+        dq, d2, d1, d0, gains = attn(
+            first[c], n, idx, doc_starts, flags, qg, kg, gains, qa, doa, kv0[c], kv1[c], kv2[c], after
         )
-        h0 += n
         dqs.append(dq)
-        d1s.append(d1)
         d0s.append(d0)
-        r1s.append(along(d2, -2))
-        gains = gain if gains is None else gains + gain
+        r1 = along(d2, -2)
+        if c < last:
+            sums.append(add_back(d1, r1))
+            r2s.append(along(sums[c], -2))
+    gain = fold(gains, sums[last - 1])
+    gain = plus(gain, swap(gain, "ctx", 1))
+    gain = plus(gain, swap(gain, "ctx", 2))
+    sums.append(add_back(d1, r1, gain))
+    r2s.append(along(sums[last], -2))
+    gain = plus(gain, swap(gain, "dp", 4), sums[last], *r2s[last - 2 : last - 1])
+    gain = plus(gain, swap(gain, "dp", 1), r2s[last - 1])
+    gain = plus(gain, swap(gain, "dp", 2))
+    gain = plus(gain, swap(gain, "ctx", 4), r2s[last])
+    gain = plus(gain, swap(gain, "ctx", 16))
+    gain = plus(gain, swap(gain, "ctx", 8))
     keeps, recvs = [], []
     for c, n in enumerate(CHUNKS):
-        r2 = along(add_back(d1s[c], r1s[c]), -2)
-        keep, send = finish(n, idx, kg, d0s[c], r2, kv0[c])
+        keep, send = finish(n, idx, kg, d0s[c], r2s[c], kv0[c])
         keeps.append(keep)
         recvs.append(swap(send, "ctx", 1))
     dk, dv = out_kv(idx, keeps, recvs)
     dq = out_q(idx, dqs, swap(split_dq(idx, dqs), "ctx", 1))
-    gain = total(jnp.sum(gains, axis=1))
     return dq[None], dk[None], dv[None], gain[0], gain[1]
 
 

time: 155 us -> 139 us (0.90)
  waiting for transfers between devices: 60.3 us -> 43.9 us
    ppermute x16, waiting for transfers between devices: 33 us -> 12.4 us  [along(): lax.ppermute(x, 'ctx', [(i, i + distance) for i in range(n) if 0 <= i + d...]
    ppermute x15, waiting for transfers between devices: 27.3 us -> 31.6 us  [swap(): return lax.ppermute(x, axis, [(i, i ^ bit) for i in range(n)])]
    pallas_call x5 -> x17, Pallas kernels: 25.8 us -> 25.9 us  [the longest x4 25.6 us: attn(): pl.pallas_call(functools.partial(attn_kernel, len(after)), grid=(n,), out...]
  transfers between devices with their start and end apart: 31 -> 31, of which waited for: 16 -> 13; matrix products, arithmetic and copies ran while one was open for 0% -> 0% of each run, Pallas kernels for 19% -> 20%
where the time goes in v2:
time: 139 us
  starting transfers between devices  59.2 us (43%)
  waiting for transfers between devices  43.9 us (32%)
  Pallas kernels  29.8 us (21%)
  local copies, waits for them, and re-layouts  4.7 us (3%)
    ppermute x16, starting transfers between devices, along(): lax.ppermute(x, 'ctx', [(i, i + distance) for i in range(n) if 0 <= i + d...  50.7 us
    ppermute x15, waiting for transfers between devices, swap(): return lax.ppermute(x, axis, [(i, i ^ bit) for i in range(n)])  31.6 us
    pallas_call x4, Pallas kernels, attn(): pl.pallas_call(functools.partial(attn_kernel, len(after)), grid=(n,), out...  25.6 us
    ppermute x16, waiting for transfers between devices, along(): lax.ppermute(x, 'ctx', [(i, i + distance) for i in range(n) if 0 <= i + d...  12.4 us
    ppermute x15, starting transfers between devices, swap(): return lax.ppermute(x, axis, [(i, i ^ bit) for i in range(n)])  8.56 us
    unnamed x20, local copies, waits for them, and re-layouts  4.17 us
  transfers between devices with their start and end apart: 31, of which 13 were waited for; matrix products, arithmetic and copies ran while one was open for 0% of the time, Pallas kernels for 20%

profile of v2, /device:TPU:6, one launch (start us, length us, event | category | flops | bytes accessed | tf_op | source)
XLA Modules:
  0.0 138.8 jit_solution(8300265494771670607)
XLA Ops:
  4.9 2.9 %collective-permute-done.1.recv = bf16[256,1024]{1,0:T(8,128)(2,1)S(1)} collective-permute-done((bf16[256,1024]{1,0:T(8,128)(2,1)S(1)}, bf16[256,1024]{1,0:T(8,128)(2,1)S(1)}, u32[]{:S(2)}, u32[]{:S(2)}) %collective-permute-start.1) | collective-permute-done | bytes 524320 | tf_op jit(solution)/shard_map/ppermute | solution.py:430
  7.9 3.8 %collective-permute-start.2 = (bf16[512,256]{1,0:T(8,128)(2,1)S(1)}, bf16[512,256]{1,0:T(8,128)(2,1)S(1)}, u32[]{:S(2)}, u32[]{:S(2)}) collective-permute-start(bf16[512,256]{1,0:T(8,128)(2,1)S(1)} %join_kv.4.kv0.kv), channel_id=1, source_target_pairs={{0,16},{8,24},{16,32},{24,40},{32,48},{40,56},{48,64},{56,72},{64,... | collective-permute-start | bytes 786440 | tf_op jit(solution)/shard_map/ppermute | solution.py:425
  11.8 3.8 %collective-permute-start.4 = (bf16[512,256]{1,0:T(8,128)(2,1)S(1)}, bf16[512,256]{1,0:T(8,128)(2,1)S(1)}, u32[]{:S(2)}, u32[]{:S(2)}) collective-permute-start(bf16[512,256]{1,0:T(8,128)(2,1)S(1)} %join_kv.5.kv0.kv), channel_id=1, source_target_pairs={{0,16},{8,24},{16,32},{24,40},{32,48},{40,56},{48,64},{56,72},{64,... | collective-permute-start | bytes 786440 | tf_op jit(solution)/shard_map/ppermute | solution.py:425
  15.6 8.0 %collective-permute-done.2.kv1.rest_0_ = bf16[512,256]{1,0:T(8,128)(2,1)S(1)} collective-permute-done((bf16[512,256]{1,0:T(8,128)(2,1)S(1)}, bf16[512,256]{1,0:T(8,128)(2,1)S(1)}, u32[]{:S(2)}, u32[]{:S(2)}) %collective-permute-start.2) | collective-permute-done | bytes 262176 | tf_op jit(solution)/shard_map/ppermute | solution.py:425
  23.6 1.9 %collective-permute-start.3 = (bf16[512,256]{1,0:T(8,128)(2,1)S(1)}, bf16[512,256]{1,0:T(8,128)(2,1)S(1)}, u32[]{:S(2)}, u32[]{:S(2)}) collective-permute-start(bf16[512,256]{1,0:T(8,128)(2,1)S(1)} %collective-permute-done.2.kv1.rest_0_), channel_id=1, source_target_pairs={{0,16},{8,24},{16,32},{24,40},{32,48},{40,56},{48,64},{56,72},{64,... | collective-permute-start | bytes 786440 | tf_op jit(solution)/shard_map/ppermute | solution.py:425
  25.6 1.9 %collective-permute-start.6 = (bf16[512,256]{1,0:T(8,128)(2,1)S(1)}, bf16[512,256]{1,0:T(8,128)(2,1)S(1)}, u32[]{:S(2)}, u32[]{:S(2)}) collective-permute-start(bf16[512,256]{1,0:T(8,128)(2,1)S(1)} %join_kv.6.kv0.kv), channel_id=1, source_target_pairs={{0,16},{8,24},{16,32},{24,40},{32,48},{40,56},{48,64},{56,72},{64,... | collective-permute-start | bytes 786440 | tf_op jit(solution)/shard_map/ppermute | solution.py:425
  28.8 2.4 %collective-permute-start.8 = (bf16[512,256]{1,0:T(8,128)(2,1)S(1)}, bf16[512,256]{1,0:T(8,128)(2,1)S(1)}, u32[]{:S(2)}, u32[]{:S(2)}) collective-permute-start(bf16[512,256]{1,0:T(8,128)(2,1)S(1)} %join_kv.7.kv0.kv), channel_id=1, source_target_pairs={{0,16},{8,24},{16,32},{24,40},{32,48},{40,56},{48,64},{56,72},{64,... | collective-permute-start | bytes 786440 | tf_op jit(solution)/shard_map/ppermute | solution.py:425
  31.2 5.6 %collective-permute-start.5 = (bf16[512,256]{1,0:T(8,128)(2,1)S(1)}, bf16[512,256]{1,0:T(8,128)(2,1)S(1)}, u32[]{:S(2)}, u32[]{:S(2)}) collective-permute-start(bf16[512,256]{1,0:T(8,128)(2,1)S(1)} %collective-permute-done.4.rest_0_.kv1), channel_id=1, source_target_pairs={{0,16},{8,24},{16,32},{24,40},{32,48},{40,56},{48,64},{56,72},{64,... | collective-permute-start | bytes 786440 | tf_op jit(solution)/shard_map/ppermute | solution.py:425
  39.0 6.4 %attn.4 = (bf16[512,256]{1,0:T(8,128)(2,1)S(1)}, bf16[512,256]{1,0:T(8,128)(2,1)S(1)}, f32[512,256]{1,0:T(8,128)S(1)}, f32[512,256]{1,0:T(8,128)S(1)}, f32[2,8,128]{2,1,0:T(8,128)S(1)}) custom-call(s32[1]{0:T(128)} %bitcast.idx, s32[1,4]{1,0:T(1,128)S(1)} %copy-done.6, s32[1,32]{1,0:T(1,128)S(1)} %copy-done.7, f32[1,128]{1,0:T(1,128)S(1)} %bitcast.28, ...), custom_call_target="tpu_custom_call" | custom-call | flops 6000000000 | bytes 6000000 | tf_op jit(solution)/shard_map/attn/pallas_call | solution.py:279
  45.4 2.5 %collective-permute-start.9 = (bf16[512,256]{1,0:T(8,128)(2,1)S(1)}, bf16[512,256]{1,0:T(8,128)(2,1)S(1)}, u32[]{:S(2)}, u32[]{:S(2)}) collective-permute-start(bf16[512,256]{1,0:T(8,128)(2,1)S(1)} %get-tuple-element.44), channel_id=1, source_target_pairs={{16,0},{24,8},{32,16},{40,24},{48,32},{56,40},{64,48},{72,56},{80,... | collective-permute-start | bytes 786440 | tf_op jit(solution)/shard_map/ppermute | solution.py:425
  48.0 3.5 %collective-permute-start.7 = (bf16[512,256]{1,0:T(8,128)(2,1)S(1)}, bf16[512,256]{1,0:T(8,128)(2,1)S(1)}, u32[]{:S(2)}, u32[]{:S(2)}) collective-permute-start(bf16[512,256]{1,0:T(8,128)(2,1)S(1)} %collective-permute-done.6.rest_0_.kv1), channel_id=1, source_target_pairs={{0,16},{8,24},{16,32},{24,40},{32,48},{40,56},{48,64},{56,72},{64,... | collective-permute-start | bytes 786440 | tf_op jit(solution)/shard_map/ppermute | solution.py:425
  51.5 1.8 %collective-permute-done.5.kv2 = bf16[512,256]{1,0:T(8,128)(2,1)S(1)} collective-permute-done((bf16[512,256]{1,0:T(8,128)(2,1)S(1)}, bf16[512,256]{1,0:T(8,128)(2,1)S(1)}, u32[]{:S(2)}, u32[]{:S(2)}) %collective-permute-start.5) | collective-permute-done | bytes 262176 | tf_op jit(solution)/shard_map/ppermute | solution.py:425
  53.3 6.4 %attn.5 = (bf16[512,256]{1,0:T(8,128)(2,1)S(1)}, bf16[512,256]{1,0:T(8,128)(2,1)S(1)}, f32[512,256]{1,0:T(8,128)S(1)}, f32[512,256]{1,0:T(8,128)S(1)}, f32[2,8,128]{2,1,0:T(8,128)S(1)}) custom-call(s32[1]{0:T(128)} %bitcast.idx, s32[1,4]{1,0:T(1,128)S(1)} %copy-done.6, s32[1,32]{1,0:T(1,128)S(1)} %copy-done.7, f32[1,128]{1,0:T(1,128)S(1)} %bitcast.29, ...), custom_call_target="tpu_custom_call" | custom-call | flops 6000000000 | bytes 6000000 | tf_op jit(solution)/shard_map/attn/pallas_call | solution.py:279
  59.7 4.3 %collective-permute-start.11 = (bf16[512,256]{1,0:T(8,128)(2,1)S(1)}, bf16[512,256]{1,0:T(8,128)(2,1)S(1)}, u32[]{:S(2)}, u32[]{:S(2)}) collective-permute-start(bf16[512,256]{1,0:T(8,128)(2,1)S(1)} %get-tuple-element.48), channel_id=1, source_target_pairs={{16,0},{24,8},{32,16},{40,24},{48,32},{56,40},{64,48},{72,56},{80,... | collective-permute-start | bytes 786440 | tf_op jit(solution)/shard_map/ppermute | solution.py:425
  64.1 1.9 %collective-permute-start.10 = (bf16[512,256]{1,0:T(8,128)(2,1)S(1)}, bf16[512,256]{1,0:T(8,128)(2,1)S(1)}, u32[]{:S(2)}, u32[]{:S(2)}) collective-permute-start(bf16[512,256]{1,0:T(8,128)(2,1)S(1)} %collective-permute-done.8.rest_0_.kv1), channel_id=1, source_target_pairs={{0,16},{8,24},{16,32},{24,40},{32,48},{40,56},{48,64},{56,72},{64,... | collective-permute-start | bytes 786440 | tf_op jit(solution)/shard_map/ppermute | solution.py:425
  66.1 7.8 %collective-permute-start.12 = (bf16[512,256]{1,0:T(8,128)(2,1)S(1)}, bf16[512,256]{1,0:T(8,128)(2,1)S(1)}, u32[]{:S(2)}, u32[]{:S(2)}) collective-permute-start(bf16[512,256]{1,0:T(8,128)(2,1)S(1)} %add_back.4.rest_1_), channel_id=1, source_target_pairs={{16,0},{24,8},{32,16},{40,24},{48,32},{56,40},{64,48},{72,56},{80,... | collective-permute-start | bytes 786440 | tf_op jit(solution)/shard_map/ppermute | solution.py:425
  73.9 6.4 %attn.6 = (bf16[512,256]{1,0:T(8,128)(2,1)S(1)}, bf16[512,256]{1,0:T(8,128)(2,1)S(1)}, f32[512,256]{1,0:T(8,128)S(1)}, f32[512,256]{1,0:T(8,128)S(1)}, f32[2,8,128]{2,1,0:T(8,128)S(1)}) custom-call(s32[1]{0:T(128)} %bitcast.idx, s32[1,4]{1,0:T(1,128)S(1)} %copy-done.6, s32[1,32]{1,0:T(1,128)S(1)} %copy-done.7, f32[1,128]{1,0:T(1,128)S(1)} %bitcast.30, ...), custom_call_target="tpu_custom_call" | custom-call | flops 6000000000 | bytes 6000000 | tf_op jit(solution)/shard_map/attn/pallas_call | solution.py:279
  80.3 1.9 %collective-permute-start.15 = (bf16[512,256]{1,0:T(8,128)(2,1)S(1)}, bf16[512,256]{1,0:T(8,128)(2,1)S(1)}, u32[]{:S(2)}, u32[]{:S(2)}) collective-permute-start(bf16[512,256]{1,0:T(8,128)(2,1)S(1)} %get-tuple-element.56), channel_id=1, source_target_pairs={{16,0},{24,8},{32,16},{40,24},{48,32},{56,40},{64,48},{72,56},{80,... | collective-permute-start | bytes 786440 | tf_op jit(solution)/shard_map/ppermute | solution.py:425
  82.3 6.4 %attn.7 = (bf16[512,256]{1,0:T(8,128)(2,1)S(1)}, bf16[512,256]{1,0:T(8,128)(2,1)S(1)}, f32[512,256]{1,0:T(8,128)S(1)}, f32[512,256]{1,0:T(8,128)S(1)}, f32[2,8,128]{2,1,0:T(8,128)S(1)}) custom-call(s32[1]{0:T(128)} %bitcast.idx, s32[1,4]{1,0:T(1,128)S(1)} %copy-done.6, s32[1,32]{1,0:T(1,128)S(1)} %copy-done.7, f32[1,128]{1,0:T(1,128)S(1)} %bitcast.31, ...), custom_call_target="tpu_custom_call" | custom-call | flops 6000000000 | bytes 6000000 | tf_op jit(solution)/shard_map/attn/pallas_call | solution.py:279
  88.7 3.2 %collective-permute-start.17 = (bf16[512,256]{1,0:T(8,128)(2,1)S(1)}, bf16[512,256]{1,0:T(8,128)(2,1)S(1)}, u32[]{:S(2)}, u32[]{:S(2)}) collective-permute-start(bf16[512,256]{1,0:T(8,128)(2,1)S(1)} %get-tuple-element.60), channel_id=1, source_target_pairs={{16,0},{24,8},{32,16},{40,24},{48,32},{56,40},{64,48},{72,56},{80,... | collective-permute-start | bytes 786440 | tf_op jit(solution)/shard_map/ppermute | solution.py:425
  91.9 2.2 %collective-permute-start.14 = (bf16[512,256]{1,0:T(8,128)(2,1)S(1)}, bf16[512,256]{1,0:T(8,128)(2,1)S(1)}, u32[]{:S(2)}, u32[]{:S(2)}) collective-permute-start(bf16[512,256]{1,0:T(8,128)(2,1)S(1)} %add_back.5.rest_0_), channel_id=1, source_target_pairs={{16,0},{24,8},{32,16},{40,24},{48,32},{56,40},{64,48},{72,56},{80,... | collective-permute-start | bytes 786440 | tf_op jit(solution)/shard_map/ppermute | solution.py:425
  94.2 1.9 %collective-permute-start.16 = (bf16[512,256]{1,0:T(8,128)(2,1)S(1)}, bf16[512,256]{1,0:T(8,128)(2,1)S(1)}, u32[]{:S(2)}, u32[]{:S(2)}) collective-permute-start(bf16[512,256]{1,0:T(8,128)(2,1)S(1)} %add_back.6.rest_0_), channel_id=1, source_target_pairs={{16,0},{24,8},{32,16},{40,24},{48,32},{56,40},{64,48},{72,56},{80,... | collective-permute-start | bytes 786440 | tf_op jit(solution)/shard_map/ppermute | solution.py:425
  98.2 2.0 %collective-permute-start.19 = (f32[2,128]{1,0:T(2,128)S(1)}, f32[2,128]{1,0:T(2,128)S(1)}, u32[]{:S(2)}, u32[]{:S(2)}) collective-permute-start(f32[2,128]{1,0:T(2,128)S(1)} %plus.8.x), channel_id=1, source_target_pairs={{0,16},{8,24},{16,0},{24,8},{32,48},{40,56},{48,32},{56,40},{64,80... | collective-permute-start | bytes 3080 | tf_op jit(solution)/shard_map/ppermute | solution.py:430
  100.2 7.4 %collective-permute-done.19.y = f32[2,128]{1,0:T(2,128)S(1)} collective-permute-done((f32[2,128]{1,0:T(2,128)S(1)}, f32[2,128]{1,0:T(2,128)S(1)}, u32[]{:S(2)}, u32[]{:S(2)}) %collective-permute-start.19) | collective-permute-done | bytes 1056 | tf_op jit(solution)/shard_map/ppermute | solution.py:430
  107.7 1.9 %collective-permute-start.20 = (bf16[512,256]{1,0:T(8,128)(2,1)S(1)}, bf16[512,256]{1,0:T(8,128)(2,1)S(1)}, u32[]{:S(2)}, u32[]{:S(2)}) collective-permute-start(bf16[512,256]{1,0:T(8,128)(2,1)S(1)} %add_back.7.rest_0_), channel_id=1, source_target_pairs={{16,0},{24,8},{32,16},{40,24},{48,32},{56,40},{64,48},{72,56},{80,... | collective-permute-start | bytes 786440 | tf_op jit(solution)/shard_map/ppermute | solution.py:425
  109.6 1.6 %collective-permute-done.25.y = f32[2,128]{1,0:T(2,128)S(1)} collective-permute-done((f32[2,128]{1,0:T(2,128)S(1)}, f32[2,128]{1,0:T(2,128)S(1)}, u32[]{:S(2)}, u32[]{:S(2)}) %collective-permute-start.25) | collective-permute-done | bytes 1056 | tf_op jit(solution)/shard_map/ppermute | solution.py:430
  111.2 1.6 %collective-permute-start.26 = (f32[2,128]{1,0:T(2,128)S(1)}, f32[2,128]{1,0:T(2,128)S(1)}, u32[]{:S(2)}, u32[]{:S(2)}) collective-permute-start(f32[2,128]{1,0:T(2,128)S(1)} %plus.10.x), channel_id=1, source_target_pairs={{0,1},{1,0},{2,3},{3,2},{4,5},{5,4},{6,7},{7,6},{8,9},{9,8},{10,11... | collective-permute-start | bytes 3080 | tf_op jit(solution)/shard_map/ppermute | solution.py:430
  113.1 1.6 %collective-permute-done.26.y = f32[2,128]{1,0:T(2,128)S(1)} collective-permute-done((f32[2,128]{1,0:T(2,128)S(1)}, f32[2,128]{1,0:T(2,128)S(1)}, u32[]{:S(2)}, u32[]{:S(2)}) %collective-permute-start.26) | collective-permute-done | bytes 1056 | tf_op jit(solution)/shard_map/ppermute | solution.py:430
  114.7 3.2 %collective-permute-start.27 = (f32[2,128]{1,0:T(2,128)S(1)}, f32[2,128]{1,0:T(2,128)S(1)}, u32[]{:S(2)}, u32[]{:S(2)}) collective-permute-start(f32[2,128]{1,0:T(2,128)S(1)} %plus.11.x), channel_id=1, source_target_pairs={{0,2},{1,3},{2,0},{3,1},{4,6},{5,7},{6,4},{7,5},{8,10},{9,11},{10,... | collective-permute-start | bytes 3080 | tf_op jit(solution)/shard_map/ppermute | solution.py:430
  120.1 4.2 %collective-permute-done.28.y = f32[2,128]{1,0:T(2,128)S(1)} collective-permute-done((f32[2,128]{1,0:T(2,128)S(1)}, f32[2,128]{1,0:T(2,128)S(1)}, u32[]{:S(2)}, u32[]{:S(2)}) %collective-permute-start.28) | collective-permute-done | bytes 1056 | tf_op jit(solution)/shard_map/ppermute | solution.py:430
  124.7 4.8 %collective-permute-done.29.y = f32[2,128]{1,0:T(2,128)S(1)} collective-permute-done((f32[2,128]{1,0:T(2,128)S(1)}, f32[2,128]{1,0:T(2,128)S(1)}, u32[]{:S(2)}, u32[]{:S(2)}) %collective-permute-start.29) | collective-permute-done | bytes 1056 | tf_op jit(solution)/shard_map/ppermute | solution.py:430
  130.9 6.2 %collective-permute-done.30.y = f32[2,128]{1,0:T(2,128)S(1)} collective-permute-done((f32[2,128]{1,0:T(2,128)S(1)}, f32[2,128]{1,0:T(2,128)S(1)}, u32[]{:S(2)}, u32[]{:S(2)}) %collective-permute-start.30) | collective-permute-done | bytes 1056 | tf_op jit(solution)/shard_map/ppermute | solution.py:430
  (83 shorter events, 16.2 us)
Async XLA Ops:
  4.3 3.6 %copy-start.3 = (bf16[1,256,1024]{2,1,0:T(8,128)(2,1)S(1)}, bf16[1,256,1024]{2,1,0:T(8,128)(2,1)}, u32[]{:S(2)}) copy-start(bf16[1,256,1024]{2,1,0:T(8,128)(2,1)} %param.10) | copy-start | bytes 1572868
  4.3 32.5 %collective-permute-start = (bf16[256,2048]{1,0:T(8,128)(2,1)S(1)}, bf16[256,2048]{1,0:T(8,128)(2,1)S(1)}, u32[]{:S(2)}, u32[]{:S(2)}) collective-permute-start(bf16[256,2048]{1,0:T(8,128)(2,1)S(1)} %split_q.1), channel_id=1, source_target_pairs={{0,8},{8,0},{16,24},{24,16},{32,40},{40,32},{48,56},{56,48},{64,72... | collective-permute-start | bytes 3145736 | tf_op jit(solution)/shard_map/ppermute | solution.py:430
  4.4 3.4 %collective-permute-start.1 = (bf16[256,1024]{1,0:T(8,128)(2,1)S(1)}, bf16[256,1024]{1,0:T(8,128)(2,1)S(1)}, u32[]{:S(2)}, u32[]{:S(2)}) collective-permute-start(bf16[256,1024]{1,0:T(8,128)(2,1)S(1)} %split_kv.1.after), channel_id=1, source_target_pairs={{0,8},{8,0},{16,24},{24,16},{32,40},{40,32},{48,56},{56,48},{64,72... | collective-permute-start | bytes 1572872 | tf_op jit(solution)/shard_map/ppermute | solution.py:430
  7.9 15.7 %collective-permute-start.2 = (bf16[512,256]{1,0:T(8,128)(2,1)S(1)}, bf16[512,256]{1,0:T(8,128)(2,1)S(1)}, u32[]{:S(2)}, u32[]{:S(2)}) collective-permute-start(bf16[512,256]{1,0:T(8,128)(2,1)S(1)} %join_kv.4.kv0.kv), channel_id=1, source_target_pairs={{0,16},{8,24},{16,32},{24,40},{32,48},{40,56},{48,64},{56,72},{64,... | collective-permute-start | bytes 786440 | tf_op jit(solution)/shard_map/ppermute | solution.py:425
  11.8 16.9 %collective-permute-start.4 = (bf16[512,256]{1,0:T(8,128)(2,1)S(1)}, bf16[512,256]{1,0:T(8,128)(2,1)S(1)}, u32[]{:S(2)}, u32[]{:S(2)}) collective-permute-start(bf16[512,256]{1,0:T(8,128)(2,1)S(1)} %join_kv.5.kv0.kv), channel_id=1, source_target_pairs={{0,16},{8,24},{16,32},{24,40},{32,48},{40,56},{48,64},{56,72},{64,... | collective-permute-start | bytes 786440 | tf_op jit(solution)/shard_map/ppermute | solution.py:425
  23.6 14.7 %collective-permute-start.3 = (bf16[512,256]{1,0:T(8,128)(2,1)S(1)}, bf16[512,256]{1,0:T(8,128)(2,1)S(1)}, u32[]{:S(2)}, u32[]{:S(2)}) collective-permute-start(bf16[512,256]{1,0:T(8,128)(2,1)S(1)} %collective-permute-done.2.kv1.rest_0_), channel_id=1, source_target_pairs={{0,16},{8,24},{16,32},{24,40},{32,48},{40,56},{48,64},{56,72},{64,... | collective-permute-start | bytes 786440 | tf_op jit(solution)/shard_map/ppermute | solution.py:425
  25.6 22.4 %collective-permute-start.6 = (bf16[512,256]{1,0:T(8,128)(2,1)S(1)}, bf16[512,256]{1,0:T(8,128)(2,1)S(1)}, u32[]{:S(2)}, u32[]{:S(2)}) collective-permute-start(bf16[512,256]{1,0:T(8,128)(2,1)S(1)} %join_kv.6.kv0.kv), channel_id=1, source_target_pairs={{0,16},{8,24},{16,32},{24,40},{32,48},{40,56},{48,64},{56,72},{64,... | collective-permute-start | bytes 786440 | tf_op jit(solution)/shard_map/ppermute | solution.py:425
  28.8 35.3 %collective-permute-start.8 = (bf16[512,256]{1,0:T(8,128)(2,1)S(1)}, bf16[512,256]{1,0:T(8,128)(2,1)S(1)}, u32[]{:S(2)}, u32[]{:S(2)}) collective-permute-start(bf16[512,256]{1,0:T(8,128)(2,1)S(1)} %join_kv.7.kv0.kv), channel_id=1, source_target_pairs={{0,16},{8,24},{16,32},{24,40},{32,48},{40,56},{48,64},{56,72},{64,... | collective-permute-start | bytes 786440 | tf_op jit(solution)/shard_map/ppermute | solution.py:425
  31.2 22.1 %collective-permute-start.5 = (bf16[512,256]{1,0:T(8,128)(2,1)S(1)}, bf16[512,256]{1,0:T(8,128)(2,1)S(1)}, u32[]{:S(2)}, u32[]{:S(2)}) collective-permute-start(bf16[512,256]{1,0:T(8,128)(2,1)S(1)} %collective-permute-done.4.rest_0_.kv1), channel_id=1, source_target_pairs={{0,16},{8,24},{16,32},{24,40},{32,48},{40,56},{48,64},{56,72},{64,... | collective-permute-start | bytes 786440 | tf_op jit(solution)/shard_map/ppermute | solution.py:425
  45.4 20.6 %collective-permute-start.9 = (bf16[512,256]{1,0:T(8,128)(2,1)S(1)}, bf16[512,256]{1,0:T(8,128)(2,1)S(1)}, u32[]{:S(2)}, u32[]{:S(2)}) collective-permute-start(bf16[512,256]{1,0:T(8,128)(2,1)S(1)} %get-tuple-element.44), channel_id=1, source_target_pairs={{16,0},{24,8},{32,16},{40,24},{48,32},{56,40},{64,48},{72,56},{80,... | collective-permute-start | bytes 786440 | tf_op jit(solution)/shard_map/ppermute | solution.py:425
  48.0 25.9 %collective-permute-start.7 = (bf16[512,256]{1,0:T(8,128)(2,1)S(1)}, bf16[512,256]{1,0:T(8,128)(2,1)S(1)}, u32[]{:S(2)}, u32[]{:S(2)}) collective-permute-start(bf16[512,256]{1,0:T(8,128)(2,1)S(1)} %collective-permute-done.6.rest_0_.kv1), channel_id=1, source_target_pairs={{0,16},{8,24},{16,32},{24,40},{32,48},{40,56},{48,64},{56,72},{64,... | collective-permute-start | bytes 786440 | tf_op jit(solution)/shard_map/ppermute | solution.py:425
  59.7 22.5 %collective-permute-start.11 = (bf16[512,256]{1,0:T(8,128)(2,1)S(1)}, bf16[512,256]{1,0:T(8,128)(2,1)S(1)}, u32[]{:S(2)}, u32[]{:S(2)}) collective-permute-start(bf16[512,256]{1,0:T(8,128)(2,1)S(1)} %get-tuple-element.48), channel_id=1, source_target_pairs={{16,0},{24,8},{32,16},{40,24},{48,32},{56,40},{64,48},{72,56},{80,... | collective-permute-start | bytes 786440 | tf_op jit(solution)/shard_map/ppermute | solution.py:425
  64.1 18.2 %collective-permute-start.10 = (bf16[512,256]{1,0:T(8,128)(2,1)S(1)}, bf16[512,256]{1,0:T(8,128)(2,1)S(1)}, u32[]{:S(2)}, u32[]{:S(2)}) collective-permute-start(bf16[512,256]{1,0:T(8,128)(2,1)S(1)} %collective-permute-done.8.rest_0_.kv1), channel_id=1, source_target_pairs={{0,16},{8,24},{16,32},{24,40},{32,48},{40,56},{48,64},{56,72},{64,... | collective-permute-start | bytes 786440 | tf_op jit(solution)/shard_map/ppermute | solution.py:425
  66.1 16.2 %collective-permute-start.12 = (bf16[512,256]{1,0:T(8,128)(2,1)S(1)}, bf16[512,256]{1,0:T(8,128)(2,1)S(1)}, u32[]{:S(2)}, u32[]{:S(2)}) collective-permute-start(bf16[512,256]{1,0:T(8,128)(2,1)S(1)} %add_back.4.rest_1_), channel_id=1, source_target_pairs={{16,0},{24,8},{32,16},{40,24},{48,32},{56,40},{64,48},{72,56},{80,... | collective-permute-start | bytes 786440 | tf_op jit(solution)/shard_map/ppermute | solution.py:425
  80.3 13.8 %collective-permute-start.15 = (bf16[512,256]{1,0:T(8,128)(2,1)S(1)}, bf16[512,256]{1,0:T(8,128)(2,1)S(1)}, u32[]{:S(2)}, u32[]{:S(2)}) collective-permute-start(bf16[512,256]{1,0:T(8,128)(2,1)S(1)} %get-tuple-element.56), channel_id=1, source_target_pairs={{16,0},{24,8},{32,16},{40,24},{48,32},{56,40},{64,48},{72,56},{80,... | collective-permute-start | bytes 786440 | tf_op jit(solution)/shard_map/ppermute | solution.py:425
  88.7 18.9 %collective-permute-start.17 = (bf16[512,256]{1,0:T(8,128)(2,1)S(1)}, bf16[512,256]{1,0:T(8,128)(2,1)S(1)}, u32[]{:S(2)}, u32[]{:S(2)}) collective-permute-start(bf16[512,256]{1,0:T(8,128)(2,1)S(1)} %get-tuple-element.60), channel_id=1, source_target_pairs={{16,0},{24,8},{32,16},{40,24},{48,32},{56,40},{64,48},{72,56},{80,... | collective-permute-start | bytes 786440 | tf_op jit(solution)/shard_map/ppermute | solution.py:425
  91.9 17.7 %collective-permute-start.14 = (bf16[512,256]{1,0:T(8,128)(2,1)S(1)}, bf16[512,256]{1,0:T(8,128)(2,1)S(1)}, u32[]{:S(2)}, u32[]{:S(2)}) collective-permute-start(bf16[512,256]{1,0:T(8,128)(2,1)S(1)} %add_back.5.rest_0_), channel_id=1, source_target_pairs={{16,0},{24,8},{32,16},{40,24},{48,32},{56,40},{64,48},{72,56},{80,... | collective-permute-start | bytes 786440 | tf_op jit(solution)/shard_map/ppermute | solution.py:425
  94.2 18.9 %collective-permute-start.16 = (bf16[512,256]{1,0:T(8,128)(2,1)S(1)}, bf16[512,256]{1,0:T(8,128)(2,1)S(1)}, u32[]{:S(2)}, u32[]{:S(2)}) collective-permute-start(bf16[512,256]{1,0:T(8,128)(2,1)S(1)} %add_back.6.rest_0_), channel_id=1, source_target_pairs={{16,0},{24,8},{32,16},{40,24},{48,32},{56,40},{64,48},{72,56},{80,... | collective-permute-start | bytes 786440 | tf_op jit(solution)/shard_map/ppermute | solution.py:425
  96.2 33.3 %collective-permute-start.13 = (bf16[256,1024]{1,0:T(8,128)(2,1)S(1)}, bf16[256,1024]{1,0:T(8,128)(2,1)S(1)}, u32[]{:S(2)}, u32[]{:S(2)}) collective-permute-start(bf16[256,1024]{1,0:T(8,128)(2,1)S(1)} %split_dq.1), channel_id=1, source_target_pairs={{0,8},{8,0},{16,24},{24,16},{32,40},{40,32},{48,56},{56,48},{64,72... | collective-permute-start | bytes 1572872 | tf_op jit(solution)/shard_map/ppermute | solution.py:430
  96.3 1.9 %collective-permute-start.18 = (f32[2,128]{1,0:T(2,128)S(1)}, f32[2,128]{1,0:T(2,128)S(1)}, u32[]{:S(2)}, u32[]{:S(2)}) collective-permute-start(f32[2,128]{1,0:T(2,128)S(1)} %fold.1.x), channel_id=1, source_target_pairs={{0,8},{8,0},{16,24},{24,16},{32,40},{40,32},{48,56},{56,48},{64,72... | collective-permute-start | bytes 3080 | tf_op jit(solution)/shard_map/ppermute | solution.py:430
  98.2 9.4 %collective-permute-start.19 = (f32[2,128]{1,0:T(2,128)S(1)}, f32[2,128]{1,0:T(2,128)S(1)}, u32[]{:S(2)}, u32[]{:S(2)}) collective-permute-start(f32[2,128]{1,0:T(2,128)S(1)} %plus.8.x), channel_id=1, source_target_pairs={{0,16},{8,24},{16,0},{24,8},{32,48},{40,56},{48,32},{56,40},{64,80... | collective-permute-start | bytes 3080 | tf_op jit(solution)/shard_map/ppermute | solution.py:430
  107.6 3.6 %collective-permute-start.25 = (f32[2,128]{1,0:T(2,128)S(1)}, f32[2,128]{1,0:T(2,128)S(1)}, u32[]{:S(2)}, u32[]{:S(2)}) collective-permute-start(f32[2,128]{1,0:T(2,128)S(1)} %plus.9.rest_0_.x), channel_id=1, source_target_pairs={{0,4},{1,5},{2,6},{3,7},{4,0},{5,1},{6,2},{7,3},{8,12},{9,13},{10,... | collective-permute-start | bytes 3080 | tf_op jit(solution)/shard_map/ppermute | solution.py:430
  107.7 16.6 %collective-permute-start.20 = (bf16[512,256]{1,0:T(8,128)(2,1)S(1)}, bf16[512,256]{1,0:T(8,128)(2,1)S(1)}, u32[]{:S(2)}, u32[]{:S(2)}) collective-permute-start(bf16[512,256]{1,0:T(8,128)(2,1)S(1)} %add_back.7.rest_0_), channel_id=1, source_target_pairs={{16,0},{24,8},{32,16},{40,24},{48,32},{56,40},{64,48},{72,56},{80,... | collective-permute-start | bytes 786440 | tf_op jit(solution)/shard_map/ppermute | solution.py:425
  111.2 3.6 %collective-permute-start.26 = (f32[2,128]{1,0:T(2,128)S(1)}, f32[2,128]{1,0:T(2,128)S(1)}, u32[]{:S(2)}, u32[]{:S(2)}) collective-permute-start(f32[2,128]{1,0:T(2,128)S(1)} %plus.10.x), channel_id=1, source_target_pairs={{0,1},{1,0},{2,3},{3,2},{4,5},{5,4},{6,7},{7,6},{8,9},{9,8},{10,11... | collective-permute-start | bytes 3080 | tf_op jit(solution)/shard_map/ppermute | solution.py:430
  113.0 24.6 %collective-permute-start.21 = (bf16[256,256]{1,0:T(8,128)(2,1)S(1)}, bf16[256,256]{1,0:T(8,128)(2,1)S(1)}, u32[]{:S(2)}, u32[]{:S(2)}) collective-permute-start(bf16[256,256]{1,0:T(8,128)(2,1)S(1)} %get-tuple-element.63), channel_id=1, source_target_pairs={{0,8},{8,0},{16,24},{24,16},{32,40},{40,32},{48,56},{56,48},{64,72... | collective-permute-start | bytes 393224 | tf_op jit(solution)/shard_map/ppermute | solution.py:430
  114.7 5.1 %collective-permute-start.27 = (f32[2,128]{1,0:T(2,128)S(1)}, f32[2,128]{1,0:T(2,128)S(1)}, u32[]{:S(2)}, u32[]{:S(2)}) collective-permute-start(f32[2,128]{1,0:T(2,128)S(1)} %plus.11.x), channel_id=1, source_target_pairs={{0,2},{1,3},{2,0},{3,1},{4,6},{5,7},{6,4},{7,5},{8,10},{9,11},{10,... | collective-permute-start | bytes 3080 | tf_op jit(solution)/shard_map/ppermute | solution.py:430
  118.2 19.4 %collective-permute-start.22 = (bf16[256,256]{1,0:T(8,128)(2,1)S(1)}, bf16[256,256]{1,0:T(8,128)(2,1)S(1)}, u32[]{:S(2)}, u32[]{:S(2)}) collective-permute-start(bf16[256,256]{1,0:T(8,128)(2,1)S(1)} %get-tuple-element.64), channel_id=1, source_target_pairs={{0,8},{8,0},{16,24},{24,16},{32,40},{40,32},{48,56},{56,48},{64,72... | collective-permute-start | bytes 393224 | tf_op jit(solution)/shard_map/ppermute | solution.py:430
  119.8 4.5 %collective-permute-start.28 = (f32[2,128]{1,0:T(2,128)S(1)}, f32[2,128]{1,0:T(2,128)S(1)}, u32[]{:S(2)}, u32[]{:S(2)}) collective-permute-start(f32[2,128]{1,0:T(2,128)S(1)} %plus.12.x), channel_id=1, source_target_pairs={{0,32},{8,40},{16,48},{24,56},{32,0},{40,8},{48,16},{56,24},{64,96... | collective-permute-start | bytes 3080 | tf_op jit(solution)/shard_map/ppermute | solution.py:430
  124.3 13.3 %collective-permute-start.23 = (bf16[256,256]{1,0:T(8,128)(2,1)S(1)}, bf16[256,256]{1,0:T(8,128)(2,1)S(1)}, u32[]{:S(2)}, u32[]{:S(2)}) collective-permute-start(bf16[256,256]{1,0:T(8,128)(2,1)S(1)} %get-tuple-element.65), channel_id=1, source_target_pairs={{0,8},{8,0},{16,24},{24,16},{32,40},{40,32},{48,56},{56,48},{64,72... | collective-permute-start | bytes 393224 | tf_op jit(solution)/shard_map/ppermute | solution.py:430
  124.3 5.2 %collective-permute-start.29 = (f32[2,128]{1,0:T(2,128)S(1)}, f32[2,128]{1,0:T(2,128)S(1)}, u32[]{:S(2)}, u32[]{:S(2)}) collective-permute-start(f32[2,128]{1,0:T(2,128)S(1)} %plus.13.x), channel_id=1, source_target_pairs={{0,128},{8,136},{16,144},{24,152},{32,160},{40,168},{48,176},{56,1... | collective-permute-start | bytes 3080 | tf_op jit(solution)/shard_map/ppermute | solution.py:430
  129.5 8.1 %collective-permute-start.24 = (bf16[256,256]{1,0:T(8,128)(2,1)S(1)}, bf16[256,256]{1,0:T(8,128)(2,1)S(1)}, u32[]{:S(2)}, u32[]{:S(2)}) collective-permute-start(bf16[256,256]{1,0:T(8,128)(2,1)S(1)} %get-tuple-element.66), channel_id=1, source_target_pairs={{0,8},{8,0},{16,24},{24,16},{32,40},{40,32},{48,56},{56,48},{64,72... | collective-permute-start | bytes 393224 | tf_op jit(solution)/shard_map/ppermute | solution.py:430
  129.5 7.6 %collective-permute-start.30 = (f32[2,128]{1,0:T(2,128)S(1)}, f32[2,128]{1,0:T(2,128)S(1)}, u32[]{:S(2)}, u32[]{:S(2)}) collective-permute-start(f32[2,128]{1,0:T(2,128)S(1)} %plus.14.x), channel_id=1, source_target_pairs={{0,64},{8,72},{16,80},{24,88},{32,96},{40,104},{48,112},{56,120},{... | collective-permute-start | bytes 3080 | tf_op jit(solution)/shard_map/ppermute | solution.py:430
  (9 other events, 11.1 us)

commit v3 on v2

--- a/solution.py
+++ b/solution.py
@@ -14,7 +14,7 @@
 T = 256
 TC = 2 * T
 NKV = 4
-CHUNKS = (1, 1, 1, 1)
+CHUNKS = (2, 2)
 LOG2E = 1.4426950408889634
 SCALE = 168.0 ** (-0.5)
 EPS = 1e-06
@@ -43,48 +43,51 @@
     return pl.multiple_of(x, n)
 
 
-def split_kv_kernel(idx, k, v, send):
-    other = 1 - idx[0] % 2
-    for h in range(NKV):
-        cols = pl.ds(al(other * (NKV * D) + h * D, D), D)
-        send[:, 2 * h * D : (2 * h + 1) * D] = k[:, cols]
-        send[:, (2 * h + 1) * D : (2 * h + 2) * D] = v[:, cols]
+def split_kv_kernel(idx, k, v, keep, send, sems):
+    a = idx[0] % 2
+    copies = []
+    for side, out in ((1 - a, send), (a, keep)):
+        for h in range(NKV):
+            cols = pl.ds(al(side * (NKV * D) + h * D, D), D)
+            for x, ref in enumerate((k, v)):
+                dst = out.at[:, (2 * h + x) * D : (2 * h + x + 1) * D]
+                copies.append(pltpu.make_async_copy(ref.at[:, cols], dst, sems.at[len(copies)]))
+    for copy in copies:
+        copy.start()
+    for copy in copies:
+        copy.wait()
 
 
 def split_kv(idx, k, v):
     return pl.pallas_call(
         split_kv_kernel,
-        out_shape=jax.ShapeDtypeStruct((T, 2 * NKV * D), bf16),
-        in_specs=[SM, VM, VM],
-        out_specs=VM,
+        out_shape=[jax.ShapeDtypeStruct((T, 2 * NKV * D), bf16)] * 2,
+        in_specs=[SM, ANY, ANY],
+        out_specs=[VM, VM],
+        scratch_shapes=[pltpu.SemaphoreType.DMA((4 * NKV,))],
         compiler_params=SMALL,
         cost_estimate=cost(1),
         name="split_kv",
     )(idx, k, v)
 
 
-def join_kv_kernel(h0, n, idx, k, v, recv, *rest):
+def join_kv_kernel(cols, idx, keep, recv, *rest):
     out = rest[-1]
     a = idx[0] % 2
-    mine = pl.ds(al(a * T, T), T)
-    theirs = pl.ds(al((1 - a) * T, T), T)
-    for i in range(n):
-        cols = pl.ds(al(a * (NKV * D) + (h0 + i) * D, D), D)
-        out[mine, 2 * i * D : (2 * i + 1) * D] = k[:, cols]
-        out[mine, (2 * i + 1) * D : (2 * i + 2) * D] = v[:, cols]
-    out[theirs, :] = recv[:, 2 * h0 * D : 2 * (h0 + n) * D]
-
-
-def join_kv(h0, n, idx, k, v, recv, after):
-    return pl.pallas_call(
-        functools.partial(join_kv_kernel, h0, n),
+    out[pl.ds(al(a * T, T), T), :] = keep[:, cols]
+    out[pl.ds(al((1 - a) * T, T), T), :] = recv[:, cols]
+
+
+def join_kv(h0, n, idx, keep, recv, after):
+    return pl.pallas_call(
+        functools.partial(join_kv_kernel, slice(2 * h0 * D, 2 * (h0 + n) * D)),
         out_shape=jax.ShapeDtypeStruct((TC, 2 * n * D), bf16),
-        in_specs=[SM, VM, VM, VM] + [ANY] * len(after),
+        in_specs=[SM, VM, VM] + [ANY] * len(after),
         out_specs=VM,
         compiler_params=SMALL,
         cost_estimate=cost(0.2),
         name="join_kv",
-    )(idx, k, v, recv, *after)
+    )(idx, keep, recv, *after)
 
 
 def split_q_kernel(idx, q, do, after, send):
@@ -142,31 +145,29 @@
 
 
 def attn_kernel(
-    n_after, idx, starts, flags, qg, kg, gains_in, q, do, kv0, kv1, kv2, *rest
+    h0, n, n_after, idx, starts, flags, qg, kg, gains_in, q, do, kv0, kv1, kv2, *rest
 ):
     (
     dq, d2, d1, d0, gains,
     bias, s_scr, dp_scr, pb_scr, ds_scr, kn_scr, qn_scr, do_scr, dk_acc, dv_acc,
     ) = rest[n_after:]
-    step = pl.program_id(0)
     first = (idx[0] // 2) * TC
 
     jl = lax.broadcasted_iota(jnp.int32, (T, T), 0)
     il = lax.broadcasted_iota(jnp.int32, (T, T), 1)
     late = jl > il
 
-    @pl.when(step == 0)
-    def _():
+    if True:
         gains[...] = gains_in[...]
         for qb in range(2):
             base = first + qb * T
             qpos = base + lax.broadcasted_iota(jnp.int32, (1, T), 1)
             lo = jnp.maximum(qpos - (WINDOW - 1), 0)
-            for n in range(starts.shape[1]):
-                b = starts[0, n]
+            for m in range(starts.shape[1]):
+                b = starts[0, m]
                 lo = jnp.maximum(lo, jnp.where(b <= qpos, b, 0))
-            for n in range(flags.shape[1]):
-                b = flags[0, n] * (n * T)
+            for m in range(flags.shape[1]):
+                b = flags[0, m] * (m * T)
                 lo = jnp.maximum(lo, jnp.where(b <= qpos, b, 0))
             for t in range(4):
                 if t == 0:
@@ -175,110 +176,141 @@
                     kpos = base - WINDOW + t * T + jl
                 bias[qb, t] = jnp.where(kpos >= lo, 0.0, -jnp.inf).astype(f32)
 
-    dkg = jnp.zeros((8, D), f32)
-    for b, ref in enumerate((kv2, kv1, kv0)):
-        xh, _ = unit_of(ref[:, :D].astype(f32))
-        kn_scr[b * TC : (b + 1) * TC, :] = (xh * kg[...]).astype(bf16)
-    for qb in range(2):
-        for g in range(2):
-            x = q[qb * T : (qb + 1) * T, g * D : (g + 1) * D].astype(f32)
-            xh, _ = unit_of(x)
-            qn_scr[qb, g * T : (g + 1) * T, :] = (xh * qg[...]).astype(bf16)
-            do_scr[qb, g * T : (g + 1) * T, :] = do[qb * T : (qb + 1) * T, g * D : (g + 1) * D]
-
-    def keys(kb):
-        return kn_scr[kb * T : (kb + 1) * T, :]
-
-    def vals(kb):
-        ref = (kv2, kv1, kv0)[kb // 2]
-        return ref[(kb % 2) * T : (kb % 2 + 1) * T, D:]
-
-    dqg = jnp.zeros((8, D), f32)
-    for qb in range(2):
-        for g in range(2):
-            lanes = slice(g * T, (g + 1) * T)
-            qn = qn_scr[qb, lanes, :]
-            dog = do_scr[qb, lanes, :]
-            m = None
-            for t in range(4):
-                s = dot(keys(qb + t), qn, NT)
-                if t == 0:
-                    s = jnp.where(late, s, dot(keys(qb + 4), qn, NT))
-                s = s * (SCALE * LOG2E) + bias[qb, t]
-                s_scr[t] = s
-                mt = rows8(s, jnp.max)
-                m = mt if m is None else jnp.maximum(m, mt)
-            m = jnp.max(m, axis=0, keepdims=True)
-            el = None
-            for t in range(4):
-                e = jnp.exp2(s_scr[t] - m)
-                s_scr[t] = e
-                lt = rows8(e, jnp.sum)
-                el = lt if el is None else el + lt
-            rl = 1.0 / jnp.sum(el, axis=0, keepdims=True)
-            delta = None
-            for t in range(4):
-                dp = dot(vals(qb + t), dog, NT)
-                if t == 0:
-                    dp = jnp.where(late, dp, dot(vals(qb + 4), dog, NT))
-                dp_scr[t] = dp
-                p = s_scr[t] * rl
-                s_scr[t] = p
-                pb = p.astype(bf16)
-                dt = rows8(pb.astype(f32) * dp, jnp.sum)
-                delta = dt if delta is None else delta + dt
-                if t == 0:
-                    pb_scr[0, :, lanes] = jnp.where(late, p, 0.0).astype(bf16)
-                    pb_scr[4, :, lanes] = jnp.where(late, 0.0, p).astype(bf16)
-                else:
-                    pb_scr[t, :, lanes] = pb
-            delta = jnp.sum(delta, axis=0, keepdims=True)
-            for t in range(4):
-                ds = s_scr[t] * (dp_scr[t] - delta) * SCALE
-                if t == 0:
-                    ds_scr[0, :, lanes] = jnp.where(late, ds, 0.0).astype(bf16)
-                    ds_scr[4, :, lanes] = jnp.where(late, 0.0, ds).astype(bf16)
-                else:
-                    ds_scr[t, :, lanes] = ds.astype(bf16)
-            dqn = None
-            for t in range(5):
-                part = dot(ds_scr[t, :, lanes], keys(qb + t), TN)
-                dqn = part if dqn is None else dqn + part
-            xh, r = unit_of(q[qb * T : (qb + 1) * T, g * D : (g + 1) * D].astype(f32))
-            dqg = dqg + rows8(dqn * xh, jnp.sum)
+    for h in range(n):
+        kc = slice(2 * h * D, (2 * h + 1) * D)
+        vc = slice((2 * h + 1) * D, (2 * h + 2) * D)
+        R = 128
+        for b, ref in enumerate((kv2, kv1, kv0)):
+            xh, _ = unit_of(ref[:, kc].astype(f32))
+            kn_scr[b * TC : (b + 1) * TC, :] = (xh * kg[...]).astype(bf16)
+        for qb in range(2):
+            for g in range(2):
+                rows = slice((2 * qb + g) * T, (2 * qb + g + 1) * T)
+                xh, _ = unit_of(q[qb * T : (qb + 1) * T, (2 * (h0 + h) + g) * D : (2 * (h0 + h) + g + 1) * D].astype(f32))
+                qn_scr[rows, :] = (xh * qg[...]).astype(bf16)
+                do_scr[rows, :] = do[qb * T : (qb + 1) * T, (2 * (h0 + h) + g) * D : (2 * (h0 + h) + g + 1) * D]
+
+        kvs = (kv2, kv1, kv0)
+
+        def vals(row):
+            return kvs[row // TC][row % TC : row % TC + R, vc]
+
+        def late_of(r):
+            return jl[:R] + r * R > il[:R]
+
+        tasks = [(t, r) for t in range(4) for r in range(T // R)]
+        st = [dict(m=None, l=None, delta=None) for _ in range(4)]
+
+        def span(i):
+            return slice(i * T, (i + 1) * T)
+
+        def join(x, y, op):
+            return y if x is None else op(x, y)
+
+        def scores(i, t, r):
+            qb, row = i // 2, (i // 2 + t) * T + r * R
+            s = dot(kn_scr[row : row + R, :], qn_scr[span(i), :], NT)
+            if t == 0:
+                far = dot(kn_scr[row + 4 * T : row + 4 * T + R, :], qn_scr[span(i), :], NT)
+                s = jnp.where(late_of(r), s, far)
+            s = s * (SCALE * LOG2E) + bias[qb, t, r * R : (r + 1) * R, :]
+            s_scr[i % 2, t * T + r * R : t * T + (r + 1) * R, :] = s
+            st[i]["m"] = join(st[i]["m"], rows8(s, jnp.max), jnp.maximum)
+
+        def grads(i, t, r):
+            row = (i // 2 + t) * T + r * R
+            dp = dot(vals(row), do_scr[span(i), :], NT)
+            if t == 0:
+                dp = jnp.where(late_of(r), dp, dot(vals(row + 4 * T), do_scr[span(i), :], NT))
+            dp_scr[i % 2, t * T + r * R : t * T + (r + 1) * R, :] = dp
+
+        def expo(i, t, r):
+            rows = slice(t * T + r * R, t * T + (r + 1) * R)
+            e = jnp.exp2(s_scr[i % 2, rows, :] - st[i]["m"])
+            s_scr[i % 2, rows, :] = e
+            st[i]["l"] = join(st[i]["l"], rows8(e, jnp.sum), jnp.add)
+
+        def store(ref, i, t, r, x):
+            row = (i // 2 + t) * T + r * R
+            if t == 0:
+                late = late_of(r)
+                ref[row : row + R, span(i)] = jnp.where(late, x, 0.0).astype(bf16)
+                ref[row + 4 * T : row + 4 * T + R, span(i)] = jnp.where(late, 0.0, x).astype(bf16)
+            else:
+                ref[row : row + R, span(i)] = x.astype(bf16)
+
+        def probs(i, t, r):
+            rows = slice(t * T + r * R, t * T + (r + 1) * R)
+            p = s_scr[i % 2, rows, :] * st[i]["rl"]
+            store(pb_scr, i, t, r, p)
+            d = rows8(p.astype(bf16).astype(f32) * dp_scr[i % 2, rows, :], jnp.sum)
+            st[i]["delta"] = join(st[i]["delta"], d, jnp.add)
+
+        def dscores(i, t, r):
+            rows = slice(t * T + r * R, t * T + (r + 1) * R)
+            ds = s_scr[i % 2, rows, :] * (dp_scr[i % 2, rows, :] - st[i]["delta"]) * st[i]["rs"]
+            store(ds_scr, i, t, r, ds)
+
+        dqg = []
+
+        def dquery(i):
+            qb, g = i // 2, i % 2
+            rows, cols = slice(qb * T, (qb + 1) * T), slice((2 * h + g) * D, (2 * h + g + 1) * D)
+            dqn = dot(ds_scr[qb * T : (qb + 5) * T, span(i)], kn_scr[qb * T : (qb + 5) * T, :], TN)
+            xh, r = unit_of(q[rows, slice((2 * (h0 + h) + g) * D, (2 * (h0 + h) + g + 1) * D)].astype(f32))
+            dqg.append(rows8(dqn * xh, jnp.sum))
             dxh = dqn * qg[...]
             dx = r * (dxh - xh * jnp.mean(dxh * xh, axis=-1, keepdims=True))
-            dq[qb * T : (qb + 1) * T, g * D : (g + 1) * D] = dx.astype(bf16)
-        for t in range(5):
-            kb = qb + t
-            rows = slice(kb * T, (kb + 1) * T)
-            dv = dot(pb_scr[t], do_scr[qb], NN)
-            dk = dot(ds_scr[t], qn_scr[qb], NN)
-            if qb == 0 or t == 4:
-                dv_acc[rows, :] = dv
-                dk_acc[rows, :] = dk
-            else:
-                dv_acc[rows, :] += dv
-                dk_acc[rows, :] += dk
-
-    for b, (ref, out) in enumerate(((kv2, d2), (kv1, d1), (kv0, d0))):
-        xh, _ = unit_of(ref[:, :D].astype(f32))
-        dk = dk_acc[b * TC : (b + 1) * TC, :]
-        dkg = dkg + rows8(dk * xh, jnp.sum)
-        out[:, :D] = dk.astype(out.dtype)
-        out[:, D:] = dv_acc[b * TC : (b + 1) * TC, :].astype(out.dtype)
-    gains[0] += dqg
-    gains[1] += dkg
+            dq[rows, cols] = dx.astype(bf16)
+
+        def do_all(fs):
+            for tr in tasks:
+                for f in fs:
+                    f(*tr)
+
+        def top(f, i):
+            return lambda t, r: f(i, t, r)
+
+        def dkeys(k0, k1, l0, l1):
+            rows, lanes = slice(k0 * T, k1 * T), slice(l0 * T, l1 * T)
+            dv_acc[rows, :] = dot(pb_scr[rows, lanes], do_scr[lanes, :], NN)
+            dk_acc[rows, :] = dot(ds_scr[rows, lanes], qn_scr[lanes, :], NN)
+
+        inter = False
+        do_all([top(scores, 0)])
+        for i in range(4):
+            st[i]["m"] = jnp.max(st[i]["m"], axis=0, keepdims=True)
+            do_all([top(expo, i), top(grads, i)])
+            st[i]["rl"] = 1.0 / jnp.sum(st[i]["l"], axis=0, keepdims=True)
+            st[i]["rs"] = st[i]["rl"] * SCALE
+            do_all([top(probs, i)] + ([top(scores, i + 1)] if inter and i < 3 else []))
+            st[i]["delta"] = jnp.sum(st[i]["delta"], axis=0, keepdims=True)
+            if inter and i > 0:
+                dquery(i - 1)
+            do_all([top(dscores, i)] + ([top(scores, i + 1)] if not inter and i < 3 else []))
+            if not inter:
+                dquery(i)
+        if inter:
+            dquery(3)
+        dkeys(0, 1, 0, 2)
+        for kb in range(1, 5):
+            dkeys(kb, kb + 1, 0, 4)
+        dkeys(5, 6, 2, 4)
+
+        dkg = jnp.zeros((8, D), f32)
+        for b, (ref, out) in enumerate(((kv2, d2), (kv1, d1), (kv0, d0))):
+            xh, _ = unit_of(ref[:, kc].astype(f32))
+            dk = dk_acc[b * TC : (b + 1) * TC, :]
+            dkg = dkg + rows8(dk * xh, jnp.sum)
+            out[:, kc] = dk.astype(out.dtype)
+            out[:, vc] = dv_acc[b * TC : (b + 1) * TC, :].astype(out.dtype)
+        gains[0] += dqg[0] + dqg[1] + dqg[2] + dqg[3]
+        gains[1] += dkg
 
 
 def attn(h0, n, idx, starts, flags, qg, kg, gains, q, do, kv0, kv1, kv2, after):
-    col = pl.BlockSpec((TC, 2 * D), lambda i: (0, i))
-    qcol = pl.BlockSpec((TC, 2 * D), lambda i: (0, h0 + i))
-    full = pl.BlockSpec((1, D), lambda i: (0, 0))
-    gain = pl.BlockSpec((2, 8, D), lambda i: (0, 0, 0))
-    return pl.pallas_call(
-        functools.partial(attn_kernel, len(after)),
-        grid=(n,),
+    return pl.pallas_call(
+        functools.partial(attn_kernel, h0, n, len(after)),
         out_shape=[
             jax.ShapeDtypeStruct((TC, 2 * n * D), bf16),
             jax.ShapeDtypeStruct((TC, 2 * n * D), bf16),
@@ -286,17 +318,17 @@
             jax.ShapeDtypeStruct((TC, 2 * n * D), f32),
             jax.ShapeDtypeStruct((2, 8, D), f32),
         ],
-        in_specs=[SM, SM, SM, full, full, gain, qcol, qcol, col, col, col] + [ANY] * len(after),
-        out_specs=[col, col, col, col, gain],
+        in_specs=[SM] * 3 + [VM] * 8 + [ANY] * len(after),
+        out_specs=[VM] * 5,
         scratch_shapes=[
             pltpu.VMEM((2, 4, T, T), f32),
-            pltpu.VMEM((4, T, T), f32),
-            pltpu.VMEM((4, T, T), f32),
-            pltpu.VMEM((5, T, 2 * T), bf16),
-            pltpu.VMEM((5, T, 2 * T), bf16),
+            pltpu.VMEM((2, WINDOW, T), f32),
+            pltpu.VMEM((2, WINDOW, T), f32),
+            pltpu.VMEM((3 * TC, 4 * T), bf16),
+            pltpu.VMEM((3 * TC, 4 * T), bf16),
             pltpu.VMEM((3 * TC, D), bf16),
-            pltpu.VMEM((2, 2 * T, D), bf16),
-            pltpu.VMEM((2, 2 * T, D), bf16),
+            pltpu.VMEM((4 * T, D), bf16),
+            pltpu.VMEM((4 * T, D), bf16),
             pltpu.VMEM((3 * TC, D), f32),
             pltpu.VMEM((3 * TC, D), f32),
         ],
@@ -469,14 +501,14 @@
     count = len(CHUNKS)
     first = [sum(CHUNKS[:c]) for c in range(count)]
 
-    send = split_kv(idx, k, v)
+    keep, send = split_kv(idx, k, v)
     recv = swap(send, "ctx", 1)
     kv0, kv1, kv2 = [], [], []
     for c, n in enumerate(CHUNKS):
-        kv0.append(join_kv(first[c], n, idx, k, v, recv, kv1[c - 2 : c - 1] if c >= 2 else []))
+        kv0.append(join_kv(first[c], n, idx, keep, recv, kv1[c - 1 : c] if c >= 2 else []))
         kv1.append(along(kv0[c], 2))
     kv2 = [along(x, 2) for x in kv1]
-    qa, doa = join_q(idx, q, do, swap(split_q(idx, q, do, send), "ctx", 1))
+    qa, doa = join_q(idx, q, do, swap(split_q(idx, q, do, kv0[0]), "ctx", 1))
 
     last = count - 1
     dqs, d0s, sums, r2s, gains = [], [], [], [], jnp.zeros((2, 8, D), f32)
@@ -497,14 +529,14 @@
             r2s.append(along(sums[c], -2))
     gain = fold(gains, sums[last - 1])
     gain = plus(gain, swap(gain, "ctx", 1))
-    gain = plus(gain, swap(gain, "ctx", 2))
+    gain = plus(gain, swap(gain, "dp", 1))
+    gain = plus(gain, swap(gain, "dp", 2))
     sums.append(add_back(d1, r1, gain))
     r2s.append(along(sums[last], -2))
     gain = plus(gain, swap(gain, "dp", 4), sums[last], *r2s[last - 2 : last - 1])
-    gain = plus(gain, swap(gain, "dp", 1), r2s[last - 1])
-    gain = plus(gain, swap(gain, "dp", 2))
-    gain = plus(gain, swap(gain, "ctx", 4), r2s[last])
-    gain = plus(gain, swap(gain, "ctx", 16))
+    gain = plus(gain, swap(gain, "ctx", 16), r2s[last - 1])
+    gain = plus(gain, swap(gain, "ctx", 2), r2s[last])
+    gain = plus(gain, swap(gain, "ctx", 4))
     gain = plus(gain, swap(gain, "ctx", 8))
     keeps, recvs = [], []
     for c, n in enumerate(CHUNKS):

time: 139 us -> 128 us (0.921)
  starting transfers between devices: 59.2 us -> 36.2 us
  waiting for transfers between devices: 43.9 us -> 60 us
  Pallas kernels: 29.8 us -> 27.4 us
  local copies, waits for them, and re-layouts: 4.7 us -> 3.3 us
    ppermute x16 -> x8, starting transfers between devices: 50.7 us -> 28.6 us  [along(): lax.ppermute(x, 'ctx', [(i, i + distance) for i in range(n) if 0 <= i + d...]
    ppermute x16 -> x8, waiting for transfers between devices: 12.4 us -> 32.3 us  [along(): lax.ppermute(x, 'ctx', [(i, i + distance) for i in range(n) if 0 <= i + d...]
    ppermute x15 -> x13, waiting for transfers between devices: 31.6 us -> 27.7 us  [swap(): return lax.ppermute(x, axis, [(i, i ^ bit) for i in range(n)])]
    pallas_call x9 -> x5, Pallas kernels: 26 us -> 23.6 us  [the longest x2 23.1 us: attn(): pl.pallas_call(functools.partial(attn_kernel, h0, n, len(after)), out_sha...]
    unnamed x20 -> x16, local copies, waits for them, and re-layouts: 4.17 us -> 2.77 us
    ppermute x15 -> x13, starting transfers between devices: 8.56 us -> 7.57 us  [swap(): return lax.ppermute(x, axis, [(i, i ^ bit) for i in range(n)])]
  transfers between devices with their start and end apart: 31 -> 21, of which waited for: 13 -> 13; matrix products, arithmetic and copies ran while one was open for 0% -> 0% of each run, Pallas kernels for 20% -> 20%
where the time goes in v3:
time: 128 us
  waiting for transfers between devices  60 us (47%)
  starting transfers between devices  36.2 us (28%)
  Pallas kernels  27.4 us (21%)
  local copies, waits for them, and re-layouts  3.3 us (3%)
    ppermute x8, waiting for transfers between devices, along(): lax.ppermute(x, 'ctx', [(i, i + distance) for i in range(n) if 0 <= i + d...  32.3 us
    ppermute x8, starting transfers between devices, along(): lax.ppermute(x, 'ctx', [(i, i + distance) for i in range(n) if 0 <= i + d...  28.6 us
    ppermute x13, waiting for transfers between devices, swap(): return lax.ppermute(x, axis, [(i, i ^ bit) for i in range(n)])  27.7 us
    pallas_call x2, Pallas kernels, attn(): pl.pallas_call(functools.partial(attn_kernel, h0, n, len(after)), out_sha...  23.1 us
    ppermute x13, starting transfers between devices, swap(): return lax.ppermute(x, axis, [(i, i ^ bit) for i in range(n)])  7.57 us
    unnamed x16, local copies, waits for them, and re-layouts  2.77 us
  transfers between devices with their start and end apart: 21, of which 13 were waited for; matrix products, arithmetic and copies ran while one was open for 0% of the time, Pallas kernels for 20%

profile of v3, /device:TPU:6, one launch (start us, length us, event | category | flops | bytes accessed | tf_op | source)
XLA Modules:
  0.0 127.9 jit_solution(15940721189350283632)
XLA Ops:
  0.6 1.0 copy-done.2
  1.7 1.0 copy-done.3
  3.3 1.9 %collective-permute-done.recv = bf16[256,1024]{1,0:T(8,128)(2,1)S(1)} collective-permute-done((bf16[256,1024]{1,0:T(8,128)(2,1)S(1)}, bf16[256,1024]{1,0:T(8,128)(2,1)S(1)}, u32[]{:S(2)}, u32[]{:S(2)}) %collective-permute-start) | collective-permute-done | bytes 524320 | tf_op jit(solution)/shard_map/ppermute | solution.py:462
  5.6 3.8 %collective-permute-start.2 = (bf16[512,512]{1,0:T(8,128)(2,1)S(1)}, bf16[512,512]{1,0:T(8,128)(2,1)S(1)}, u32[]{:S(2)}, u32[]{:S(2)}) collective-permute-start(bf16[512,512]{1,0:T(8,128)(2,1)S(1)} %join_kv.2.after.kv0.kv), channel_id=1, source_target_pairs={{0,16},{8,24},{16,32},{24,40},{32,48},{40,56},{48,64},{56,72},{64,... | collective-permute-start | bytes 1572872 | tf_op jit(solution)/shard_map/ppermute | solution.py:457
  9.5 3.8 %collective-permute-start.4 = (bf16[512,512]{1,0:T(8,128)(2,1)S(1)}, bf16[512,512]{1,0:T(8,128)(2,1)S(1)}, u32[]{:S(2)}, u32[]{:S(2)}) collective-permute-start(bf16[512,512]{1,0:T(8,128)(2,1)S(1)} %join_kv.3.kv0.kv), channel_id=1, source_target_pairs={{0,16},{8,24},{16,32},{24,40},{32,48},{40,56},{48,64},{56,72},{64,... | collective-permute-start | bytes 1572872 | tf_op jit(solution)/shard_map/ppermute | solution.py:457
  13.3 13.6 %collective-permute-done.2.kv1 = bf16[512,512]{1,0:T(8,128)(2,1)S(1)} collective-permute-done((bf16[512,512]{1,0:T(8,128)(2,1)S(1)}, bf16[512,512]{1,0:T(8,128)(2,1)S(1)}, u32[]{:S(2)}, u32[]{:S(2)}) %collective-permute-start.2) | collective-permute-done | bytes 524320 | tf_op jit(solution)/shard_map/ppermute | solution.py:457
  26.9 1.9 %collective-permute-start.3 = (bf16[512,512]{1,0:T(8,128)(2,1)S(1)}, bf16[512,512]{1,0:T(8,128)(2,1)S(1)}, u32[]{:S(2)}, u32[]{:S(2)}) collective-permute-start(bf16[512,512]{1,0:T(8,128)(2,1)S(1)} %collective-permute-done.2.kv1), channel_id=1, source_target_pairs={{0,16},{8,24},{16,32},{24,40},{32,48},{40,56},{48,64},{56,72},{64,... | collective-permute-start | bytes 1572872 | tf_op jit(solution)/shard_map/ppermute | solution.py:457
  28.9 9.3 %collective-permute-done.4.rest_0_.kv1 = bf16[512,512]{1,0:T(8,128)(2,1)S(1)} collective-permute-done((bf16[512,512]{1,0:T(8,128)(2,1)S(1)}, bf16[512,512]{1,0:T(8,128)(2,1)S(1)}, u32[]{:S(2)}, u32[]{:S(2)}) %collective-permute-start.4) | collective-permute-done | bytes 524320 | tf_op jit(solution)/shard_map/ppermute | solution.py:457
  38.2 1.9 %collective-permute-start.5 = (bf16[512,512]{1,0:T(8,128)(2,1)S(1)}, bf16[512,512]{1,0:T(8,128)(2,1)S(1)}, u32[]{:S(2)}, u32[]{:S(2)}) collective-permute-start(bf16[512,512]{1,0:T(8,128)(2,1)S(1)} %collective-permute-done.4.rest_0_.kv1), channel_id=1, source_target_pairs={{0,16},{8,24},{16,32},{24,40},{32,48},{40,56},{48,64},{56,72},{64,... | collective-permute-start | bytes 1572872 | tf_op jit(solution)/shard_map/ppermute | solution.py:457
  40.3 9.1 %collective-permute-done.3.kv2 = bf16[512,512]{1,0:T(8,128)(2,1)S(1)} collective-permute-done((bf16[512,512]{1,0:T(8,128)(2,1)S(1)}, bf16[512,512]{1,0:T(8,128)(2,1)S(1)}, u32[]{:S(2)}, u32[]{:S(2)}) %collective-permute-start.3) | collective-permute-done | bytes 524320 | tf_op jit(solution)/shard_map/ppermute | solution.py:457
  49.4 0.6 copy-done.4
  50.1 11.5 %attn.2 = (bf16[512,512]{1,0:T(8,128)(2,1)S(1)}, bf16[512,512]{1,0:T(8,128)(2,1)S(1)}, f32[512,512]{1,0:T(8,128)S(1)}, f32[512,512]{1,0:T(8,128)S(1)}, f32[2,8,128]{2,1,0:T(8,128)S(1)}) custom-call(s32[1]{0:T(128)} %bitcast.idx, s32[1,4]{1,0:T(1,128)S(1)} %copy-done.4, s32[1,32]{1,0:T(1,128)S(1)} %copy-done.5, f32[1,128]{1,0:T(1,128)S(1)} %bitcast.20, ...), custom_call_target="tpu_custom_call" | custom-call | flops 12000000000 | bytes 12000000 | tf_op jit(solution)/shard_map/attn/pallas_call | solution.py:312
  61.6 4.1 %collective-permute-start.7 = (bf16[512,512]{1,0:T(8,128)(2,1)S(1)}, bf16[512,512]{1,0:T(8,128)(2,1)S(1)}, u32[]{:S(2)}, u32[]{:S(2)}) collective-permute-start(bf16[512,512]{1,0:T(8,128)(2,1)S(1)} %get-tuple-element.34), channel_id=1, source_target_pairs={{16,0},{24,8},{32,16},{40,24},{48,32},{56,40},{64,48},{72,56},{80,... | collective-permute-start | bytes 1572872 | tf_op jit(solution)/shard_map/ppermute | solution.py:457
  65.7 11.5 %attn.3 = (bf16[512,512]{1,0:T(8,128)(2,1)S(1)}, bf16[512,512]{1,0:T(8,128)(2,1)S(1)}, f32[512,512]{1,0:T(8,128)S(1)}, f32[512,512]{1,0:T(8,128)S(1)}, f32[2,8,128]{2,1,0:T(8,128)S(1)}) custom-call(s32[1]{0:T(128)} %bitcast.idx, s32[1,4]{1,0:T(1,128)S(1)} %copy-done.4, s32[1,32]{1,0:T(1,128)S(1)} %copy-done.5, f32[1,128]{1,0:T(1,128)S(1)} %bitcast.21, ...), custom_call_target="tpu_custom_call" | custom-call | flops 12000000000 | bytes 12000000 | tf_op jit(solution)/shard_map/attn/pallas_call | solution.py:312
  77.3 2.9 %collective-permute-start.9 = (bf16[512,512]{1,0:T(8,128)(2,1)S(1)}, bf16[512,512]{1,0:T(8,128)(2,1)S(1)}, u32[]{:S(2)}, u32[]{:S(2)}) collective-permute-start(bf16[512,512]{1,0:T(8,128)(2,1)S(1)} %get-tuple-element.38), channel_id=1, source_target_pairs={{16,0},{24,8},{32,16},{40,24},{48,32},{56,40},{64,48},{72,56},{80,... | collective-permute-start | bytes 1572872 | tf_op jit(solution)/shard_map/ppermute | solution.py:457
  80.3 3.7 %collective-permute-start.8 = (bf16[512,512]{1,0:T(8,128)(2,1)S(1)}, bf16[512,512]{1,0:T(8,128)(2,1)S(1)}, u32[]{:S(2)}, u32[]{:S(2)}) collective-permute-start(bf16[512,512]{1,0:T(8,128)(2,1)S(1)} %add_back.2.rest_0_), channel_id=1, source_target_pairs={{16,0},{24,8},{32,16},{40,24},{48,32},{56,40},{64,48},{72,56},{80,... | collective-permute-start | bytes 1572872 | tf_op jit(solution)/shard_map/ppermute | solution.py:457
  84.1 1.1 collective-permute-done.10.y
  85.2 1.6 %collective-permute-start.11 = (f32[2,128]{1,0:T(2,128)S(1)}, f32[2,128]{1,0:T(2,128)S(1)}, u32[]{:S(2)}, u32[]{:S(2)}) collective-permute-start(f32[2,128]{1,0:T(2,128)S(1)} %plus.8.x), channel_id=1, source_target_pairs={{0,1},{1,0},{2,3},{3,2},{4,5},{5,4},{6,7},{7,6},{8,9},{9,8},{10,11... | collective-permute-start | bytes 3080 | tf_op jit(solution)/shard_map/ppermute | solution.py:462
  86.8 2.0 %collective-permute-done.11.y = f32[2,128]{1,0:T(2,128)S(1)} collective-permute-done((f32[2,128]{1,0:T(2,128)S(1)}, f32[2,128]{1,0:T(2,128)S(1)}, u32[]{:S(2)}, u32[]{:S(2)}) %collective-permute-start.11) | collective-permute-done | bytes 1056 | tf_op jit(solution)/shard_map/ppermute | solution.py:462
  88.8 3.2 %collective-permute-start.12 = (f32[2,128]{1,0:T(2,128)S(1)}, f32[2,128]{1,0:T(2,128)S(1)}, u32[]{:S(2)}, u32[]{:S(2)}) collective-permute-start(f32[2,128]{1,0:T(2,128)S(1)} %plus.9.x), channel_id=1, source_target_pairs={{0,2},{1,3},{2,0},{3,1},{4,6},{5,7},{6,4},{7,5},{8,10},{9,11},{10,... | collective-permute-start | bytes 3080 | tf_op jit(solution)/shard_map/ppermute | solution.py:462
  92.0 1.9 %collective-permute-done.12.y = f32[2,128]{1,0:T(2,128)S(1)} collective-permute-done((f32[2,128]{1,0:T(2,128)S(1)}, f32[2,128]{1,0:T(2,128)S(1)}, u32[]{:S(2)}, u32[]{:S(2)}) %collective-permute-start.12) | collective-permute-done | bytes 1056 | tf_op jit(solution)/shard_map/ppermute | solution.py:462
  94.1 6.5 %collective-permute-start.13 = (bf16[512,512]{1,0:T(8,128)(2,1)S(1)}, bf16[512,512]{1,0:T(8,128)(2,1)S(1)}, u32[]{:S(2)}, u32[]{:S(2)}) collective-permute-start(bf16[512,512]{1,0:T(8,128)(2,1)S(1)} %add_back.3.rest_0_), channel_id=1, source_target_pairs={{16,0},{24,8},{32,16},{40,24},{48,32},{56,40},{64,48},{72,56},{80,... | collective-permute-start | bytes 1572872 | tf_op jit(solution)/shard_map/ppermute | solution.py:457
  100.9 3.6 %collective-permute-done.16.y = f32[2,128]{1,0:T(2,128)S(1)} collective-permute-done((f32[2,128]{1,0:T(2,128)S(1)}, f32[2,128]{1,0:T(2,128)S(1)}, u32[]{:S(2)}, u32[]{:S(2)}) %collective-permute-start.16) | collective-permute-done | bytes 1056 | tf_op jit(solution)/shard_map/ppermute | solution.py:462
  104.5 5.1 %collective-permute-done.17.y = f32[2,128]{1,0:T(2,128)S(1)} collective-permute-done((f32[2,128]{1,0:T(2,128)S(1)}, f32[2,128]{1,0:T(2,128)S(1)}, u32[]{:S(2)}, u32[]{:S(2)}) %collective-permute-start.17) | collective-permute-done | bytes 1056 | tf_op jit(solution)/shard_map/ppermute | solution.py:462
  109.6 0.6 finish.2
  110.2 4.0 %collective-permute-done.18.y = f32[2,128]{1,0:T(2,128)S(1)} collective-permute-done((f32[2,128]{1,0:T(2,128)S(1)}, f32[2,128]{1,0:T(2,128)S(1)}, u32[]{:S(2)}, u32[]{:S(2)}) %collective-permute-start.18) | collective-permute-done | bytes 1056 | tf_op jit(solution)/shard_map/ppermute | solution.py:462
  114.2 0.6 finish.3
  114.9 3.8 %collective-permute-done.19.y = f32[2,128]{1,0:T(2,128)S(1)} collective-permute-done((f32[2,128]{1,0:T(2,128)S(1)}, f32[2,128]{1,0:T(2,128)S(1)}, u32[]{:S(2)}, u32[]{:S(2)}) %collective-permute-start.19) | collective-permute-done | bytes 1056 | tf_op jit(solution)/shard_map/ppermute | solution.py:462
  118.7 2.0 %collective-permute-start.20 = (f32[2,128]{1,0:T(2,128)S(1)}, f32[2,128]{1,0:T(2,128)S(1)}, u32[]{:S(2)}, u32[]{:S(2)}) collective-permute-start(f32[2,128]{1,0:T(2,128)S(1)} %plus.14.x), channel_id=1, source_target_pairs={{0,64},{8,72},{16,80},{24,88},{32,96},{40,104},{48,112},{56,120},{... | collective-permute-start | bytes 3080 | tf_op jit(solution)/shard_map/ppermute | solution.py:462
  120.7 1.1 out_q.1
  121.8 4.4 %collective-permute-done.20.y = f32[2,128]{1,0:T(2,128)S(1)} collective-permute-done((f32[2,128]{1,0:T(2,128)S(1)}, f32[2,128]{1,0:T(2,128)S(1)}, u32[]{:S(2)}, u32[]{:S(2)}) %collective-permute-start.20) | collective-permute-done | bytes 1056 | tf_op jit(solution)/shard_map/ppermute | solution.py:462
  126.7 1.2 out_kv.1
  (51 shorter events, 2.6 us)
Async XLA Ops:
  0.6 1.0 copy-start.2
  1.7 1.0 copy-start.3
  2.7 2.5 %copy-start.1 = (bf16[1,256,2048]{2,1,0:T(8,128)(2,1)S(1)}, bf16[1,256,2048]{2,1,0:T(8,128)(2,1)}, u32[]{:S(2)}) copy-start(bf16[1,256,2048]{2,1,0:T(8,128)(2,1)} %param.11) | copy-start | bytes 3145732
  3.2 2.1 %copy-start = (bf16[1,256,2048]{2,1,0:T(8,128)(2,1)S(1)}, bf16[1,256,2048]{2,1,0:T(8,128)(2,1)}, u32[]{:S(2)}) copy-start(bf16[1,256,2048]{2,1,0:T(8,128)(2,1)} %param.8) | copy-start | bytes 3145732
  3.2 2.0 %collective-permute-start = (bf16[256,1024]{1,0:T(8,128)(2,1)S(1)}, bf16[256,1024]{1,0:T(8,128)(2,1)S(1)}, u32[]{:S(2)}, u32[]{:S(2)}) collective-permute-start(bf16[256,1024]{1,0:T(8,128)(2,1)S(1)} %get-tuple-element.26), channel_id=1, source_target_pairs={{0,8},{8,0},{16,24},{24,16},{32,40},{40,32},{48,56},{56,48},{64,72... | collective-permute-start | bytes 1572872 | tf_op jit(solution)/shard_map/ppermute | solution.py:462
  5.4 34.7 %collective-permute-start.1 = (bf16[256,2048]{1,0:T(8,128)(2,1)S(1)}, bf16[256,2048]{1,0:T(8,128)(2,1)S(1)}, u32[]{:S(2)}, u32[]{:S(2)}) collective-permute-start(bf16[256,2048]{1,0:T(8,128)(2,1)S(1)} %split_q.1), channel_id=1, source_target_pairs={{0,8},{8,0},{16,24},{24,16},{32,40},{40,32},{48,56},{56,48},{64,72... | collective-permute-start | bytes 3145736 | tf_op jit(solution)/shard_map/ppermute | solution.py:462
  5.6 21.4 %collective-permute-start.2 = (bf16[512,512]{1,0:T(8,128)(2,1)S(1)}, bf16[512,512]{1,0:T(8,128)(2,1)S(1)}, u32[]{:S(2)}, u32[]{:S(2)}) collective-permute-start(bf16[512,512]{1,0:T(8,128)(2,1)S(1)} %join_kv.2.after.kv0.kv), channel_id=1, source_target_pairs={{0,16},{8,24},{16,32},{24,40},{32,48},{40,56},{48,64},{56,72},{64,... | collective-permute-start | bytes 1572872 | tf_op jit(solution)/shard_map/ppermute | solution.py:457
  9.5 28.7 %collective-permute-start.4 = (bf16[512,512]{1,0:T(8,128)(2,1)S(1)}, bf16[512,512]{1,0:T(8,128)(2,1)S(1)}, u32[]{:S(2)}, u32[]{:S(2)}) collective-permute-start(bf16[512,512]{1,0:T(8,128)(2,1)S(1)} %join_kv.3.kv0.kv), channel_id=1, source_target_pairs={{0,16},{8,24},{16,32},{24,40},{32,48},{40,56},{48,64},{56,72},{64,... | collective-permute-start | bytes 1572872 | tf_op jit(solution)/shard_map/ppermute | solution.py:457
  26.9 22.5 %collective-permute-start.3 = (bf16[512,512]{1,0:T(8,128)(2,1)S(1)}, bf16[512,512]{1,0:T(8,128)(2,1)S(1)}, u32[]{:S(2)}, u32[]{:S(2)}) collective-permute-start(bf16[512,512]{1,0:T(8,128)(2,1)S(1)} %collective-permute-done.2.kv1), channel_id=1, source_target_pairs={{0,16},{8,24},{16,32},{24,40},{32,48},{40,56},{48,64},{56,72},{64,... | collective-permute-start | bytes 1572872 | tf_op jit(solution)/shard_map/ppermute | solution.py:457
  38.2 27.5 %collective-permute-start.5 = (bf16[512,512]{1,0:T(8,128)(2,1)S(1)}, bf16[512,512]{1,0:T(8,128)(2,1)S(1)}, u32[]{:S(2)}, u32[]{:S(2)}) collective-permute-start(bf16[512,512]{1,0:T(8,128)(2,1)S(1)} %collective-permute-done.4.rest_0_.kv1), channel_id=1, source_target_pairs={{0,16},{8,24},{16,32},{24,40},{32,48},{40,56},{48,64},{56,72},{64,... | collective-permute-start | bytes 1572872 | tf_op jit(solution)/shard_map/ppermute | solution.py:457
  49.4 0.7 copy-start.4
  49.4 0.7 copy-start.5
  49.4 0.7 copy-start.6
  49.4 0.7 copy-start.7
  61.6 18.5 %collective-permute-start.7 = (bf16[512,512]{1,0:T(8,128)(2,1)S(1)}, bf16[512,512]{1,0:T(8,128)(2,1)S(1)}, u32[]{:S(2)}, u32[]{:S(2)}) collective-permute-start(bf16[512,512]{1,0:T(8,128)(2,1)S(1)} %get-tuple-element.34), channel_id=1, source_target_pairs={{16,0},{24,8},{32,16},{40,24},{48,32},{56,40},{64,48},{72,56},{80,... | collective-permute-start | bytes 1572872 | tf_op jit(solution)/shard_map/ppermute | solution.py:457
  77.3 16.8 %collective-permute-start.9 = (bf16[512,512]{1,0:T(8,128)(2,1)S(1)}, bf16[512,512]{1,0:T(8,128)(2,1)S(1)}, u32[]{:S(2)}, u32[]{:S(2)}) collective-permute-start(bf16[512,512]{1,0:T(8,128)(2,1)S(1)} %get-tuple-element.38), channel_id=1, source_target_pairs={{16,0},{24,8},{32,16},{40,24},{48,32},{56,40},{64,48},{72,56},{80,... | collective-permute-start | bytes 1572872 | tf_op jit(solution)/shard_map/ppermute | solution.py:457
  80.3 29.3 %collective-permute-start.8 = (bf16[512,512]{1,0:T(8,128)(2,1)S(1)}, bf16[512,512]{1,0:T(8,128)(2,1)S(1)}, u32[]{:S(2)}, u32[]{:S(2)}) collective-permute-start(bf16[512,512]{1,0:T(8,128)(2,1)S(1)} %add_back.2.rest_0_), channel_id=1, source_target_pairs={{16,0},{24,8},{32,16},{40,24},{48,32},{56,40},{64,48},{72,56},{80,... | collective-permute-start | bytes 1572872 | tf_op jit(solution)/shard_map/ppermute | solution.py:457
  84.0 1.2 collective-permute-start.10
  85.2 3.6 %collective-permute-start.11 = (f32[2,128]{1,0:T(2,128)S(1)}, f32[2,128]{1,0:T(2,128)S(1)}, u32[]{:S(2)}, u32[]{:S(2)}) collective-permute-start(f32[2,128]{1,0:T(2,128)S(1)} %plus.8.x), channel_id=1, source_target_pairs={{0,1},{1,0},{2,3},{3,2},{4,5},{5,4},{6,7},{7,6},{8,9},{9,8},{10,11... | collective-permute-start | bytes 3080 | tf_op jit(solution)/shard_map/ppermute | solution.py:462
  88.8 5.1 %collective-permute-start.12 = (f32[2,128]{1,0:T(2,128)S(1)}, f32[2,128]{1,0:T(2,128)S(1)}, u32[]{:S(2)}, u32[]{:S(2)}) collective-permute-start(f32[2,128]{1,0:T(2,128)S(1)} %plus.9.x), channel_id=1, source_target_pairs={{0,2},{1,3},{2,0},{3,1},{4,6},{5,7},{6,4},{7,5},{8,10},{9,11},{10,... | collective-permute-start | bytes 3080 | tf_op jit(solution)/shard_map/ppermute | solution.py:462
  94.1 20.1 %collective-permute-start.13 = (bf16[512,512]{1,0:T(8,128)(2,1)S(1)}, bf16[512,512]{1,0:T(8,128)(2,1)S(1)}, u32[]{:S(2)}, u32[]{:S(2)}) collective-permute-start(bf16[512,512]{1,0:T(8,128)(2,1)S(1)} %add_back.3.rest_0_), channel_id=1, source_target_pairs={{16,0},{24,8},{32,16},{40,24},{48,32},{56,40},{64,48},{72,56},{80,... | collective-permute-start | bytes 1572872 | tf_op jit(solution)/shard_map/ppermute | solution.py:457
  100.7 20.0 %collective-permute-start.6 = (bf16[256,1024]{1,0:T(8,128)(2,1)S(1)}, bf16[256,1024]{1,0:T(8,128)(2,1)S(1)}, u32[]{:S(2)}, u32[]{:S(2)}) collective-permute-start(bf16[256,1024]{1,0:T(8,128)(2,1)S(1)} %split_dq.1), channel_id=1, source_target_pairs={{0,8},{8,0},{16,24},{24,16},{32,40},{40,32},{48,56},{56,48},{64,72... | collective-permute-start | bytes 1572872 | tf_op jit(solution)/shard_map/ppermute | solution.py:462
  100.8 3.7 %collective-permute-start.16 = (f32[2,128]{1,0:T(2,128)S(1)}, f32[2,128]{1,0:T(2,128)S(1)}, u32[]{:S(2)}, u32[]{:S(2)}) collective-permute-start(f32[2,128]{1,0:T(2,128)S(1)} %plus.10.rest_0_.x), channel_id=1, source_target_pairs={{0,4},{1,5},{2,6},{3,7},{4,0},{5,1},{6,2},{7,3},{8,12},{9,13},{10,... | collective-permute-start | bytes 3080 | tf_op jit(solution)/shard_map/ppermute | solution.py:462
  104.5 5.1 %collective-permute-start.17 = (f32[2,128]{1,0:T(2,128)S(1)}, f32[2,128]{1,0:T(2,128)S(1)}, u32[]{:S(2)}, u32[]{:S(2)}) collective-permute-start(f32[2,128]{1,0:T(2,128)S(1)} %plus.11.x), channel_id=1, source_target_pairs={{0,128},{8,136},{16,144},{24,152},{32,160},{40,168},{48,176},{56,1... | collective-permute-start | bytes 3080 | tf_op jit(solution)/shard_map/ppermute | solution.py:462
  109.6 4.7 %collective-permute-start.18 = (f32[2,128]{1,0:T(2,128)S(1)}, f32[2,128]{1,0:T(2,128)S(1)}, u32[]{:S(2)}, u32[]{:S(2)}) collective-permute-start(f32[2,128]{1,0:T(2,128)S(1)} %plus.12.x), channel_id=1, source_target_pairs={{0,16},{8,24},{16,0},{24,8},{32,48},{40,56},{48,32},{56,40},{64,80... | collective-permute-start | bytes 3080 | tf_op jit(solution)/shard_map/ppermute | solution.py:462
  110.1 16.6 %collective-permute-start.14 = (bf16[256,512]{1,0:T(8,128)(2,1)S(1)}, bf16[256,512]{1,0:T(8,128)(2,1)S(1)}, u32[]{:S(2)}, u32[]{:S(2)}) collective-permute-start(bf16[256,512]{1,0:T(8,128)(2,1)S(1)} %get-tuple-element.41), channel_id=1, source_target_pairs={{0,8},{8,0},{16,24},{24,16},{32,40},{40,32},{48,56},{56,48},{64,72... | collective-permute-start | bytes 786440 | tf_op jit(solution)/shard_map/ppermute | solution.py:462
  114.2 4.5 %collective-permute-start.19 = (f32[2,128]{1,0:T(2,128)S(1)}, f32[2,128]{1,0:T(2,128)S(1)}, u32[]{:S(2)}, u32[]{:S(2)}) collective-permute-start(f32[2,128]{1,0:T(2,128)S(1)} %plus.13.x), channel_id=1, source_target_pairs={{0,32},{8,40},{16,48},{24,56},{32,0},{40,8},{48,16},{56,24},{64,96... | collective-permute-start | bytes 3080 | tf_op jit(solution)/shard_map/ppermute | solution.py:462
  114.8 11.9 %collective-permute-start.15 = (bf16[256,512]{1,0:T(8,128)(2,1)S(1)}, bf16[256,512]{1,0:T(8,128)(2,1)S(1)}, u32[]{:S(2)}, u32[]{:S(2)}) collective-permute-start(bf16[256,512]{1,0:T(8,128)(2,1)S(1)} %get-tuple-element.42), channel_id=1, source_target_pairs={{0,8},{8,0},{16,24},{24,16},{32,40},{40,32},{48,56},{56,48},{64,72... | collective-permute-start | bytes 786440 | tf_op jit(solution)/shard_map/ppermute | solution.py:462
  118.7 7.5 %collective-permute-start.20 = (f32[2,128]{1,0:T(2,128)S(1)}, f32[2,128]{1,0:T(2,128)S(1)}, u32[]{:S(2)}, u32[]{:S(2)}) collective-permute-start(f32[2,128]{1,0:T(2,128)S(1)} %plus.14.x), channel_id=1, source_target_pairs={{0,64},{8,72},{16,80},{24,88},{32,96},{40,104},{48,112},{56,120},{... | collective-permute-start | bytes 3080 | tf_op jit(solution)/shard_map/ppermute | solution.py:462

commit v4 on v3

--- a/solution.py
+++ b/solution.py
@@ -354,7 +354,7 @@
     )(d1, r1, *after)
 
 
-def finish_kernel(n, idx, kg, d0, r2, kv, keep, send):
+def finish_kernel(n, idx, kg, d0, r2, kv, after, keep, send):
     a = idx[0] % 2
     for out, rows in ((keep, pl.ds(al(a * T, T), T)), (send, pl.ds(al((1 - a) * T, T), T))):
         for i in range(n):
@@ -368,16 +368,16 @@
             out[:, vc] = (d0[rows, vc] + r2[rows, vc].astype(f32)).astype(bf16)
 
 
-def finish(n, idx, kg, d0, r2, kv):
+def finish(n, idx, kg, d0, r2, kv, after):
     return pl.pallas_call(
         functools.partial(finish_kernel, n),
         out_shape=[jax.ShapeDtypeStruct((T, 2 * n * D), bf16)] * 2,
-        in_specs=[SM, VM, VM, VM, VM],
+        in_specs=[SM, VM, VM, VM, VM, ANY],
         out_specs=[VM, VM],
         compiler_params=SMALL,
         cost_estimate=cost(1),
         name="finish",
-    )(idx, kg, d0, r2, kv)
+    )(idx, kg, d0, r2, kv, after)
 
 
 def out_kv_kernel(idx, *refs):
@@ -460,6 +460,28 @@
 def swap(x, axis, bit):
     n = lax.axis_size(axis)
     return lax.ppermute(x, axis, [(i, i ^ bit) for i in range(n)])
+
+
+def turned(x, chips):
+    n = lax.axis_size("ctx")
+    return lax.ppermute(x, "ctx", [(i, i // 16 * 16 + (i + 2 * chips) % 16) for i in range(n)])
+
+
+def ends_kernel(x, y, dq_gain, dk_gain):
+    dq_gain[...] = x[:1, :] + y[:1, :]
+    dk_gain[...] = x[1:, :] + y[1:, :]
+
+
+def ends(x, y):
+    return pl.pallas_call(
+        ends_kernel,
+        out_shape=[jax.ShapeDtypeStruct((1, D), f32)] * 2,
+        in_specs=[VM, VM],
+        out_specs=[VM, VM],
+        compiler_params=SMALL,
+        cost_estimate=cost(0.1),
+        name="ends",
+    )(x, y)
 
 
 def fold_kernel(gains, *rest):
@@ -529,23 +551,25 @@
             r2s.append(along(sums[c], -2))
     gain = fold(gains, sums[last - 1])
     gain = plus(gain, swap(gain, "ctx", 1))
-    gain = plus(gain, swap(gain, "dp", 1))
-    gain = plus(gain, swap(gain, "dp", 2))
+    gain = plus(gain, turned(gain, 1))
+    gain = plus(gain, turned(gain, 2))
     sums.append(add_back(d1, r1, gain))
     r2s.append(along(sums[last], -2))
-    gain = plus(gain, swap(gain, "dp", 4), sums[last], *r2s[last - 2 : last - 1])
-    gain = plus(gain, swap(gain, "ctx", 16), r2s[last - 1])
-    gain = plus(gain, swap(gain, "ctx", 2), r2s[last])
-    gain = plus(gain, swap(gain, "ctx", 4))
-    gain = plus(gain, swap(gain, "ctx", 8))
+    gain = plus(gain, swap(gain, "dp", 1), sums[last], *r2s[last - 2 : last - 1])
+    gain = plus(gain, swap(gain, "dp", 4))
+    gain = plus(gain, swap(gain, "dp", 2))
+    steps = [gain]
+    gain = plus(gain, swap(gain, "ctx", 16))
+    steps.append(gain)
+    dq_gain, dk_gain = ends(gain, turned(gain, 4))
     keeps, recvs = [], []
     for c, n in enumerate(CHUNKS):
-        keep, send = finish(n, idx, kg, d0s[c], r2s[c], kv0[c])
+        keep, send = finish(n, idx, kg, d0s[c], r2s[c], kv0[c], steps[c - count])
         keeps.append(keep)
         recvs.append(swap(send, "ctx", 1))
     dk, dv = out_kv(idx, keeps, recvs)
     dq = out_q(idx, dqs, swap(split_dq(idx, dqs), "ctx", 1))
-    return dq[None], dk[None], dv[None], gain[0], gain[1]
+    return dq[None], dk[None], dv[None], dq_gain.reshape(D), dk_gain.reshape(D)
 
 
 def solution(mesh):

time: 128 us -> 130 us (1.016)
  waiting for transfers between devices: 60 us -> 64.3 us
  starting transfers between devices: 36.2 us -> 33.3 us
    ppermute x0 -> x3, waiting for transfers between devices: none -> 16.6 us  [turned(): lax.ppermute(x, 'ctx', [(i, i // 16 * 16 + (i + 2 * chips) % 16) for i in...]
    ppermute x13 -> x10, waiting for transfers between devices: 27.7 us -> 15.6 us  [swap(): return lax.ppermute(x, axis, [(i, i ^ bit) for i in range(n)])]
    ppermute x8, starting transfers between devices: 28.6 us -> 27 us  [along(): lax.ppermute(x, 'ctx', [(i, i + distance) for i in range(n) if 0 <= i + d...]
    ppermute x13 -> x10, starting transfers between devices: 7.57 us -> 6 us  [swap(): return lax.ppermute(x, axis, [(i, i ^ bit) for i in range(n)])]
  transfers between devices with their start and end apart: 21 -> 21, of which waited for: 13 -> 12; matrix products, arithmetic and copies ran while one was open for 0% -> 0% of each run, Pallas kernels for 20% -> 20%
where the time goes in v4:
time: 130 us; the launch traced here: 129 us
  waiting for transfers between devices  64.3 us (49%)
  starting transfers between devices  33.3 us (26%)
  Pallas kernels  27.9 us (21%)
  local copies, waits for them, and re-layouts  2.77 us (2%)
    ppermute x8, waiting for transfers between devices, along(): lax.ppermute(x, 'ctx', [(i, i + distance) for i in range(n) if 0 <= i + d...  32.1 us
    ppermute x8, starting transfers between devices, along(): lax.ppermute(x, 'ctx', [(i, i + distance) for i in range(n) if 0 <= i + d...  27 us
    pallas_call x2, Pallas kernels, attn(): pl.pallas_call(functools.partial(attn_kernel, h0, n, len(after)), out_sha...  23.1 us
    ppermute x3, waiting for transfers between devices, turned(): lax.ppermute(x, 'ctx', [(i, i // 16 * 16 + (i + 2 * chips) % 16) for i in...  16.6 us
    ppermute x10, waiting for transfers between devices, swap(): return lax.ppermute(x, axis, [(i, i ^ bit) for i in range(n)])  15.6 us
    ppermute x10, starting transfers between devices, swap(): return lax.ppermute(x, axis, [(i, i ^ bit) for i in range(n)])  6 us
    unnamed x16, local copies, waits for them, and re-layouts  2.77 us
  transfers between devices with their start and end apart: 21, of which 12 were waited for; matrix products, arithmetic and copies ran while one was open for 0% of the time, Pallas kernels for 20%

profile of v4, /device:TPU:6, one launch (start us, length us, event | category | flops | bytes accessed | tf_op | source)
XLA Modules:
  0.0 129.2 jit_solution(11014553415522792573)
XLA Ops:
  0.6 1.0 copy-done.2
  1.7 1.0 copy-done.3
  3.3 1.9 %collective-permute-done.recv = bf16[256,1024]{1,0:T(8,128)(2,1)S(1)} collective-permute-done((bf16[256,1024]{1,0:T(8,128)(2,1)S(1)}, bf16[256,1024]{1,0:T(8,128)(2,1)S(1)}, u32[]{:S(2)}, u32[]{:S(2)}) %collective-permute-start) | collective-permute-done | bytes 524320 | tf_op jit(solution)/shard_map/ppermute | solution.py:462
  5.6 3.8 %collective-permute-start.2 = (bf16[512,512]{1,0:T(8,128)(2,1)S(1)}, bf16[512,512]{1,0:T(8,128)(2,1)S(1)}, u32[]{:S(2)}, u32[]{:S(2)}) collective-permute-start(bf16[512,512]{1,0:T(8,128)(2,1)S(1)} %join_kv.2.after.kv0.kv), channel_id=1, source_target_pairs={{0,16},{8,24},{16,32},{24,40},{32,48},{40,56},{48,64},{56,72},{64,... | collective-permute-start | bytes 1572872 | tf_op jit(solution)/shard_map/ppermute | solution.py:457
  9.5 3.8 %collective-permute-start.4 = (bf16[512,512]{1,0:T(8,128)(2,1)S(1)}, bf16[512,512]{1,0:T(8,128)(2,1)S(1)}, u32[]{:S(2)}, u32[]{:S(2)}) collective-permute-start(bf16[512,512]{1,0:T(8,128)(2,1)S(1)} %join_kv.3.kv0.kv), channel_id=1, source_target_pairs={{0,16},{8,24},{16,32},{24,40},{32,48},{40,56},{48,64},{56,72},{64,... | collective-permute-start | bytes 1572872 | tf_op jit(solution)/shard_map/ppermute | solution.py:457
  13.3 13.6 %collective-permute-done.2.kv1 = bf16[512,512]{1,0:T(8,128)(2,1)S(1)} collective-permute-done((bf16[512,512]{1,0:T(8,128)(2,1)S(1)}, bf16[512,512]{1,0:T(8,128)(2,1)S(1)}, u32[]{:S(2)}, u32[]{:S(2)}) %collective-permute-start.2) | collective-permute-done | bytes 524320 | tf_op jit(solution)/shard_map/ppermute | solution.py:457
  26.9 1.9 %collective-permute-start.3 = (bf16[512,512]{1,0:T(8,128)(2,1)S(1)}, bf16[512,512]{1,0:T(8,128)(2,1)S(1)}, u32[]{:S(2)}, u32[]{:S(2)}) collective-permute-start(bf16[512,512]{1,0:T(8,128)(2,1)S(1)} %collective-permute-done.2.kv1), channel_id=1, source_target_pairs={{0,16},{8,24},{16,32},{24,40},{32,48},{40,56},{48,64},{56,72},{64,... | collective-permute-start | bytes 1572872 | tf_op jit(solution)/shard_map/ppermute | solution.py:457
  28.9 9.3 %collective-permute-done.4.rest_0_.kv1 = bf16[512,512]{1,0:T(8,128)(2,1)S(1)} collective-permute-done((bf16[512,512]{1,0:T(8,128)(2,1)S(1)}, bf16[512,512]{1,0:T(8,128)(2,1)S(1)}, u32[]{:S(2)}, u32[]{:S(2)}) %collective-permute-start.4) | collective-permute-done | bytes 524320 | tf_op jit(solution)/shard_map/ppermute | solution.py:457
  38.2 1.9 %collective-permute-start.5 = (bf16[512,512]{1,0:T(8,128)(2,1)S(1)}, bf16[512,512]{1,0:T(8,128)(2,1)S(1)}, u32[]{:S(2)}, u32[]{:S(2)}) collective-permute-start(bf16[512,512]{1,0:T(8,128)(2,1)S(1)} %collective-permute-done.4.rest_0_.kv1), channel_id=1, source_target_pairs={{0,16},{8,24},{16,32},{24,40},{32,48},{40,56},{48,64},{56,72},{64,... | collective-permute-start | bytes 1572872 | tf_op jit(solution)/shard_map/ppermute | solution.py:457
  40.3 9.1 %collective-permute-done.3.kv2 = bf16[512,512]{1,0:T(8,128)(2,1)S(1)} collective-permute-done((bf16[512,512]{1,0:T(8,128)(2,1)S(1)}, bf16[512,512]{1,0:T(8,128)(2,1)S(1)}, u32[]{:S(2)}, u32[]{:S(2)}) %collective-permute-start.3) | collective-permute-done | bytes 524320 | tf_op jit(solution)/shard_map/ppermute | solution.py:457
  49.4 0.6 copy-done.4
  50.1 11.5 %attn.2 = (bf16[512,512]{1,0:T(8,128)(2,1)S(1)}, bf16[512,512]{1,0:T(8,128)(2,1)S(1)}, f32[512,512]{1,0:T(8,128)S(1)}, f32[512,512]{1,0:T(8,128)S(1)}, f32[2,8,128]{2,1,0:T(8,128)S(1)}) custom-call(s32[1]{0:T(128)} %bitcast.idx, s32[1,4]{1,0:T(1,128)S(1)} %copy-done.4, s32[1,32]{1,0:T(1,128)S(1)} %copy-done.5, f32[1,128]{1,0:T(1,128)S(1)} %bitcast.18, ...), custom_call_target="tpu_custom_call" | custom-call | flops 12000000000 | bytes 12000000 | tf_op jit(solution)/shard_map/attn/pallas_call | solution.py:312
  61.6 4.1 %collective-permute-start.7 = (bf16[512,512]{1,0:T(8,128)(2,1)S(1)}, bf16[512,512]{1,0:T(8,128)(2,1)S(1)}, u32[]{:S(2)}, u32[]{:S(2)}) collective-permute-start(bf16[512,512]{1,0:T(8,128)(2,1)S(1)} %get-tuple-element.36), channel_id=1, source_target_pairs={{16,0},{24,8},{32,16},{40,24},{48,32},{56,40},{64,48},{72,56},{80,... | collective-permute-start | bytes 1572872 | tf_op jit(solution)/shard_map/ppermute | solution.py:457
  65.7 11.5 %attn.3 = (bf16[512,512]{1,0:T(8,128)(2,1)S(1)}, bf16[512,512]{1,0:T(8,128)(2,1)S(1)}, f32[512,512]{1,0:T(8,128)S(1)}, f32[512,512]{1,0:T(8,128)S(1)}, f32[2,8,128]{2,1,0:T(8,128)S(1)}) custom-call(s32[1]{0:T(128)} %bitcast.idx, s32[1,4]{1,0:T(1,128)S(1)} %copy-done.4, s32[1,32]{1,0:T(1,128)S(1)} %copy-done.5, f32[1,128]{1,0:T(1,128)S(1)} %bitcast.19, ...), custom_call_target="tpu_custom_call" | custom-call | flops 12000000000 | bytes 12000000 | tf_op jit(solution)/shard_map/attn/pallas_call | solution.py:312
  77.3 2.9 %collective-permute-start.13 = (bf16[512,512]{1,0:T(8,128)(2,1)S(1)}, bf16[512,512]{1,0:T(8,128)(2,1)S(1)}, u32[]{:S(2)}, u32[]{:S(2)}) collective-permute-start(bf16[512,512]{1,0:T(8,128)(2,1)S(1)} %get-tuple-element.39), channel_id=1, source_target_pairs={{16,0},{24,8},{32,16},{40,24},{48,32},{56,40},{64,48},{72,56},{80,... | collective-permute-start | bytes 1572872 | tf_op jit(solution)/shard_map/ppermute | solution.py:457
  80.3 3.7 %collective-permute-start.8 = (bf16[512,512]{1,0:T(8,128)(2,1)S(1)}, bf16[512,512]{1,0:T(8,128)(2,1)S(1)}, u32[]{:S(2)}, u32[]{:S(2)}) collective-permute-start(bf16[512,512]{1,0:T(8,128)(2,1)S(1)} %add_back.2.rest_0_), channel_id=1, source_target_pairs={{16,0},{24,8},{32,16},{40,24},{48,32},{56,40},{64,48},{72,56},{80,... | collective-permute-start | bytes 1572872 | tf_op jit(solution)/shard_map/ppermute | solution.py:457
  84.1 1.1 collective-permute-done.9.y
  85.5 4.5 %collective-permute-done.10.y = f32[2,128]{1,0:T(2,128)S(1)} collective-permute-done((f32[2,128]{1,0:T(2,128)S(1)}, f32[2,128]{1,0:T(2,128)S(1)}, u32[]{:S(2)}, u32[]{:S(2)}) %collective-permute-start.10) | collective-permute-done | bytes 1056 | tf_op jit(solution)/shard_map/ppermute | solution.py:467
  90.0 5.7 %collective-permute-done.11.y = f32[2,128]{1,0:T(2,128)S(1)} collective-permute-done((f32[2,128]{1,0:T(2,128)S(1)}, f32[2,128]{1,0:T(2,128)S(1)}, u32[]{:S(2)}, u32[]{:S(2)}) %collective-permute-start.11) | collective-permute-done | bytes 1056 | tf_op jit(solution)/shard_map/ppermute | solution.py:467
  95.8 4.9 %collective-permute-start.16 = (bf16[512,512]{1,0:T(8,128)(2,1)S(1)}, bf16[512,512]{1,0:T(8,128)(2,1)S(1)}, u32[]{:S(2)}, u32[]{:S(2)}) collective-permute-start(bf16[512,512]{1,0:T(8,128)(2,1)S(1)} %add_back.3.rest_0_), channel_id=1, source_target_pairs={{16,0},{24,8},{32,16},{40,24},{48,32},{56,40},{64,48},{72,56},{80,... | collective-permute-start | bytes 1572872 | tf_op jit(solution)/shard_map/ppermute | solution.py:457
  100.8 1.7 %collective-permute-start.12 = (f32[2,128]{1,0:T(2,128)S(1)}, f32[2,128]{1,0:T(2,128)S(1)}, u32[]{:S(2)}, u32[]{:S(2)}) collective-permute-start(f32[2,128]{1,0:T(2,128)S(1)} %plus.9.rest_0_.x), channel_id=1, source_target_pairs={{0,1},{1,0},{2,3},{3,2},{4,5},{5,4},{6,7},{7,6},{8,9},{9,8},{10,11... | collective-permute-start | bytes 3080 | tf_op jit(solution)/shard_map/ppermute | solution.py:462
  102.5 2.0 %collective-permute-done.12.y = f32[2,128]{1,0:T(2,128)S(1)} collective-permute-done((f32[2,128]{1,0:T(2,128)S(1)}, f32[2,128]{1,0:T(2,128)S(1)}, u32[]{:S(2)}, u32[]{:S(2)}) %collective-permute-start.12) | collective-permute-done | bytes 1056 | tf_op jit(solution)/shard_map/ppermute | solution.py:462
  104.5 3.6 %collective-permute-done.14.y = f32[2,128]{1,0:T(2,128)S(1)} collective-permute-done((f32[2,128]{1,0:T(2,128)S(1)}, f32[2,128]{1,0:T(2,128)S(1)}, u32[]{:S(2)}, u32[]{:S(2)}) %collective-permute-start.14) | collective-permute-done | bytes 1056 | tf_op jit(solution)/shard_map/ppermute | solution.py:462
  108.1 3.2 %collective-permute-start.15 = (f32[2,128]{1,0:T(2,128)S(1)}, f32[2,128]{1,0:T(2,128)S(1)}, u32[]{:S(2)}, u32[]{:S(2)}) collective-permute-start(f32[2,128]{1,0:T(2,128)S(1)} %plus.11.x), channel_id=1, source_target_pairs={{0,2},{1,3},{2,0},{3,1},{4,6},{5,7},{6,4},{7,5},{8,10},{9,11},{10,... | collective-permute-start | bytes 3080 | tf_op jit(solution)/shard_map/ppermute | solution.py:462
  111.2 1.9 %collective-permute-done.15.y = f32[2,128]{1,0:T(2,128)S(1)} collective-permute-done((f32[2,128]{1,0:T(2,128)S(1)}, f32[2,128]{1,0:T(2,128)S(1)}, u32[]{:S(2)}, u32[]{:S(2)}) %collective-permute-start.15) | collective-permute-done | bytes 1056 | tf_op jit(solution)/shard_map/ppermute | solution.py:462
  113.1 5.1 %collective-permute-done.17.y = f32[2,128]{1,0:T(2,128)S(1)} collective-permute-done((f32[2,128]{1,0:T(2,128)S(1)}, f32[2,128]{1,0:T(2,128)S(1)}, u32[]{:S(2)}, u32[]{:S(2)}) %collective-permute-start.17) | collective-permute-done | bytes 1056 | tf_op jit(solution)/shard_map/ppermute | solution.py:462
  118.2 0.5 finish.2
  118.9 0.6 finish.3
  119.5 0.6 collective-permute-start.19
  120.0 1.1 out_q.1
  121.1 6.4 %collective-permute-done.20.y = f32[2,128]{1,0:T(2,128)S(1)} collective-permute-done((f32[2,128]{1,0:T(2,128)S(1)}, f32[2,128]{1,0:T(2,128)S(1)}, u32[]{:S(2)}, u32[]{:S(2)}) %collective-permute-start.20) | collective-permute-done | bytes 1056 | tf_op jit(solution)/shard_map/ppermute | solution.py:467
  128.0 1.2 out_kv.1
  (50 shorter events, 2.6 us)
Async XLA Ops:
  0.6 1.0 copy-start.2
  1.7 1.0 copy-start.3
  2.7 2.5 %copy-start.1 = (bf16[1,256,2048]{2,1,0:T(8,128)(2,1)S(1)}, bf16[1,256,2048]{2,1,0:T(8,128)(2,1)}, u32[]{:S(2)}) copy-start(bf16[1,256,2048]{2,1,0:T(8,128)(2,1)} %param.11) | copy-start | bytes 3145732
  3.2 2.1 %copy-start = (bf16[1,256,2048]{2,1,0:T(8,128)(2,1)S(1)}, bf16[1,256,2048]{2,1,0:T(8,128)(2,1)}, u32[]{:S(2)}) copy-start(bf16[1,256,2048]{2,1,0:T(8,128)(2,1)} %param.8) | copy-start | bytes 3145732
  3.2 2.0 %collective-permute-start = (bf16[256,1024]{1,0:T(8,128)(2,1)S(1)}, bf16[256,1024]{1,0:T(8,128)(2,1)S(1)}, u32[]{:S(2)}, u32[]{:S(2)}) collective-permute-start(bf16[256,1024]{1,0:T(8,128)(2,1)S(1)} %get-tuple-element.28), channel_id=1, source_target_pairs={{0,8},{8,0},{16,24},{24,16},{32,40},{40,32},{48,56},{56,48},{64,72... | collective-permute-start | bytes 1572872 | tf_op jit(solution)/shard_map/ppermute | solution.py:462
  5.4 34.7 %collective-permute-start.1 = (bf16[256,2048]{1,0:T(8,128)(2,1)S(1)}, bf16[256,2048]{1,0:T(8,128)(2,1)S(1)}, u32[]{:S(2)}, u32[]{:S(2)}) collective-permute-start(bf16[256,2048]{1,0:T(8,128)(2,1)S(1)} %split_q.1), channel_id=1, source_target_pairs={{0,8},{8,0},{16,24},{24,16},{32,40},{40,32},{48,56},{56,48},{64,72... | collective-permute-start | bytes 3145736 | tf_op jit(solution)/shard_map/ppermute | solution.py:462
  5.6 21.4 %collective-permute-start.2 = (bf16[512,512]{1,0:T(8,128)(2,1)S(1)}, bf16[512,512]{1,0:T(8,128)(2,1)S(1)}, u32[]{:S(2)}, u32[]{:S(2)}) collective-permute-start(bf16[512,512]{1,0:T(8,128)(2,1)S(1)} %join_kv.2.after.kv0.kv), channel_id=1, source_target_pairs={{0,16},{8,24},{16,32},{24,40},{32,48},{40,56},{48,64},{56,72},{64,... | collective-permute-start | bytes 1572872 | tf_op jit(solution)/shard_map/ppermute | solution.py:457
  9.5 28.7 %collective-permute-start.4 = (bf16[512,512]{1,0:T(8,128)(2,1)S(1)}, bf16[512,512]{1,0:T(8,128)(2,1)S(1)}, u32[]{:S(2)}, u32[]{:S(2)}) collective-permute-start(bf16[512,512]{1,0:T(8,128)(2,1)S(1)} %join_kv.3.kv0.kv), channel_id=1, source_target_pairs={{0,16},{8,24},{16,32},{24,40},{32,48},{40,56},{48,64},{56,72},{64,... | collective-permute-start | bytes 1572872 | tf_op jit(solution)/shard_map/ppermute | solution.py:457
  26.9 22.5 %collective-permute-start.3 = (bf16[512,512]{1,0:T(8,128)(2,1)S(1)}, bf16[512,512]{1,0:T(8,128)(2,1)S(1)}, u32[]{:S(2)}, u32[]{:S(2)}) collective-permute-start(bf16[512,512]{1,0:T(8,128)(2,1)S(1)} %collective-permute-done.2.kv1), channel_id=1, source_target_pairs={{0,16},{8,24},{16,32},{24,40},{32,48},{40,56},{48,64},{56,72},{64,... | collective-permute-start | bytes 1572872 | tf_op jit(solution)/shard_map/ppermute | solution.py:457
  38.2 27.5 %collective-permute-start.5 = (bf16[512,512]{1,0:T(8,128)(2,1)S(1)}, bf16[512,512]{1,0:T(8,128)(2,1)S(1)}, u32[]{:S(2)}, u32[]{:S(2)}) collective-permute-start(bf16[512,512]{1,0:T(8,128)(2,1)S(1)} %collective-permute-done.4.rest_0_.kv1), channel_id=1, source_target_pairs={{0,16},{8,24},{16,32},{24,40},{32,48},{40,56},{48,64},{56,72},{64,... | collective-permute-start | bytes 1572872 | tf_op jit(solution)/shard_map/ppermute | solution.py:457
  49.4 0.7 copy-start.4
  49.4 0.7 copy-start.5
  49.4 0.7 copy-start.6
  49.4 0.7 copy-start.7
  61.6 18.6 %collective-permute-start.7 = (bf16[512,512]{1,0:T(8,128)(2,1)S(1)}, bf16[512,512]{1,0:T(8,128)(2,1)S(1)}, u32[]{:S(2)}, u32[]{:S(2)}) collective-permute-start(bf16[512,512]{1,0:T(8,128)(2,1)S(1)} %get-tuple-element.36), channel_id=1, source_target_pairs={{16,0},{24,8},{32,16},{40,24},{48,32},{56,40},{64,48},{72,56},{80,... | collective-permute-start | bytes 1572872 | tf_op jit(solution)/shard_map/ppermute | solution.py:457
  77.3 18.4 %collective-permute-start.13 = (bf16[512,512]{1,0:T(8,128)(2,1)S(1)}, bf16[512,512]{1,0:T(8,128)(2,1)S(1)}, u32[]{:S(2)}, u32[]{:S(2)}) collective-permute-start(bf16[512,512]{1,0:T(8,128)(2,1)S(1)} %get-tuple-element.39), channel_id=1, source_target_pairs={{16,0},{24,8},{32,16},{40,24},{48,32},{56,40},{64,48},{72,56},{80,... | collective-permute-start | bytes 1572872 | tf_op jit(solution)/shard_map/ppermute | solution.py:457
  80.3 37.9 %collective-permute-start.8 = (bf16[512,512]{1,0:T(8,128)(2,1)S(1)}, bf16[512,512]{1,0:T(8,128)(2,1)S(1)}, u32[]{:S(2)}, u32[]{:S(2)}) collective-permute-start(bf16[512,512]{1,0:T(8,128)(2,1)S(1)} %add_back.2.rest_0_), channel_id=1, source_target_pairs={{16,0},{24,8},{32,16},{40,24},{48,32},{56,40},{64,48},{72,56},{80,... | collective-permute-start | bytes 1572872 | tf_op jit(solution)/shard_map/ppermute | solution.py:457
  84.0 1.2 collective-permute-start.9
  85.2 4.8 %collective-permute-start.10 = (f32[2,128]{1,0:T(2,128)S(1)}, f32[2,128]{1,0:T(2,128)S(1)}, u32[]{:S(2)}, u32[]{:S(2)}) collective-permute-start(f32[2,128]{1,0:T(2,128)S(1)} %plus.7.x), channel_id=1, source_target_pairs={{0,16},{8,24},{16,32},{24,40},{32,48},{40,56},{48,64},{56,72},{64,... | collective-permute-start | bytes 3080 | tf_op jit(solution)/shard_map/ppermute | solution.py:467
  90.0 5.7 %collective-permute-start.11 = (f32[2,128]{1,0:T(2,128)S(1)}, f32[2,128]{1,0:T(2,128)S(1)}, u32[]{:S(2)}, u32[]{:S(2)}) collective-permute-start(f32[2,128]{1,0:T(2,128)S(1)} %plus.8.x), channel_id=1, source_target_pairs={{0,32},{8,40},{16,48},{24,56},{32,64},{40,72},{48,80},{56,88},{64,... | collective-permute-start | bytes 3080 | tf_op jit(solution)/shard_map/ppermute | solution.py:467
  95.8 23.1 %collective-permute-start.16 = (bf16[512,512]{1,0:T(8,128)(2,1)S(1)}, bf16[512,512]{1,0:T(8,128)(2,1)S(1)}, u32[]{:S(2)}, u32[]{:S(2)}) collective-permute-start(bf16[512,512]{1,0:T(8,128)(2,1)S(1)} %add_back.3.rest_0_), channel_id=1, source_target_pairs={{16,0},{24,8},{32,16},{40,24},{48,32},{56,40},{64,48},{72,56},{80,... | collective-permute-start | bytes 1572872 | tf_op jit(solution)/shard_map/ppermute | solution.py:457
  100.7 19.3 %collective-permute-start.6 = (bf16[256,1024]{1,0:T(8,128)(2,1)S(1)}, bf16[256,1024]{1,0:T(8,128)(2,1)S(1)}, u32[]{:S(2)}, u32[]{:S(2)}) collective-permute-start(bf16[256,1024]{1,0:T(8,128)(2,1)S(1)} %split_dq.1), channel_id=1, source_target_pairs={{0,8},{8,0},{16,24},{24,16},{32,40},{40,32},{48,56},{56,48},{64,72... | collective-permute-start | bytes 1572872 | tf_op jit(solution)/shard_map/ppermute | solution.py:462
  100.8 3.7 %collective-permute-start.12 = (f32[2,128]{1,0:T(2,128)S(1)}, f32[2,128]{1,0:T(2,128)S(1)}, u32[]{:S(2)}, u32[]{:S(2)}) collective-permute-start(f32[2,128]{1,0:T(2,128)S(1)} %plus.9.rest_0_.x), channel_id=1, source_target_pairs={{0,1},{1,0},{2,3},{3,2},{4,5},{5,4},{6,7},{7,6},{8,9},{9,8},{10,11... | collective-permute-start | bytes 3080 | tf_op jit(solution)/shard_map/ppermute | solution.py:462
  104.5 3.6 %collective-permute-start.14 = (f32[2,128]{1,0:T(2,128)S(1)}, f32[2,128]{1,0:T(2,128)S(1)}, u32[]{:S(2)}, u32[]{:S(2)}) collective-permute-start(f32[2,128]{1,0:T(2,128)S(1)} %plus.10.x), channel_id=1, source_target_pairs={{0,4},{1,5},{2,6},{3,7},{4,0},{5,1},{6,2},{7,3},{8,12},{9,13},{10,... | collective-permute-start | bytes 3080 | tf_op jit(solution)/shard_map/ppermute | solution.py:462
  108.1 5.1 %collective-permute-start.15 = (f32[2,128]{1,0:T(2,128)S(1)}, f32[2,128]{1,0:T(2,128)S(1)}, u32[]{:S(2)}, u32[]{:S(2)}) collective-permute-start(f32[2,128]{1,0:T(2,128)S(1)} %plus.11.x), channel_id=1, source_target_pairs={{0,2},{1,3},{2,0},{3,1},{4,6},{5,7},{6,4},{7,5},{8,10},{9,11},{10,... | collective-permute-start | bytes 3080 | tf_op jit(solution)/shard_map/ppermute | solution.py:462
  113.1 5.1 %collective-permute-start.17 = (f32[2,128]{1,0:T(2,128)S(1)}, f32[2,128]{1,0:T(2,128)S(1)}, u32[]{:S(2)}, u32[]{:S(2)}) collective-permute-start(f32[2,128]{1,0:T(2,128)S(1)} %plus.12.after.x), channel_id=1, source_target_pairs={{0,128},{8,136},{16,144},{24,152},{32,160},{40,168},{48,176},{56,1... | collective-permute-start | bytes 3080 | tf_op jit(solution)/shard_map/ppermute | solution.py:462
  118.8 9.2 %collective-permute-start.18 = (bf16[256,512]{1,0:T(8,128)(2,1)S(1)}, bf16[256,512]{1,0:T(8,128)(2,1)S(1)}, u32[]{:S(2)}, u32[]{:S(2)}) collective-permute-start(bf16[256,512]{1,0:T(8,128)(2,1)S(1)} %get-tuple-element.43), channel_id=1, source_target_pairs={{0,8},{8,0},{16,24},{24,16},{32,40},{40,32},{48,56},{56,48},{64,72... | collective-permute-start | bytes 786440 | tf_op jit(solution)/shard_map/ppermute | solution.py:462
  119.5 8.6 %collective-permute-start.19 = (bf16[256,512]{1,0:T(8,128)(2,1)S(1)}, bf16[256,512]{1,0:T(8,128)(2,1)S(1)}, u32[]{:S(2)}, u32[]{:S(2)}) collective-permute-start(bf16[256,512]{1,0:T(8,128)(2,1)S(1)} %get-tuple-element.44), channel_id=1, source_target_pairs={{0,8},{8,0},{16,24},{24,16},{32,40},{40,32},{48,56},{56,48},{64,72... | collective-permute-start | bytes 786440 | tf_op jit(solution)/shard_map/ppermute | solution.py:462
  120.0 7.5 %collective-permute-start.20 = (f32[2,128]{1,0:T(2,128)S(1)}, f32[2,128]{1,0:T(2,128)S(1)}, u32[]{:S(2)}, u32[]{:S(2)}) collective-permute-start(f32[2,128]{1,0:T(2,128)S(1)} %plus.13.after.x), channel_id=1, source_target_pairs={{0,64},{8,72},{16,80},{24,88},{32,96},{40,104},{48,112},{56,120},{... | collective-permute-start | bytes 3080 | tf_op jit(solution)/shard_map/ppermute | solution.py:467
